TPU v7x, 512 devices: a whole 4x4x16 slice. The times are simulated.
512 devices in a mesh: layer: 16 (over y, z_hi, core), row: 4 (over x), col: 8 (over z_lo).
Axes of the slice: x: 4, y: 4, z: 16 (z_hi: 2, z_lo: 8; z = z_hi * 8 + z_lo), core: 2. Of those that a mesh axis runs over, the one named last changes fastest.
Arguments:
- front: float32 [16, 4096, 4096], P('layer', 'row', 'col'), may hold values from -0.875 to 0.875
- inverses: float32 [16, 2, 512, 512], P('layer', None, 'row')
- pattern: int32 [2, 32, 32], replicated, may hold values 0 or 1
- order: int32 [8], replicated, may hold values from 0 to 7, each once
- lists: int32 [16, 32, 32], P('layer'), may hold values from 0 to 15
Outputs:
- ancestor: float32 [16, 4096, 4096], P('layer', 'row', 'col')
Inputs may be any that keep to these rules, and one draw needn't show every extreme that they name: `order`: every panel appears once.
All inputs are finite; a program needn't handle non-finite values.
Results may differ from a plain program's by a relative error of at most 0.00022.
Values sent between devices are 32-bit elements; how exact they have to be, the bound alone decides.
No kernel may reach another device: no remote copies, remote signals or barrier semaphores. Data moves between devices by JAX's collectives and lax.ppermute only.
A program may use at most 64 MiB of HBM per device.

v0:
```python
import jax
import jax.numpy as jnp
from jax import lax
from jax.sharding import PartitionSpec as P

F = 4096
P_SIZE = 512
BLK = 128
SECTIONS = 2


EXACT_PRECISION = lax.Precision.HIGHEST


def broadcast(value, axis, source):
    kept = jnp.where(lax.axis_index(axis) == source, value, 0).astype(value.dtype)
    return lax.psum(kept, axis)


def from_partner(value, axis, bit):
    mask = 2**bit
    pairs = [(source, source ^ mask) for source in range(lax.axis_size(axis))]
    return lax.ppermute(value, axis, pairs)


def matmul(left_side, right_side):
    return jnp.dot(
        left_side, right_side, precision=EXACT_PRECISION, preferred_element_type=jnp.float32
    )


def lookup_alive(block_panels, panel_numbers, alive_panels):
    onehot = (block_panels[:, None] == panel_numbers[None, :]).astype(jnp.float32)
    return jnp.sum(onehot * alive_panels[None, :], axis=1)


def body(front, inverses, pattern, order, lists):
    matrix = front[0]
    local_inverse = inverses[0]
    row_count, column_count = matrix.shape
    row_blocks = row_count // BLK
    column_blocks = column_count // BLK
    row_index = lax.axis_index("row")
    column_index = lax.axis_index("col")
    row_first = row_index * row_blocks
    column_first = column_index * column_blocks
    panel_numbers = jnp.arange(F // P_SIZE)
    row_panels = (row_first + jnp.arange(row_blocks)) // (P_SIZE // BLK)
    column_panels = (column_first + jnp.arange(column_blocks)) // (P_SIZE // BLK)
    eliminated = jnp.zeros((F // P_SIZE,), jnp.float32)
    for section_index in range(SECTIONS):
        target = order[section_index]
        first_index = target * P_SIZE
        eliminated = eliminated + (panel_numbers == target).astype(jnp.float32)
        alive_panels = 1.0 - eliminated
        row_candidate = lax.dynamic_slice_in_dim(matrix, first_index % row_count, P_SIZE, 0)
        pivot_row = broadcast(row_candidate, "row", first_index // row_count)
        column_candidate = matrix
        scaled_part = matmul(local_inverse[section_index], pivot_row)
        right_side = lax.all_gather(scaled_part, "row", axis=0, tiled=True)
        left_side = broadcast(column_candidate, "col", first_index // column_count)
        update = matmul(left_side, right_side)
        alive_rows = lookup_alive(row_panels, panel_numbers, alive_panels)
        alive_columns = lookup_alive(column_panels, panel_numbers, alive_panels)
        local_pattern = lax.dynamic_slice(
            pattern[section_index], (row_first, column_first), (row_blocks, column_blocks)
        ).astype(jnp.float32)
        update_mask = local_pattern * alive_rows[:, None] * alive_columns[None, :]
        blocked = (
            matrix.reshape(row_blocks, BLK, column_blocks, BLK)
            - update.reshape(row_blocks, BLK, column_blocks, BLK) * update_mask[:, None, :, None]
        )
        matrix = blocked.reshape(row_count, column_count)
    alive_panels = 1.0 - eliminated
    alive_rows = lookup_alive(row_panels, panel_numbers, alive_panels)
    alive_columns = lookup_alive(column_panels, panel_numbers, alive_panels)
    keep_mask = alive_rows[:, None] * alive_columns[None, :]
    accumulated = matrix.reshape(row_blocks, BLK, column_blocks, BLK) * keep_mask[:, None, :, None]
    local_lists = lax.dynamic_slice(
        lists[0], (row_first, column_first), (row_blocks, column_blocks)
    )
    level_count = lax.axis_size("layer").bit_length() - 1
    for level_bit in range(level_count):
        partner = from_partner(accumulated, "layer", level_bit)
        weights = (local_lists // 2**level_bit % 2).astype(jnp.float32)
        accumulated = accumulated + partner * weights[:, None, :, None]
    return accumulated.reshape(row_count, column_count)[None]


def solution(mesh):
    placed = (
        P("layer", "row", "col"),
        P("layer", None, "row", None),
        P(),
        P(),
        P("layer", None, None),
    )
    return jax.shard_map(
        body, mesh=mesh, in_specs=placed, out_specs=P("layer", "row", "col"), check_vma=False
    )
```

profile of v0, /device:TPU:24, one launch (start us, length us, event | category | flops | bytes accessed | tf_op | source)
XLA Modules:
  0.0 832.9 jit_solution(2448835506107057574)
XLA Ops:
  6.5 1.4 fusion.23
  8.5 2.3 select_bitcast_fusion
  11.0 1.5 bitcast_select_fusion
  12.6 63.8 %all-reduce.7.cloned.1.call-done = f32[512,512]{1,0:T(8,128)} async-done(((f32[512,512]{1,0:T(8,128)}), f32[512,512]{1,0:T(8,128)}) %all-reduce.7.cloned.1.call-update) | async-done | bytes 1048592 | tf_op jit(solution)/shard_map/psum | solution.py:17
  76.4 3.7 convolution_bitcast_fusion.1
  81.1 1.1 fusion.19
  82.7 138.8 %all-reduce.5.cloned.1.call-done = f32[1024,512]{1,0:T(8,128)} async-done(((f32[1024,512]{1,0:T(8,128)}), f32[1024,512]{1,0:T(8,128)}) %all-reduce.5.cloned.1.call-update) | async-done | bytes 2097168 | tf_op jit(solution)/shard_map/psum | solution.py:17
  221.5 31.2 %all-gather.3.cloned.1.call-done = f32[512,512]{0,1:T(8,128)} async-done(((f32[128,512]{0,1:T(8,128)}), f32[512,512]{0,1:T(8,128)}) %all-gather.3.cloned.1.call-update) | async-done | bytes 1048592 | tf_op jit(solution)/shard_map/all_gather | solution.py:60
  253.1 1.2 copy-done.4
  254.3 6.5 broadcast_select_fusion
  262.7 61.6 %all-reduce.11.cloned.1.call-done = f32[512,512]{1,0:T(8,128)} async-done(((f32[512,512]{1,0:T(8,128)}), f32[512,512]{1,0:T(8,128)}) %all-reduce.11.cloned.1.call-update) | async-done | bytes 1048592 | tf_op jit(solution)/shard_map/psum | solution.py:17
  324.3 3.7 convolution_bitcast_fusion
  328.1 1.8 reshape_squeeze.3
  330.2 2.9 reshape.284
  333.1 135.5 %all-reduce.9.cloned.1.call-done = f32[1024,512]{1,0:T(8,128)} async-done(((f32[1024,512]{1,0:T(8,128)}), f32[1024,512]{1,0:T(8,128)}) %all-reduce.9.cloned.1.call-update) | async-done | bytes 2097168 | tf_op jit(solution)/shard_map/psum | solution.py:17
  468.6 30.9 %all-gather.5.cloned.1.call-done = f32[512,512]{0,1:T(8,128)} async-done(((f32[128,512]{0,1:T(8,128)}), f32[512,512]{0,1:T(8,128)}) %all-gather.5.cloned.1.call-update) | async-done | bytes 1048592 | tf_op jit(solution)/shard_map/all_gather | solution.py:60
  499.4 6.6 fusion.24
  506.1 3.1 reshape.285
  509.1 4.4 subtract_multiply_fusion
  513.5 1.9 collective-permute-start
  515.7 4.2 collective-permute-done
  519.9 2.8 multiply_add_fusion.3
  522.7 12.8 %collective-permute-start.1 = (f32[8,128,4,128]{3,2,1,0:T(4,128)S(1)}, f32[8,128,4,128]{3,2,1,0:T(4,128)}, u32[]{:S(2)}, u32[]{:S(2)}) collective-permute-start(f32[8,128,4,128]{3,2,1,0:T(4,128)S(1)} %multiply_add_fusion.3), channel_id=1, source_target_pairs={{0,64},{32,96},{64,0},{96,32},{128,192},{160,224},{192,128},{224,1... | collective-permute-start | bytes 6291464 | tf_op jit(solution)/shard_map/ppermute | solution.py:23
  535.6 180.9 %collective-permute-done.1 = f32[8,128,4,128]{3,2,1,0:T(4,128)} collective-permute-done((f32[8,128,4,128]{3,2,1,0:T(4,128)S(1)}, f32[8,128,4,128]{3,2,1,0:T(4,128)}, u32[]{:S(2)}, u32[]{:S(2)}) %collective-permute-start.1) | collective-permute-done | bytes 2097184 | tf_op jit(solution)/shard_map/ppermute | solution.py:23
  716.5 3.5 multiply_add_fusion.2
  720.0 2.7 collective-permute-start.2
  722.9 46.2 %collective-permute-done.2 = f32[8,128,4,128]{3,2,1,0:T(4,128)} collective-permute-done((f32[8,128,4,128]{3,2,1,0:T(4,128)}, f32[8,128,4,128]{3,2,1,0:T(4,128)}, u32[]{:S(2)}, u32[]{:S(2)}) %collective-permute-start.2) | collective-permute-done | bytes 2097184 | tf_op jit(solution)/shard_map/ppermute | solution.py:23
  769.1 2.8 multiply_add_fusion.1
  771.9 2.1 collective-permute-start.3
  774.1 47.2 %collective-permute-done.3 = f32[8,128,4,128]{3,2,1,0:T(4,128)} collective-permute-done((f32[8,128,4,128]{3,2,1,0:T(4,128)S(1)}, f32[8,128,4,128]{3,2,1,0:T(4,128)}, u32[]{:S(2)}, u32[]{:S(2)}) %collective-permute-start.3) | collective-permute-done | bytes 2097184 | tf_op jit(solution)/shard_map/ppermute | solution.py:23
  821.4 2.8 multiply_add_fusion
  824.2 1.8 broadcast_in_dim_reshape.3
  (47 shorter events, 4.0 us)
Async XLA Ops:
  6.5 508.9 %copy-start = (s32[1,32,32]{2,1,0:T(8,128)S(1)}, s32[1,32,32]{2,1,0:T(8,128)}, u32[]{:S(2)}) copy-start(s32[1,32,32]{2,1,0:T(8,128)} %param.9) | copy-start | bytes 12292
  6.5 4.4 copy-start.1
  6.5 69.9 %all-reduce.7.cloned.1.call-start = ((), (), s32[]{:S(2)}) async-start(), calls=%async_computation.1 | async-start | bytes 2097152 | tf_op jit(solution)/shard_map/psum | solution.py:17
  10.9 210.6 %all-reduce.5.cloned.1.call-start = ((), (), s32[]{:S(2)}) async-start(), calls=%async_computation | async-start | bytes 4194304 | tf_op jit(solution)/shard_map/psum | solution.py:17
  12.5 63.9 %copy-start.5 = (f32[1,2,128,512]{3,2,1,0:T(8,128)S(1)}, f32[1,2,128,512]{3,2,1,0:T(8,128)}, u32[]{:S(2)}) copy-start(f32[1,2,128,512]{3,2,1,0:T(8,128)} %param.6) | copy-start | bytes 1572868
  12.5 68.3 %copy-start.6 = (s32[2,32,32]{2,1,0:T(8,128)S(1)}, s32[2,32,32]{2,1,0:T(8,128)}, u32[]{:S(2)}) copy-start(s32[2,32,32]{2,1,0:T(8,128)} %param.7) | copy-start | bytes 24580
  12.5 240.2 %all-gather.3.cloned.1.call-start = ((), (), s32[]{:S(2)}) async-start(), calls=%async_computation.2 | async-start | bytes 1310720 | tf_op jit(solution)/shard_map/all_gather | solution.py:60
  80.2 244.1 %all-reduce.11.cloned.1.call-start = ((), (), s32[]{:S(2)}) async-start(), calls=%async_computation.4 | async-start | bytes 2097152 | tf_op jit(solution)/shard_map/psum | solution.py:17
  252.7 1.6 copy-start.4
  261.9 206.7 %all-reduce.9.cloned.1.call-start = ((), (), s32[]{:S(2)}) async-start(), calls=%async_computation.3 | async-start | bytes 4194304 | tf_op jit(solution)/shard_map/psum | solution.py:17
  262.5 237.0 %all-gather.5.cloned.1.call-start = ((), (), s32[]{:S(2)}) async-start(), calls=%async_computation.5 | async-start | bytes 1310720 | tf_op jit(solution)/shard_map/all_gather | solution.py:60
  506.1 3.1 copy-start.2
  513.5 6.4 collective-permute-start
  522.7 193.8 %collective-permute-start.1 = (f32[8,128,4,128]{3,2,1,0:T(4,128)S(1)}, f32[8,128,4,128]{3,2,1,0:T(4,128)}, u32[]{:S(2)}, u32[]{:S(2)}) collective-permute-start(f32[8,128,4,128]{3,2,1,0:T(4,128)S(1)} %multiply_add_fusion.3), channel_id=1, source_target_pairs={{0,64},{32,96},{64,0},{96,32},{128,192},{160,224},{192,128},{224,1... | collective-permute-start | bytes 6291464 | tf_op jit(solution)/shard_map/ppermute | solution.py:23
  720.0 49.0 %collective-permute-start.2 = (f32[8,128,4,128]{3,2,1,0:T(4,128)}, f32[8,128,4,128]{3,2,1,0:T(4,128)}, u32[]{:S(2)}, u32[]{:S(2)}) collective-permute-start(f32[8,128,4,128]{3,2,1,0:T(4,128)} %multiply_add_fusion.2), channel_id=1, source_target_pairs={{0,128},{32,160},{64,192},{96,224},{128,0},{160,32},{192,64},{224,... | collective-permute-start | bytes 6291464 | tf_op jit(solution)/shard_map/ppermute | solution.py:23
  771.9 2.2 copy-start.3
  771.9 49.4 %collective-permute-start.3 = (f32[8,128,4,128]{3,2,1,0:T(4,128)S(1)}, f32[8,128,4,128]{3,2,1,0:T(4,128)}, u32[]{:S(2)}, u32[]{:S(2)}) collective-permute-start(f32[8,128,4,128]{3,2,1,0:T(4,128)S(1)} %multiply_add_fusion.1), channel_id=1, source_target_pairs={{0,256},{32,288},{64,320},{96,352},{128,384},{160,416},{192,448},{... | collective-permute-start | bytes 6291464 | tf_op jit(solution)/shard_map/ppermute | solution.py:23
Sparse Core Ops, SparseCore 0:
  11.0 65.3 all-reduce.6
  79.6 141.7 all-reduce.4
  223.8 28.8 all-gather.2
  262.0 62.2 all-reduce.10
  327.1 141.4 all-reduce.8
  470.5 28.8 all-gather.4
where the time goes:
time: 833 us
  waiting for transfers between devices  741 us (89%)
  other arithmetic  23.1 us (3%)
  matrix products  20.5 us (2%)
  starting transfers between devices  20 us (2%)
  between operations  14.8 us (2%)
  local copies, waits for them, and re-layouts  13.5 us (2%)
    psum x4, waiting for transfers between devices, broadcast(): return lax.psum(kept, axis)  400 us
    ppermute x4, waiting for transfers between devices, from_partner(): return lax.ppermute(value, axis, pairs)  279 us
    all_gather x2, waiting for transfers between devices, body(): right_side = lax.all_gather(scaled_part, 'row', axis=0, tiled=True)  62.1 us
    dot_general x4, matrix products, matmul(): jnp.dot(left_side, right_side, precision=EXACT_PRECISION, preferred_eleme...  20.5 us
    ppermute x4, starting transfers between devices, from_partner(): return lax.ppermute(value, axis, pairs)  19.6 us
  transfers between devices with their start and end apart: 10, of which 10 were waited for; matrix products, arithmetic and copies ran while one was open for 2% of the time, Pallas kernels for 0%

commit v1 on v0

v1 whole, which is shorter than its diff:
```python
import jax
import jax.numpy as jnp
from jax import lax
from jax.sharding import PartitionSpec as P

F = 4096
P_SIZE = 512
BLK = 128
PB = P_SIZE // BLK


def matmul(left_side, right_side):
    return jnp.dot(
        left_side,
        right_side,
        precision=lax.Precision.HIGH,
        preferred_element_type=jnp.float32,
    )


def xor_send(value, axis, mask):
    pairs = [(source, source ^ mask) for source in range(lax.axis_size(axis))]
    return lax.ppermute(value, axis, pairs)


def pick(parts, index):
    out = parts[0]
    for k in range(1, len(parts)):
        out = jnp.where(index == k, parts[k], out)
    return out


def by_blocks(value, weights):
    rows, cols = value.shape
    wide = jnp.repeat(weights, BLK, axis=1)
    return (value.reshape(rows // BLK, BLK, cols) * wide[:, None, :]).reshape(rows, cols)


def gather_row(part, row):
    got = [part] + [xor_send(part, "row", k) for k in (1, 2, 3)]
    return [pick(got, row ^ q) for q in range(4)]


def body(front, inverses, pattern, order, lists):
    matrix = front[0]
    rows, cols = matrix.shape
    row = lax.axis_index("row")
    col = lax.axis_index("col")
    layer = lax.axis_index("layer")
    q0, q1 = order[0], order[1]
    rb, cb = rows // BLK, cols // BLK
    row_first, col_first = row * rb, col * cb
    half = rows // 2
    quarter = cols // 4

    every_list = lax.all_gather(lists[0], "layer", axis=0)

    h1 = q1 % 2
    own_first = lax.dynamic_slice_in_dim(matrix, h1 * half, half, 0)
    own_rest = lax.dynamic_slice_in_dim(matrix, (1 - h1) * half, half, 0)
    first = lax.psum(jnp.where(col == q0, own_first, 0.0), "col")
    rest = lax.psum(jnp.where(col == q0, own_rest, 0.0), "col")
    c1 = lax.psum(jnp.where(col == q1, matrix, 0.0), "col")

    inv_parts = gather_row(inverses[0], row)
    inv = jnp.concatenate(inv_parts, axis=1)
    cand = jnp.stack(
        [
            lax.dynamic_slice_in_dim(matrix, (q0 % 2) * half, half, 0),
            lax.dynamic_slice_in_dim(matrix, (q1 % 2) * half, half, 0),
        ]
    )

    def quarter_of(value, q):
        return lax.dynamic_slice_in_dim(value, q * quarter, quarter, 2)

    got = [quarter_of(cand, row)] + [
        xor_send(quarter_of(cand, row ^ k), "row", k) for k in (1, 2, 3)
    ]
    r0 = pick([g[0] for g in got], row ^ (q0 // 2))
    r1 = pick([g[1] for g in got], row ^ (q1 // 2))

    s0q = matmul(inv[0], r0)
    s0 = jnp.concatenate(gather_row(s0q, row), axis=1)
    s0xq = lax.psum(jnp.where(col == q1, s0q, 0.0), "col")
    s0x = jnp.concatenate(gather_row(s0xq, row), axis=1)

    panels = jnp.arange(F // P_SIZE)
    alive0 = (panels != q0).astype(jnp.float32)
    alive1 = alive0 * (panels != q1).astype(jnp.float32)
    a0 = jnp.repeat(alive0, PB)
    a1 = jnp.repeat(alive1, PB)
    full0 = pattern[0].astype(jnp.float32) * a0[:, None] * a0[None, :]
    full1 = pattern[1].astype(jnp.float32) * a1[:, None] * a1[None, :]
    keep = a1[:, None] * a1[None, :]

    def block(mask, at, shape):
        return lax.dynamic_slice(mask, at, shape)

    here = ((row_first, col_first), (rb, cb))
    mask0 = block(full0, *here)
    mask1 = block(full1, *here)
    kept = block(keep, *here)
    mask_c = block(full0, (row_first, q1 * PB), (rb, PB))
    mask_r = block(full0, (q1 * PB, col_first), (PB, cb))
    mask_rq = lax.dynamic_slice_in_dim(mask_r, row, 1, 1)

    y_got = [first] + [xor_send(first, "row", k) for k in (1, 2, 3)]
    y = pick(y_got, row ^ (q1 // 2))
    r1 = r1 - by_blocks(matmul(y, s0_quarter(s0, row, quarter)), mask_rq)
    s1q = matmul(inv[1], r1)
    s1 = jnp.concatenate(gather_row(s1q, row), axis=1)

    l0 = jnp.where(
        h1 == 0,
        jnp.concatenate([first, rest], axis=0),
        jnp.concatenate([rest, first], axis=0),
    )
    l1 = c1 - by_blocks(matmul(l0, s0x), mask_c)
    acc = by_blocks(
        matrix - by_blocks(matmul(l0, s0), mask0) - by_blocks(matmul(l1, s1), mask1), kept
    )

    mine = block(lists[0], *here)

    def bit(values, b):
        return (values // 2**b % 2).astype(jnp.float32)

    acc = acc + by_blocks(xor_send(acc, "layer", 1), bit(mine, 0))

    yy = layer // 4
    qrows = rows // 4
    qb = rb // 4
    quarters = acc.reshape(4, qrows, cols)

    def own(q):
        return lax.dynamic_index_in_dim(quarters, q, 0, keepdims=False)

    held = [own(yy)] + [xor_send(own(yy ^ k), "layer", 4 * k) for k in (1, 2, 3)]
    w = [
        lax.dynamic_slice(
            every_list, (layer ^ (4 * k), row_first + yy * qb, col_first), (1, qb, cb)
        )[0]
        for k in range(4)
    ]
    for k in range(4):
        other = xor_send(held[k], "layer", 2)
        held[k] = held[k] + by_blocks(other, bit(w[k], 1))
    for b in (2, 3):
        d = b - 1
        held = [held[k] + by_blocks(held[k ^ d], bit(w[k], b)) for k in range(4)]
    back = [held[0]] + [xor_send(held[k], "layer", 4 * k) for k in (1, 2, 3)]
    out = jnp.zeros((4, qrows, cols), jnp.float32)
    for k in range(4):
        out = lax.dynamic_update_index_in_dim(out, back[k], yy ^ k, 0)
    return out.reshape(1, rows, cols)


def s0_quarter(s0, row, quarter):
    return lax.dynamic_slice_in_dim(s0, row * quarter, quarter, 1)


def solution(mesh):
    placed = (
        P("layer", "row", "col"),
        P("layer", None, "row", None),
        P(),
        P(),
        P("layer", None, None),
    )
    return jax.shard_map(
        body, mesh=mesh, in_specs=placed, out_specs=P("layer", "row", "col"), check_vma=False
    )
```

time: 833 us -> 672 us (0.81)
  waiting for transfers between devices: 741 us -> 463 us
  starting transfers between devices: 20 us -> 113 us
  blocking collectives: 0 us -> 37.9 us
    psum x4 -> x1, waiting for transfers between devices: 400 us -> 217 us  [body(): rest = lax.psum(jnp.where(col == q0, own_rest, 0.0), 'col')]
    ppermute x4 -> x29, starting transfers between devices: 19.6 us -> 113 us  [xor_send(): return lax.ppermute(value, axis, pairs)]
    all_gather x2 -> x0, waiting for transfers between devices: 62.1 us -> none  [body(): right_side = lax.all_gather(scaled_part, 'row', axis=0, tiled=True)]
    all_gather x0 -> x1, blocking collectives: none -> 37.9 us  [body(): every_list = lax.all_gather(lists[0], 'layer', axis=0)]
    ppermute x4 -> x29, waiting for transfers between devices: 279 us -> 246 us  [xor_send(): return lax.ppermute(value, axis, pairs)]
    add x4 -> x3, other arithmetic: 12 us -> 2.88 us  [the longest x1 2.1 us: body(): acc = acc + by_blocks(xor_send(acc, 'layer', 1), bit(mine, 0))]
    dot_general x4 -> x6, matrix products: 20.5 us -> 14.2 us  [matmul(): jnp.dot(left_side, right_side, precision=lax.Precision.HIGH, preferred_el...]
  transfers between devices with their start and end apart: 10 -> 30, of which waited for: 10 -> 19; matrix products, arithmetic and copies ran while one was open for 2% -> 4% of each run, Pallas kernels for 0% -> 0%
where the time goes in v1:
time: 672 us; the launch traced here: 670 us
  waiting for transfers between devices  463 us (69%)
  starting transfers between devices  113 us (17%)
  blocking collectives  37.9 us (6%)
  between operations  21.3 us (3%)
  other arithmetic  14.9 us (2%)
  matrix products  14.2 us (2%)
    ppermute x29, waiting for transfers between devices, xor_send(): return lax.ppermute(value, axis, pairs)  246 us
    psum x1, waiting for transfers between devices, body(): rest = lax.psum(jnp.where(col == q0, own_rest, 0.0), 'col')  217 us
    ppermute x29, starting transfers between devices, xor_send(): return lax.ppermute(value, axis, pairs)  113 us
    all_gather x1, blocking collectives, body(): every_list = lax.all_gather(lists[0], 'layer', axis=0)  37.9 us
    dot_general x6, matrix products, matmul(): jnp.dot(left_side, right_side, precision=lax.Precision.HIGH, preferred_el...  14.2 us
  transfers between devices with their start and end apart: 30, of which 19 were waited for; matrix products, arithmetic and copies ran while one was open for 4% of the time, Pallas kernels for 0%

profile of v1, /device:TPU:24, one launch (start us, length us, event | category | flops | bytes accessed | tf_op | source)
XLA Modules:
  0.0 670.3 jit_solution(3830725769073510616)
XLA Ops:
  6.5 4.7 collective-permute-start
  22.2 3.6 select_bitcast_fusion.1
  27.1 4.7 collective-permute-start.3
  39.9 17.3 %collective-permute-done.3 = f32[2,512,128]{2,1,0:T(8,128)S(1)} collective-permute-done((f32[2,512,128]{2,1,0:T(8,128)}, f32[2,512,128]{2,1,0:T(8,128)S(1)}, u32[]{:S(2)}, u32[]{:S(2)}) %collective-permute-start.3) | collective-permute-done | bytes 524320 | tf_op jit(solution)/shard_map/ppermute | solution.py:23
  61.6 4.7 collective-permute-start.6
  73.1 3.3 collective-permute-done.6
  84.5 217.4 %all-reduce.3.cloned.1.call-done = (f32[512,512]{1,0:T(8,128)}, f32[512,512]{1,0:T(8,128)}, f32[1024,512]{1,0:T(8,128)}, f32[512,128]{0,1:T(8,128)}) async-done(((f32[512,512]{1,0:T(8,128)}, f32[512,512]{1,0:T(8,128)}, f32[1024,512]{1,0:T(8,128)}, f32[512,128]{0,1:T(8,128)}), (f32[512,512]{1,0:T(8,128)}, f32[512,512]{1,0:T(8,128)}, f32[1024,512]{1,0:T(8,128)}, ...) | async-done | bytes 4456464 | tf_op jit(solution)/shard_map/psum | solution.py:62
  301.9 4.7 collective-permute-start.12
  314.3 4.9 collective-permute-start.10
  321.7 3.4 fusion.4
  325.2 27.4 %collective-permute-done.12 = f32[512,512]{1,0:T(8,128)} collective-permute-done((f32[512,512]{1,0:T(8,128)}, f32[512,512]{1,0:T(8,128)}, u32[]{:S(2)}, u32[]{:S(2)}) %collective-permute-start.12) | collective-permute-done | bytes 1048608 | tf_op jit(solution)/shard_map/ppermute | solution.py:23
  352.6 4.6 collective-permute-start.9
  361.0 2.9 collective-permute-start.15
  363.9 4.0 collective-permute-start.16
  367.9 3.1 collective-permute-start.17
  373.8 4.9 collective-permute-done.15
  379.1 3.4 bitcast_multiply_fusion.1
  384.7 37.9 %all_gather.3 = s32[16,32,32]{2,1,0:T(8,128)S(1)} all-gather(s32[1,32,32]{2,1,0:T(8,128)S(1)} %copy-done.17), channel_id=1, replica_groups=mesh['layer'=16,'row'=4,'col'=8] {'layer'}, dimensions={0}, use_global_device_ids=true | all-gather | bytes 69632 | tf_op jit(solution)/shard_map/all_gather | solution.py:56
  427.3 7.0 %collective-permute-start.22 = (f32[256,512]{1,0:T(8,128)S(1)}, f32[256,512]{1,0:T(8,128)S(1)}, u32[]{:S(2)}, u32[]{:S(2)}) collective-permute-start(f32[256,512]{1,0:T(8,128)S(1)} %get-tuple-element.30), channel_id=1, source_target_pairs={{0,256},{32,288},{64,320},{96,352},{128,384},{160,416},{192,448},{... | collective-permute-start | bytes 1572872 | tf_op jit(solution)/shard_map/ppermute | solution.py:23
  436.4 7.5 %collective-permute-start.19 = (f32[256,512]{1,0:T(8,128)S(1)}, f32[256,512]{1,0:T(8,128)S(1)}, u32[]{:S(2)}, u32[]{:S(2)}) collective-permute-start(f32[256,512]{1,0:T(8,128)S(1)} %get-tuple-element.28), channel_id=1, source_target_pairs={{0,64},{32,96},{64,0},{96,32},{128,192},{160,224},{192,128},{224,1... | collective-permute-start | bytes 1572872 | tf_op jit(solution)/shard_map/ppermute | solution.py:23
  443.9 7.1 %collective-permute-start.21 = (f32[256,512]{1,0:T(8,128)S(1)}, f32[256,512]{1,0:T(8,128)S(1)}, u32[]{:S(2)}, u32[]{:S(2)}) collective-permute-start(f32[256,512]{1,0:T(8,128)S(1)} %collective-permute-done.20), channel_id=1, source_target_pairs={{0,64},{32,96},{64,0},{96,32},{128,192},{160,224},{192,128},{224,1... | collective-permute-start | bytes 1572872 | tf_op jit(solution)/shard_map/ppermute | solution.py:23
  451.0 4.8 collective-permute-done.22
  455.8 6.7 collective-permute-start.23
  462.5 7.9 %collective-permute-start.25 = (f32[256,512]{1,0:T(8,128)S(1)}, f32[256,512]{1,0:T(8,128)S(1)}, u32[]{:S(2)}, u32[]{:S(2)}) collective-permute-start(f32[256,512]{1,0:T(8,128)S(1)} %collective-permute-done.24), channel_id=1, source_target_pairs={{0,64},{32,96},{64,0},{96,32},{128,192},{160,224},{192,128},{224,1... | collective-permute-start | bytes 1572872 | tf_op jit(solution)/shard_map/ppermute | solution.py:23
  470.7 121.5 %collective-permute-done.19 = f32[256,512]{1,0:T(8,128)S(1)} collective-permute-done((f32[256,512]{1,0:T(8,128)S(1)}, f32[256,512]{1,0:T(8,128)S(1)}, u32[]{:S(2)}, u32[]{:S(2)}) %collective-permute-start.19) | collective-permute-done | bytes 524320 | tf_op jit(solution)/shard_map/ppermute | solution.py:23
  592.1 11.2 %collective-permute-done.21 = f32[256,512]{1,0:T(8,128)S(1)} collective-permute-done((f32[256,512]{1,0:T(8,128)S(1)}, f32[256,512]{1,0:T(8,128)S(1)}, u32[]{:S(2)}, u32[]{:S(2)}) %collective-permute-start.21) | collective-permute-done | bytes 524320 | tf_op jit(solution)/shard_map/ppermute | solution.py:23
  603.4 11.2 %collective-permute-done.23 = f32[256,512]{1,0:T(8,128)S(1)} collective-permute-done((f32[256,512]{1,0:T(8,128)S(1)}, f32[256,512]{1,0:T(8,128)S(1)}, u32[]{:S(2)}, u32[]{:S(2)}) %collective-permute-start.23) | collective-permute-done | bytes 524320 | tf_op jit(solution)/shard_map/ppermute | solution.py:23
  614.6 11.1 %collective-permute-done.25 = f32[256,512]{1,0:T(8,128)S(1)} collective-permute-done((f32[256,512]{1,0:T(8,128)S(1)}, f32[256,512]{1,0:T(8,128)S(1)}, u32[]{:S(2)}, u32[]{:S(2)}) %collective-permute-start.25) | collective-permute-done | bytes 524320 | tf_op jit(solution)/shard_map/ppermute | solution.py:23
  628.5 6.1 collective-permute-start.27
  637.4 5.9 collective-permute-done.26
  643.3 12.3 %collective-permute-done.27 = f32[256,512]{1,0:T(8,128)S(1)} collective-permute-done((f32[256,512]{1,0:T(8,128)S(1)}, f32[256,512]{1,0:T(8,128)S(1)}, u32[]{:S(2)}, u32[]{:S(2)}) %collective-permute-start.27) | collective-permute-done | bytes 524320 | tf_op jit(solution)/shard_map/ppermute | solution.py:23
  655.7 6.4 collective-permute-done.28
  (141 shorter events, 65.6 us)
Async XLA Ops:
  6.5 295.3 %all-reduce.3.cloned.1.call-start = ((), (), s32[]{:S(2)}) async-start(), calls=%async_computation | async-start | bytes 8912896 | tf_op jit(solution)/shard_map/psum | solution.py:62
  6.5 29.4 %collective-permute-start = (f32[2,128,512]{2,1,0:T(8,128)}, f32[2,128,512]{2,1,0:T(8,128)S(1)}, u32[]{:S(2)}, u32[]{:S(2)}) collective-permute-start(f32[2,128,512]{2,1,0:T(8,128)} %bitcast.324), channel_id=1, source_target_pairs={{0,24},{8,16},{16,8},{24,0},{1,25},{9,17},{17,9},{25,1},{2,26},{10... | collective-permute-start | bytes 1572872 | tf_op jit(solution)/shard_map/ppermute | solution.py:23
  11.2 28.2 %collective-permute-start.1 = (f32[2,128,512]{2,1,0:T(8,128)}, f32[2,128,512]{2,1,0:T(8,128)S(1)}, u32[]{:S(2)}, u32[]{:S(2)}) collective-permute-start(f32[2,128,512]{2,1,0:T(8,128)} %bitcast.325), channel_id=1, source_target_pairs={{0,16},{8,24},{16,0},{24,8},{1,17},{9,25},{17,1},{25,9},{2,18},{10... | collective-permute-start | bytes 1572872 | tf_op jit(solution)/shard_map/ppermute | solution.py:23
  13.9 25.5 %collective-permute-start.2 = (f32[2,128,512]{2,1,0:T(8,128)}, f32[2,128,512]{2,1,0:T(8,128)S(1)}, u32[]{:S(2)}, u32[]{:S(2)}) collective-permute-start(f32[2,128,512]{2,1,0:T(8,128)} %bitcast.326), channel_id=1, source_target_pairs={{0,8},{8,0},{16,24},{24,16},{1,9},{9,1},{17,25},{25,17},{2,10},{10... | collective-permute-start | bytes 1572872 | tf_op jit(solution)/shard_map/ppermute | solution.py:23
  27.1 30.1 %collective-permute-start.3 = (f32[2,512,128]{2,1,0:T(8,128)}, f32[2,512,128]{2,1,0:T(8,128)S(1)}, u32[]{:S(2)}, u32[]{:S(2)}) collective-permute-start(f32[2,512,128]{2,1,0:T(8,128)} %get-tuple-element.32), channel_id=1, source_target_pairs={{0,24},{8,16},{16,8},{24,0},{1,25},{9,17},{17,9},{25,1},{2,26},{10... | collective-permute-start | bytes 1572872 | tf_op jit(solution)/shard_map/ppermute | solution.py:23
  31.8 25.5 %collective-permute-start.4 = (f32[2,512,128]{2,1,0:T(8,128)}, f32[2,512,128]{2,1,0:T(8,128)}, u32[]{:S(2)}, u32[]{:S(2)}) collective-permute-start(f32[2,512,128]{2,1,0:T(8,128)} %get-tuple-element.33), channel_id=1, source_target_pairs={{0,16},{8,24},{16,0},{24,8},{1,17},{9,25},{17,1},{25,9},{2,18},{10... | collective-permute-start | bytes 1572872 | tf_op jit(solution)/shard_map/ppermute | solution.py:23
  35.9 24.0 %collective-permute-start.5 = (f32[2,512,128]{2,1,0:T(8,128)}, f32[2,512,128]{2,1,0:T(8,128)}, u32[]{:S(2)}, u32[]{:S(2)}) collective-permute-start(f32[2,512,128]{2,1,0:T(8,128)} %get-tuple-element.34), channel_id=1, source_target_pairs={{0,8},{8,0},{16,24},{24,16},{1,9},{9,1},{17,25},{25,17},{2,10},{10... | collective-permute-start | bytes 1572872 | tf_op jit(solution)/shard_map/ppermute | solution.py:23
  61.6 14.7 %collective-permute-start.6 = (f32[512,128]{0,1:T(8,128)S(1)}, f32[512,128]{0,1:T(8,128)S(1)}, u32[]{:S(2)}, u32[]{:S(2)}) collective-permute-start(f32[512,128]{0,1:T(8,128)S(1)} %fusion.6), channel_id=1, source_target_pairs={{0,24},{8,16},{16,8},{24,0},{1,25},{9,17},{17,9},{25,1},{2,26},{10... | collective-permute-start | bytes 786440 | tf_op jit(solution)/shard_map/ppermute | solution.py:23
  66.3 12.6 %collective-permute-start.7 = (f32[512,128]{0,1:T(8,128)S(1)}, f32[512,128]{0,1:T(8,128)S(1)}, u32[]{:S(2)}, u32[]{:S(2)}) collective-permute-start(f32[512,128]{0,1:T(8,128)S(1)} %fusion.6), channel_id=1, source_target_pairs={{0,16},{8,24},{16,0},{24,8},{1,17},{9,25},{17,1},{25,9},{2,18},{10... | collective-permute-start | bytes 786440 | tf_op jit(solution)/shard_map/ppermute | solution.py:23
  69.0 10.8 %collective-permute-start.8 = (f32[512,128]{0,1:T(8,128)S(1)}, f32[512,128]{0,1:T(8,128)S(1)}, u32[]{:S(2)}, u32[]{:S(2)}) collective-permute-start(f32[512,128]{0,1:T(8,128)S(1)} %fusion.6), channel_id=1, source_target_pairs={{0,8},{8,0},{16,24},{24,16},{1,9},{9,1},{17,25},{25,17},{2,10},{10... | collective-permute-start | bytes 786440 | tf_op jit(solution)/shard_map/ppermute | solution.py:23
  301.9 50.7 %collective-permute-start.12 = (f32[512,512]{1,0:T(8,128)}, f32[512,512]{1,0:T(8,128)}, u32[]{:S(2)}, u32[]{:S(2)}) collective-permute-start(f32[512,512]{1,0:T(8,128)} %get-tuple-element.6), channel_id=1, source_target_pairs={{0,24},{8,16},{16,8},{24,0},{1,25},{9,17},{17,9},{25,1},{2,26},{10... | collective-permute-start | bytes 3145736 | tf_op jit(solution)/shard_map/ppermute | solution.py:23
  306.6 50.6 %collective-permute-start.13 = (f32[512,512]{1,0:T(8,128)}, f32[512,512]{1,0:T(8,128)}, u32[]{:S(2)}, u32[]{:S(2)}) collective-permute-start(f32[512,512]{1,0:T(8,128)} %get-tuple-element.6), channel_id=1, source_target_pairs={{0,16},{8,24},{16,0},{24,8},{1,17},{9,25},{17,1},{25,9},{2,18},{10... | collective-permute-start | bytes 3145736 | tf_op jit(solution)/shard_map/ppermute | solution.py:23
  309.4 47.8 %collective-permute-start.14 = (f32[512,512]{1,0:T(8,128)}, f32[512,512]{1,0:T(8,128)}, u32[]{:S(2)}, u32[]{:S(2)}) collective-permute-start(f32[512,512]{1,0:T(8,128)} %get-tuple-element.6), channel_id=1, source_target_pairs={{0,8},{8,0},{16,24},{24,16},{1,9},{9,1},{17,25},{25,17},{2,10},{10... | collective-permute-start | bytes 3145736 | tf_op jit(solution)/shard_map/ppermute | solution.py:23
  314.3 53.6 %collective-permute-start.10 = (f32[512,128]{0,1:T(8,128)S(1)}, f32[512,128]{0,1:T(8,128)S(1)}, u32[]{:S(2)}, u32[]{:S(2)}) collective-permute-start(f32[512,128]{0,1:T(8,128)S(1)} %copy-done.15), channel_id=1, source_target_pairs={{0,16},{8,24},{16,0},{24,8},{1,17},{9,25},{17,1},{25,9},{2,18},{10... | collective-permute-start | bytes 786440 | tf_op jit(solution)/shard_map/ppermute | solution.py:23
  319.2 51.8 %collective-permute-start.11 = (f32[512,128]{0,1:T(8,128)S(1)}, f32[512,128]{0,1:T(8,128)S(1)}, u32[]{:S(2)}, u32[]{:S(2)}) collective-permute-start(f32[512,128]{0,1:T(8,128)S(1)} %copy-done.15), channel_id=1, source_target_pairs={{0,8},{8,0},{16,24},{24,16},{1,9},{9,1},{17,25},{25,17},{2,10},{10... | collective-permute-start | bytes 786440 | tf_op jit(solution)/shard_map/ppermute | solution.py:23
  325.2 33.9 %copy-start.2 = (f32[2,512,512]{2,1,0:T(8,128)S(1)}, f32[2,512,512]{2,1,0:T(8,128)}, u32[]{:S(2)}) copy-start(f32[2,512,512]{2,1,0:T(8,128)} %copy-done.1) | copy-start | bytes 6291460
  325.2 33.9 %copy-start.7 = (f32[2,512,128]{2,1,0:T(8,128)S(1)}, f32[2,512,128]{2,1,0:T(8,128)}, u32[]{:S(2)}) copy-start(f32[2,512,128]{2,1,0:T(8,128)} %copy-done.6) | copy-start | bytes 1572868
  352.6 19.2 %collective-permute-start.9 = (f32[512,128]{0,1:T(8,128)S(1)}, f32[512,128]{0,1:T(8,128)S(1)}, u32[]{:S(2)}, u32[]{:S(2)}) collective-permute-start(f32[512,128]{0,1:T(8,128)S(1)} %copy-done.15), channel_id=1, source_target_pairs={{0,24},{8,16},{16,8},{24,0},{1,25},{9,17},{17,9},{25,1},{2,26},{10... | collective-permute-start | bytes 786440 | tf_op jit(solution)/shard_map/ppermute | solution.py:23
  361.0 17.7 %collective-permute-start.15 = (f32[512,128]{0,1:T(8,128)S(1)}, f32[512,128]{0,1:T(8,128)S(1)}, u32[]{:S(2)}, u32[]{:S(2)}) collective-permute-start(f32[512,128]{0,1:T(8,128)S(1)} %fusion.5), channel_id=1, source_target_pairs={{0,24},{8,16},{16,8},{24,0},{1,25},{9,17},{17,9},{25,1},{2,26},{10... | collective-permute-start | bytes 786440 | tf_op jit(solution)/shard_map/ppermute | solution.py:23
  363.9 14.8 %collective-permute-start.16 = (f32[512,128]{0,1:T(8,128)S(1)}, f32[512,128]{0,1:T(8,128)S(1)}, u32[]{:S(2)}, u32[]{:S(2)}) collective-permute-start(f32[512,128]{0,1:T(8,128)S(1)} %fusion.5), channel_id=1, source_target_pairs={{0,16},{8,24},{16,0},{24,8},{1,17},{9,25},{17,1},{25,9},{2,18},{10... | collective-permute-start | bytes 786440 | tf_op jit(solution)/shard_map/ppermute | solution.py:23
  367.9 11.0 %collective-permute-start.17 = (f32[512,128]{0,1:T(8,128)S(1)}, f32[512,128]{0,1:T(8,128)S(1)}, u32[]{:S(2)}, u32[]{:S(2)}) collective-permute-start(f32[512,128]{0,1:T(8,128)S(1)} %fusion.5), channel_id=1, source_target_pairs={{0,8},{8,0},{16,24},{24,16},{1,9},{9,1},{17,25},{25,17},{2,10},{10... | collective-permute-start | bytes 786440 | tf_op jit(solution)/shard_map/ppermute | solution.py:23
  382.5 40.5 %collective-permute-start.18 = (f32[1024,512]{1,0:T(8,128)}, f32[1024,512]{1,0:T(8,128)S(1)}, u32[]{:S(2)}, u32[]{:S(2)}) collective-permute-start(f32[1024,512]{1,0:T(8,128)} %bitcast_multiply_fusion.1), channel_id=1, source_target_pairs={{0,32},{32,0},{64,96},{96,64},{128,160},{160,128},{192,224},{224,1... | collective-permute-start | bytes 6291464 | tf_op jit(solution)/shard_map/ppermute | solution.py:23
  425.4 18.5 %collective-permute-start.20 = (f32[256,512]{1,0:T(8,128)S(1)}, f32[256,512]{1,0:T(8,128)S(1)}, u32[]{:S(2)}, u32[]{:S(2)}) collective-permute-start(f32[256,512]{1,0:T(8,128)S(1)} %get-tuple-element.31), channel_id=1, source_target_pairs={{0,128},{32,160},{64,192},{96,224},{128,0},{160,32},{192,64},{224,... | collective-permute-start | bytes 1572872 | tf_op jit(solution)/shard_map/ppermute | solution.py:23
  427.3 28.5 %collective-permute-start.22 = (f32[256,512]{1,0:T(8,128)S(1)}, f32[256,512]{1,0:T(8,128)S(1)}, u32[]{:S(2)}, u32[]{:S(2)}) collective-permute-start(f32[256,512]{1,0:T(8,128)S(1)} %get-tuple-element.30), channel_id=1, source_target_pairs={{0,256},{32,288},{64,320},{96,352},{128,384},{160,416},{192,448},{... | collective-permute-start | bytes 1572872 | tf_op jit(solution)/shard_map/ppermute | solution.py:23
  434.3 28.2 %collective-permute-start.24 = (f32[256,512]{1,0:T(8,128)S(1)}, f32[256,512]{1,0:T(8,128)S(1)}, u32[]{:S(2)}, u32[]{:S(2)}) collective-permute-start(f32[256,512]{1,0:T(8,128)S(1)} %get-tuple-element.29), channel_id=1, source_target_pairs={{0,384},{32,416},{64,448},{96,480},{128,256},{160,288},{192,320},{... | collective-permute-start | bytes 1572872 | tf_op jit(solution)/shard_map/ppermute | solution.py:23
  436.4 155.7 %collective-permute-start.19 = (f32[256,512]{1,0:T(8,128)S(1)}, f32[256,512]{1,0:T(8,128)S(1)}, u32[]{:S(2)}, u32[]{:S(2)}) collective-permute-start(f32[256,512]{1,0:T(8,128)S(1)} %get-tuple-element.28), channel_id=1, source_target_pairs={{0,64},{32,96},{64,0},{96,32},{128,192},{160,224},{192,128},{224,1... | collective-permute-start | bytes 1572872 | tf_op jit(solution)/shard_map/ppermute | solution.py:23
  443.9 159.5 %collective-permute-start.21 = (f32[256,512]{1,0:T(8,128)S(1)}, f32[256,512]{1,0:T(8,128)S(1)}, u32[]{:S(2)}, u32[]{:S(2)}) collective-permute-start(f32[256,512]{1,0:T(8,128)S(1)} %collective-permute-done.20), channel_id=1, source_target_pairs={{0,64},{32,96},{64,0},{96,32},{128,192},{160,224},{192,128},{224,1... | collective-permute-start | bytes 1572872 | tf_op jit(solution)/shard_map/ppermute | solution.py:23
  455.8 158.8 %collective-permute-start.23 = (f32[256,512]{1,0:T(8,128)S(1)}, f32[256,512]{1,0:T(8,128)S(1)}, u32[]{:S(2)}, u32[]{:S(2)}) collective-permute-start(f32[256,512]{1,0:T(8,128)S(1)} %collective-permute-done.22), channel_id=1, source_target_pairs={{0,64},{32,96},{64,0},{96,32},{128,192},{160,224},{192,128},{224,1... | collective-permute-start | bytes 1572872 | tf_op jit(solution)/shard_map/ppermute | solution.py:23
  462.5 163.3 %collective-permute-start.25 = (f32[256,512]{1,0:T(8,128)S(1)}, f32[256,512]{1,0:T(8,128)S(1)}, u32[]{:S(2)}, u32[]{:S(2)}) collective-permute-start(f32[256,512]{1,0:T(8,128)S(1)} %collective-permute-done.24), channel_id=1, source_target_pairs={{0,64},{32,96},{64,0},{96,32},{128,192},{160,224},{192,128},{224,1... | collective-permute-start | bytes 1572872 | tf_op jit(solution)/shard_map/ppermute | solution.py:23
  626.6 16.7 %collective-permute-start.26 = (f32[256,512]{1,0:T(8,128)S(1)}, f32[256,512]{1,0:T(8,128)S(1)}, u32[]{:S(2)}, u32[]{:S(2)}) collective-permute-start(f32[256,512]{1,0:T(8,128)S(1)} %fusion.32), channel_id=1, source_target_pairs={{0,128},{32,160},{64,192},{96,224},{128,0},{160,32},{192,64},{224,... | collective-permute-start | bytes 1572872 | tf_op jit(solution)/shard_map/ppermute | solution.py:23
  628.5 27.2 %collective-permute-start.27 = (f32[256,512]{1,0:T(8,128)S(1)}, f32[256,512]{1,0:T(8,128)S(1)}, u32[]{:S(2)}, u32[]{:S(2)}) collective-permute-start(f32[256,512]{1,0:T(8,128)S(1)} %get-tuple-element.25), channel_id=1, source_target_pairs={{0,256},{32,288},{64,320},{96,352},{128,384},{160,416},{192,448},{... | collective-permute-start | bytes 1572872 | tf_op jit(solution)/shard_map/ppermute | solution.py:23
  634.6 27.5 %collective-permute-start.28 = (f32[256,512]{1,0:T(8,128)S(1)}, f32[256,512]{1,0:T(8,128)S(1)}, u32[]{:S(2)}, u32[]{:S(2)}) collective-permute-start(f32[256,512]{1,0:T(8,128)S(1)} %get-tuple-element.9), channel_id=1, source_target_pairs={{0,384},{32,416},{64,448},{96,480},{128,256},{160,288},{192,320},{... | collective-permute-start | bytes 1572872 | tf_op jit(solution)/shard_map/ppermute | solution.py:23
  (16 other events, 244.3 us)
Sparse Core Ops, SparseCore 0:
  81.1 220.6 all-reduce.2

commit v2 on v1

v2 whole, which is shorter than its diff:
```python
import functools

import jax
import jax.numpy as jnp
from jax import lax
from jax.experimental import pallas as pl
from jax.experimental.pallas import tpu as pltpu
from jax.sharding import PartitionSpec as P

F = 4096
P_SIZE = 512
BLK = 128
PB = P_SIZE // BLK
STEP = 2


def matmul(left_side, right_side):
    return jnp.dot(
        left_side,
        right_side,
        precision=lax.Precision.HIGH,
        preferred_element_type=jnp.float32,
    )


def xor_send(value, axis, mask):
    pairs = [(source, source ^ mask) for source in range(lax.axis_size(axis))]
    return lax.ppermute(value, axis, pairs)


def pick(parts, index):
    out = parts[0]
    for k in range(1, len(parts)):
        out = jnp.where(index == k, parts[k], out)
    return out


def by_blocks(value, weights):
    rows, cols = value.shape
    wide = jnp.repeat(weights, BLK, axis=1)
    return (value.reshape(rows // BLK, BLK, cols) * wide[:, None, :]).reshape(rows, cols)


def gather_row(part, row):
    got = [part] + [xor_send(part, "row", k) for k in (1, 2, 3)]
    return [pick(got, row ^ q) for q in range(4)]


def exchange_row(candidate, row, source):
    quarter = candidate.shape[1] // 4

    def part(q):
        return lax.dynamic_slice_in_dim(candidate, q * quarter, quarter, 1)

    got = [part(row)] + [xor_send(part(row ^ k), "row", k) for k in (1, 2, 3)]
    return pick(got, row ^ source)


def spread(panel, col, source):
    count = lax.axis_size("col")
    share = panel.shape[0] // count

    def branch(origin, value):
        def part(t):
            return value[t * share : (t + 1) * share]

        order = sorted((t for t in range(count) if t != origin), key=lambda t: -abs(t - origin))
        total = jnp.where(col == origin, part(origin), 0.0)
        for t in order:
            total = jnp.where(col == t, lax.ppermute(part(t), "col", [(origin, t)]), total)
        return total

    return lax.switch(source, [functools.partial(branch, p) for p in range(count)], panel)


def blocks_of(rows, cols):
    return [(i, j) for i in range(rows // BLK) for j in range(cols // BLK)]


def pack_kernel(slots, value, packed):
    for b, (i, j) in enumerate(blocks_of(*value.shape)):
        slot = slots[b]

        @pl.when(slot >= 0)
        def _():
            packed[slot] = value[i * BLK : (i + 1) * BLK, j * BLK : (j + 1) * BLK]


def add_kernel(slots, value, packed, out):
    for b, (i, j) in enumerate(blocks_of(*value.shape)):
        slot = slots[b]
        at = (slice(i * BLK, (i + 1) * BLK), slice(j * BLK, (j + 1) * BLK))

        @pl.when(slot >= 0)
        def _():
            out[at] = value[at] + packed[slot]

        @pl.when(slot < 0)
        def _():
            out[at] = value[at]


SMEM = pl.BlockSpec(memory_space=pltpu.SMEM)
VMEM = pl.BlockSpec(memory_space=pltpu.VMEM)
PARAMS = pltpu.CompilerParams(vmem_limit_bytes=24 * 2**20)


def pack(slots, value, size):
    return pl.pallas_call(
        pack_kernel,
        out_shape=jax.ShapeDtypeStruct((size, BLK, BLK), jnp.float32),
        in_specs=[SMEM, VMEM],
        out_specs=VMEM,
        compiler_params=PARAMS,
    )(slots, value)


def add_packed(slots, value, packed):
    return pl.pallas_call(
        add_kernel,
        out_shape=jax.ShapeDtypeStruct(value.shape, jnp.float32),
        in_specs=[SMEM, VMEM, VMEM],
        out_specs=VMEM,
        compiler_params=PARAMS,
    )(slots, value, packed)


def slots_of(wanted):
    flat = wanted.reshape(-1).astype(jnp.int32)
    return jnp.where(flat > 0, jnp.cumsum(flat) - 1, -1), jnp.sum(flat)


def listed_exchange(acc, wanted_here, wanted_there, mask):
    to_send, n_send = slots_of(wanted_there)
    to_add, n_add = slots_of(wanted_here)
    most = to_send.shape[0]

    def branch(size, value):
        packed = pack(to_send, value, size)
        return add_packed(to_add, value, xor_send(packed, "layer", mask))

    choices = [lambda value: value]
    choices += [functools.partial(branch, s) for s in range(STEP, most + 1, STEP)]
    return lax.switch((jnp.maximum(n_send, n_add) + STEP - 1) // STEP, choices, acc)


def body(front, inverses, pattern, order, lists):
    matrix = front[0]
    rows, cols = matrix.shape
    row = lax.axis_index("row")
    col = lax.axis_index("col")
    layer = lax.axis_index("layer")
    q0, q1 = order[0], order[1]
    rb, cb = rows // BLK, cols // BLK
    row_first, col_first = row * rb, col * cb
    half = rows // 2
    quarter = cols // 4

    panels = jnp.arange(F // P_SIZE)
    alive0 = (panels != q0).astype(jnp.float32)
    alive1 = alive0 * (panels != q1).astype(jnp.float32)
    a0 = jnp.repeat(alive0, PB)
    a1 = jnp.repeat(alive1, PB)
    here = ((row_first, col_first), (rb, cb))
    mask0 = lax.dynamic_slice(pattern[0].astype(jnp.float32) * a0[:, None] * a0[None, :], *here)
    mask1 = lax.dynamic_slice(pattern[1].astype(jnp.float32) * a1[:, None] * a1[None, :], *here)
    kept = lax.dynamic_slice(a1[:, None] * a1[None, :], *here)

    share = spread(matrix, col, q0)
    share, inverse_part, matrix, mine = lax.optimization_barrier(
        (share, inverses[0], matrix, lists[0])
    )
    left = lax.all_gather(share, "col", axis=0, tiled=True)
    mine = lax.dynamic_slice(mine, *here)
    theirs = xor_send(mine, "layer", 2)
    listed = [mine] + [xor_send(mine, "layer", 4 * k) for k in (1, 2, 3)]
    inv = jnp.concatenate(gather_row(inverse_part, row), axis=1)
    candidate = lax.dynamic_slice_in_dim(matrix, (q0 % 2) * half, half, 0)
    scaled = matmul(inv[0], exchange_row(candidate, row, q0 // 2))
    right = jnp.concatenate(gather_row(scaled, row), axis=1)
    matrix = matrix - by_blocks(matmul(left, right), mask0)

    share = spread(matrix, col, q1)
    share, matrix = lax.optimization_barrier((share, matrix))
    left = lax.all_gather(share, "col", axis=0, tiled=True)
    candidate = lax.dynamic_slice_in_dim(matrix, (q1 % 2) * half, half, 0)
    scaled = matmul(inv[1], exchange_row(candidate, row, q1 // 2))
    right = jnp.concatenate(gather_row(scaled, row), axis=1)
    acc = by_blocks(matrix - by_blocks(matmul(left, right), mask1), kept)

    def bit(values, b):
        return (values // 2**b % 2).astype(jnp.float32)

    acc = acc + by_blocks(xor_send(acc, "layer", 1), bit(mine, 0))

    acc = listed_exchange(acc, bit(mine, 1) * kept > 0, bit(theirs, 1) * kept > 0, 2)

    yy = layer // 4
    qrows = rows // 4
    qb = rb // 4
    quarters = acc.reshape(4, qrows, cols)

    def own(q):
        return lax.dynamic_index_in_dim(quarters, q, 0, keepdims=False)

    held = [own(yy)] + [xor_send(own(yy ^ k), "layer", 4 * k) for k in (1, 2, 3)]
    w = [lax.dynamic_slice_in_dim(values, yy * qb, qb, 0) for values in listed]
    for b in (2, 3):
        d = b - 1
        held = [held[k] + by_blocks(held[k ^ d], bit(w[k], b)) for k in range(4)]
    back = [held[0]] + [xor_send(held[k], "layer", 4 * k) for k in (1, 2, 3)]
    out = jnp.zeros((4, qrows, cols), jnp.float32)
    for k in range(4):
        out = lax.dynamic_update_index_in_dim(out, back[k], yy ^ k, 0)
    return out.reshape(1, rows, cols)


def solution(mesh):
    placed = (
        P("layer", "row", "col"),
        P("layer", None, "row", None),
        P(),
        P(),
        P("layer", None, None),
    )
    return jax.shard_map(
        body, mesh=mesh, in_specs=placed, out_specs=P("layer", "row", "col"), check_vma=False
    )
```

time: 672 us -> 676 us (level); the launches traced: 670 us -> 664 us
  starting transfers between devices: 113 us -> 444 us
  waiting for transfers between devices: 463 us -> 149 us
  blocking collectives: 37.9 us -> 0 us
  local copies, waits for them, and re-layouts: 5.55 us -> 16.5 us
    psum x1 -> x0, waiting for transfers between devices: 217 us -> none  [body(): rest = lax.psum(jnp.where(col == q0, own_rest, 0.0), 'col')]
    ppermute x29 -> x27, starting transfers between devices: 113 us -> 307 us  [xor_send(): return lax.ppermute(value, axis, pairs)]
    ppermute x29 -> x27, waiting for transfers between devices: 246 us -> 108 us  [xor_send(): return lax.ppermute(value, axis, pairs)]
    ppermute x0 -> x14, starting transfers between devices: none -> 137 us  [branch(): lax.ppermute(part(t), 'col', [(origin, t)])]
    all_gather x1 -> x0, blocking collectives: 37.9 us -> none  [body(): every_list = lax.all_gather(lists[0], 'layer', axis=0)]
    ppermute x0 -> x14, waiting for transfers between devices: none -> 25.6 us  [branch(): lax.ppermute(part(t), 'col', [(origin, t)])]
    all_gather x0 -> x2, waiting for transfers between devices: none -> 16.1 us  [body(): left = lax.all_gather(share, 'col', axis=0, tiled=True)]
    dot_general x6 -> x4, matrix products: 14.2 us -> 12.7 us  [matmul(): jnp.dot(left_side, right_side, precision=lax.Precision.HIGH, preferred_el...]
  transfers between devices with their start and end apart: 30 -> 43, of which waited for: 19 -> 17; matrix products, arithmetic and copies ran while one was open for 4% -> 3% of each run, Pallas kernels for 0% -> 1%
where the time goes in v2:
time: 676 us; the launch traced here: 664 us
  starting transfers between devices  444 us (66%)
  waiting for transfers between devices  149 us (22%)
  between operations  22.2 us (3%)
  local copies, waits for them, and re-layouts  16.5 us (2%)
  other arithmetic  14.4 us (2%)
  matrix products  12.7 us (2%)
    ppermute x27, starting transfers between devices, xor_send(): return lax.ppermute(value, axis, pairs)  307 us
    ppermute x14, starting transfers between devices, branch(): lax.ppermute(part(t), 'col', [(origin, t)])  137 us
    ppermute x27, waiting for transfers between devices, xor_send(): return lax.ppermute(value, axis, pairs)  108 us
    ppermute x14, waiting for transfers between devices, branch(): lax.ppermute(part(t), 'col', [(origin, t)])  25.6 us
    all_gather x2, waiting for transfers between devices, body(): left = lax.all_gather(share, 'col', axis=0, tiled=True)  16.1 us
  transfers between devices with their start and end apart: 43, of which 17 were waited for; matrix products, arithmetic and copies ran while one was open for 3% of the time, Pallas kernels for 1%

profile of v2, /device:TPU:24, one launch (start us, length us, event | category | flops | bytes accessed | tf_op | source)
XLA Modules:
  0.0 664.1 jit_solution(13581355129546124657)
XLA Ops:
  8.6 17.3 %conditional.3 = (f32[128,512]{1,0:T(8,128)S(1)}) conditional(s32[]{:T(128)} %clamp.45, (s32[]{:T(128)}, f32[1024,512]{1,0:T(8,128)}) %tuple.402, (s32[]{:T(128)}, f32[1024,512]{1,0:T(8,128)}) %tuple.403, (s32[]{:T(128)}, f32[1024,512]{1,0:T(8,128)}) %tuple.404, (s32[]{:T(128)}, f32[1024,512]{1,0:T(8,128)}) %tuple.405, ...), branch_computations={%region_0.1_spmd, %region_1.2_spmd, %region_2.3_spmd, %region_3.4_... | conditional | flops 524296 | bytes 13369712 | solution.py:73
  15.0 8.3 %collective-permute-done.24 = f32[128,512]{1,0:T(8,128)S(1)} collective-permute-done((f32[128,512]{1,0:T(8,128)S(1)}, f32[128,512]{1,0:T(8,128)S(1)}, u32[]{:S(2)}, u32[]{:S(2)}) %collective-permute-start.24) | collective-permute-done | bytes 262176 | tf_op jit(solution)/shard_map/cond/branch_1_fun/ppermute | solution.py:70
  40.1 43.3 %collective-permute-start.132 = (f32[512,128]{1,0:T(8,128)S(1)}, f32[512,128]{1,0:T(8,128)S(1)}, u32[]{:S(2)}, u32[]{:S(2)}) collective-permute-start(f32[512,128]{1,0:T(8,128)S(1)} %get-tuple-element.1024), channel_id=1, source_target_pairs={{0,24},{8,16},{16,8},{24,0},{1,25},{9,17},{17,9},{25,1},{2,26},{10... | collective-permute-start | bytes 786440 | tf_op jit(solution)/shard_map/ppermute | solution.py:28
  83.4 19.0 %collective-permute-start.133 = (f32[512,128]{1,0:T(8,128)S(1)}, f32[512,128]{1,0:T(8,128)S(1)}, u32[]{:S(2)}, u32[]{:S(2)}) collective-permute-start(f32[512,128]{1,0:T(8,128)S(1)} %get-tuple-element.1023), channel_id=1, source_target_pairs={{0,16},{8,24},{16,0},{24,8},{1,17},{9,25},{17,1},{25,9},{2,18},{10... | collective-permute-start | bytes 786440 | tf_op jit(solution)/shard_map/ppermute | solution.py:28
  105.7 19.0 %collective-permute-start.134 = (f32[512,128]{1,0:T(8,128)S(1)}, f32[512,128]{1,0:T(8,128)S(1)}, u32[]{:S(2)}, u32[]{:S(2)}) collective-permute-start(f32[512,128]{1,0:T(8,128)S(1)} %get-tuple-element.1022), channel_id=1, source_target_pairs={{0,8},{8,0},{16,24},{24,16},{1,9},{9,1},{17,25},{25,17},{2,10},{10... | collective-permute-start | bytes 786440 | tf_op jit(solution)/shard_map/ppermute | solution.py:28
  125.3 7.5 %collective-permute-done.134 = f32[512,128]{1,0:T(8,128)S(1)} collective-permute-done((f32[512,128]{1,0:T(8,128)S(1)}, f32[512,128]{1,0:T(8,128)S(1)}, u32[]{:S(2)}, u32[]{:S(2)}) %collective-permute-start.134) | collective-permute-done | bytes 262176 | tf_op jit(solution)/shard_map/ppermute | solution.py:28
  145.6 5.6 collective-permute-done.135
  158.1 149.8 %conditional.4 = (f32[128,512]{1,0:T(8,128)S(1)}) conditional(s32[]{:T(128)} %clamp.47, (s32[]{:T(128)}, f32[1024,512]{1,0:T(8,128)S(1)}) %tuple.181, (s32[]{:T(128)}, f32[1024,512]{1,0:T(8,128)S(1)}) %tuple.181, (s32[]{:T(128)}, f32[1024,512]{1,0:T(8,128)S(1)}) %tuple.181, (s32[]{:T(128)}, ...), branch_computations={%region_10.11_spmd, %region_11.12_spmd, %region_12.13_spmd, %regio... | conditional | flops 524296 | bytes 15466920 | solution.py:73
  158.3 18.1 %collective-permute-start.121 = (f32[128,512]{1,0:T(8,128)S(1)}, f32[128,512]{1,0:T(8,128)S(1)}, u32[]{:S(2)}, u32[]{:S(2)}) collective-permute-start(f32[128,512]{1,0:T(8,128)S(1)} %get-tuple-element.1009), channel_id=1, source_target_pairs={{7,6},{15,14},{23,22},{31,30},{39,38},{47,46},{55,54},{63,62},{71,... | collective-permute-start | bytes 786440 | tf_op jit(solution)/shard_map/cond/branch_7_fun/ppermute | solution.py:70
  176.4 18.4 %collective-permute-start.122 = (f32[128,512]{1,0:T(8,128)S(1)}, f32[128,512]{1,0:T(8,128)S(1)}, u32[]{:S(2)}, u32[]{:S(2)}) collective-permute-start(f32[128,512]{1,0:T(8,128)S(1)} %get-tuple-element.1008), channel_id=1, source_target_pairs={{7,5},{15,13},{23,21},{31,29},{39,37},{47,45},{55,53},{63,61},{71,... | collective-permute-start | bytes 786440 | tf_op jit(solution)/shard_map/cond/branch_7_fun/ppermute | solution.py:70
  194.8 19.1 %collective-permute-start.123 = (f32[128,512]{1,0:T(8,128)S(1)}, f32[128,512]{1,0:T(8,128)}, u32[]{:S(2)}, u32[]{:S(2)}) collective-permute-start(f32[128,512]{1,0:T(8,128)S(1)} %get-tuple-element.1007), channel_id=1, source_target_pairs={{7,4},{15,12},{23,20},{31,28},{39,36},{47,44},{55,52},{63,60},{71,... | collective-permute-start | bytes 786440 | tf_op jit(solution)/shard_map/cond/branch_7_fun/ppermute | solution.py:70
  213.8 19.1 %collective-permute-start.124 = (f32[128,512]{1,0:T(8,128)S(1)}, f32[128,512]{1,0:T(8,128)}, u32[]{:S(2)}, u32[]{:S(2)}) collective-permute-start(f32[128,512]{1,0:T(8,128)S(1)} %get-tuple-element.1006), channel_id=1, source_target_pairs={{7,3},{15,11},{23,19},{31,27},{39,35},{47,43},{55,51},{63,59},{71,... | collective-permute-start | bytes 786440 | tf_op jit(solution)/shard_map/cond/branch_7_fun/ppermute | solution.py:70
  232.9 19.1 %collective-permute-start.125 = (f32[128,512]{1,0:T(8,128)S(1)}, f32[128,512]{1,0:T(8,128)}, u32[]{:S(2)}, u32[]{:S(2)}) collective-permute-start(f32[128,512]{1,0:T(8,128)S(1)} %get-tuple-element.1005), channel_id=1, source_target_pairs={{7,2},{15,10},{23,18},{31,26},{39,34},{47,42},{55,50},{63,58},{71,... | collective-permute-start | bytes 786440 | tf_op jit(solution)/shard_map/cond/branch_7_fun/ppermute | solution.py:70
  252.0 19.1 %collective-permute-start.126 = (f32[128,512]{1,0:T(8,128)S(1)}, f32[128,512]{1,0:T(8,128)}, u32[]{:S(2)}, u32[]{:S(2)}) collective-permute-start(f32[128,512]{1,0:T(8,128)S(1)} %get-tuple-element.1004), channel_id=1, source_target_pairs={{7,1},{15,9},{23,17},{31,25},{39,33},{47,41},{55,49},{63,57},{71,6... | collective-permute-start | bytes 786440 | tf_op jit(solution)/shard_map/cond/branch_7_fun/ppermute | solution.py:70
  271.1 18.4 %collective-permute-start.127 = (f32[128,512]{1,0:T(8,128)S(1)}, f32[128,512]{1,0:T(8,128)}, u32[]{:S(2)}, u32[]{:S(2)}) collective-permute-start(f32[128,512]{1,0:T(8,128)S(1)} %get-tuple-element.1003), channel_id=1, source_target_pairs={{7,0},{15,8},{23,16},{31,24},{39,32},{47,40},{55,48},{63,56},{71,6... | collective-permute-start | bytes 786440 | tf_op jit(solution)/shard_map/cond/branch_7_fun/ppermute | solution.py:70
  289.5 17.3 %collective-permute-done.127 = f32[128,512]{1,0:T(8,128)} collective-permute-done((f32[128,512]{1,0:T(8,128)S(1)}, f32[128,512]{1,0:T(8,128)}, u32[]{:S(2)}, u32[]{:S(2)}) %collective-permute-start.127) | collective-permute-done | bytes 262176 | tf_op jit(solution)/shard_map/cond/branch_7_fun/ppermute | solution.py:70
  322.1 5.7 collective-permute-done.138
  340.0 11.6 %collective-permute-start.143 = (f32[512,128]{0,1:T(8,128)S(1)}, f32[512,128]{0,1:T(8,128)}, u32[]{:S(2)}, u32[]{:S(2)}) collective-permute-start(f32[512,128]{0,1:T(8,128)S(1)} %fusion.3), channel_id=1, source_target_pairs={{0,8},{8,0},{16,24},{24,16},{1,9},{9,1},{17,25},{25,17},{2,10},{10... | collective-permute-start | bytes 786440 | tf_op jit(solution)/shard_map/ppermute | solution.py:28
  358.9 16.1 %all-gather.5.cloned.1.call-done = f32[1024,512]{1,0:T(8,128)} async-done(((f32[128,512]{1,0:T(8,128)}), f32[1024,512]{1,0:T(8,128)}) %all-gather.5.cloned.1.call-update) | async-done | bytes 2097168 | tf_op jit(solution)/shard_map/all_gather | solution.py:185
  379.7 12.0 %collective-permute-start.144 = (f32[1024,512]{1,0:T(8,128)}, f32[1024,512]{1,0:T(8,128)S(1)}, u32[]{:S(2)}, u32[]{:S(2)}) collective-permute-start(f32[1024,512]{1,0:T(8,128)} %bitcast_multiply_fusion.1), channel_id=1, source_target_pairs={{0,32},{32,0},{64,96},{96,64},{128,160},{160,128},{192,224},{224,1... | collective-permute-start | bytes 6291464 | tf_op jit(solution)/shard_map/ppermute | solution.py:28
  392.5 14.2 %collective-permute-start.128 = (s32[8,4]{1,0:T(8,128)S(1)}, s32[8,4]{1,0:T(8,128)S(1)}, u32[]{:S(2)}, u32[]{:S(2)}) collective-permute-start(s32[8,4]{1,0:T(8,128)S(1)} %get-tuple-element.897), channel_id=1, source_target_pairs={{0,64},{32,96},{64,0},{96,32},{128,192},{160,224},{192,128},{224,1... | collective-permute-start | bytes 392 | tf_op jit(solution)/shard_map/ppermute | solution.py:28
  413.4 9.6 %collective-permute-start.149 = (s32[8,4]{1,0:T(8,128)S(1)}, s32[8,4]{1,0:T(8,128)S(1)}, u32[]{:S(2)}, u32[]{:S(2)}) collective-permute-start(s32[8,4]{1,0:T(8,128)S(1)} %get-tuple-element.897), channel_id=1, source_target_pairs={{0,128},{32,160},{64,192},{96,224},{128,0},{160,32},{192,64},{224,... | collective-permute-start | bytes 392 | tf_op jit(solution)/shard_map/ppermute | solution.py:28
  432.2 53.2 %conditional.5 = (f32[4,256,512]{2,1,0:T(8,128)}) conditional(s32[]{:T(128)} %clamp.46, f32[1024,512]{1,0:T(8,128)} %fusion, (pred[8,4]{1,0:T(8,128)(4,1)S(1)}, s32[32,1]{1,0:T(8,128)S(1)}, pred[8,4]{1,0:T(8,128)(4,1)S(1)}, s32[32,1]{1,0:T(8,128)S(1)}, f32[1024,512]{1,0:T(8,128)S(1)}) %tuple.381, ...), branch_computations={%region_20.21_spmd, %region_21.22_spmd, %region_22.23_spmd, %regio... | conditional | flops 256 | bytes 16779148 | solution.py:144
  434.4 14.2 %collective-permute-start.6 = (f32[14,128,128]{2,1,0:T(8,128)S(1)}, f32[14,128,128]{2,1,0:T(8,128)S(1)}, u32[]{:S(2)}, u32[]{:S(2)}) collective-permute-start(f32[14,128,128]{2,1,0:T(8,128)S(1)} %branch_7_fun.2), channel_id=1, source_target_pairs={{0,64},{32,96},{64,0},{96,32},{128,192},{160,224},{192,128},{224,1... | collective-permute-start | bytes 2752520 | tf_op jit(solution)/shard_map/cond/branch_7_fun/ppermute | solution.py:28
  448.8 32.9 %collective-permute-done.6.packed = f32[14,128,128]{2,1,0:T(8,128)S(1)} collective-permute-done((f32[14,128,128]{2,1,0:T(8,128)S(1)}, f32[14,128,128]{2,1,0:T(8,128)S(1)}, u32[]{:S(2)}, u32[]{:S(2)}) %collective-permute-start.6) | collective-permute-done | bytes 917536 | tf_op jit(solution)/shard_map/cond/branch_7_fun/ppermute | solution.py:28
  486.9 85.7 %collective-permute-start.145 = (f32[256,512]{1,0:T(8,128)S(1)}, f32[256,512]{1,0:T(8,128)S(1)}, u32[]{:S(2)}, u32[]{:S(2)}) collective-permute-start(f32[256,512]{1,0:T(8,128)S(1)} %get-tuple-element.1016), channel_id=1, source_target_pairs={{0,128},{32,160},{64,192},{96,224},{128,0},{160,32},{192,64},{224,... | collective-permute-start | bytes 1572872 | tf_op jit(solution)/shard_map/ppermute | solution.py:28
  580.8 5.3 collective-permute-done.145
  586.1 11.5 %collective-permute-done.146 = f32[256,512]{1,0:T(8,128)S(1)} collective-permute-done((f32[256,512]{1,0:T(8,128)S(1)}, f32[256,512]{1,0:T(8,128)S(1)}, u32[]{:S(2)}, u32[]{:S(2)}) %collective-permute-start.146) | collective-permute-done | bytes 524320 | tf_op jit(solution)/shard_map/ppermute | solution.py:28
  597.6 6.4 collective-permute-done.147
  605.4 18.7 %collective-permute-start.151 = (f32[256,512]{1,0:T(8,128)S(1)}, f32[256,512]{1,0:T(8,128)S(1)}, u32[]{:S(2)}, u32[]{:S(2)}) collective-permute-start(f32[256,512]{1,0:T(8,128)S(1)} %get-tuple-element.1011), channel_id=1, source_target_pairs={{0,128},{32,160},{64,192},{96,224},{128,0},{160,32},{192,64},{224,... | collective-permute-start | bytes 1572872 | tf_op jit(solution)/shard_map/ppermute | solution.py:28
  637.6 11.4 %collective-permute-done.152 = f32[256,512]{1,0:T(8,128)S(1)} collective-permute-done((f32[256,512]{1,0:T(8,128)S(1)}, f32[256,512]{1,0:T(8,128)S(1)}, u32[]{:S(2)}, u32[]{:S(2)}) %collective-permute-start.152) | collective-permute-done | bytes 524320 | tf_op jit(solution)/shard_map/ppermute | solution.py:28
  649.1 6.4 collective-permute-done.153
  (161 shorter events, 128.6 us)
Async XLA Ops:
  6.5 147.4 %all-gather.3.cloned.1.call-start = ((), (), s32[]{:S(2)}) async-start(), calls=%async_computation | async-start | bytes 2359296 | tf_op jit(solution)/shard_map/all_gather | solution.py:173
  26.6 348.3 %all-gather.5.cloned.1.call-start = ((), (), s32[]{:S(2)}) async-start(), calls=%async_computation.1 | async-start | bytes 2359296 | tf_op jit(solution)/shard_map/all_gather | solution.py:185
  26.7 79.0 %collective-permute-start.129 = (f32[2,128,512]{2,1,0:T(8,128)S(1)}, f32[2,128,512]{2,1,0:T(8,128)S(1)}, u32[]{:S(2)}, u32[]{:S(2)}) collective-permute-start(f32[2,128,512]{2,1,0:T(8,128)S(1)} %bitcast.247), channel_id=1, source_target_pairs={{0,24},{8,16},{16,8},{24,0},{1,25},{9,17},{17,9},{25,1},{2,26},{10... | collective-permute-start | bytes 1572872 | tf_op jit(solution)/shard_map/ppermute | solution.py:28
  31.3 93.4 %collective-permute-start.130 = (f32[2,128,512]{2,1,0:T(8,128)S(1)}, f32[2,128,512]{2,1,0:T(8,128)S(1)}, u32[]{:S(2)}, u32[]{:S(2)}) collective-permute-start(f32[2,128,512]{2,1,0:T(8,128)S(1)} %bitcast.248), channel_id=1, source_target_pairs={{0,16},{8,24},{16,0},{24,8},{1,17},{9,25},{17,1},{25,9},{2,18},{10... | collective-permute-start | bytes 1572872 | tf_op jit(solution)/shard_map/ppermute | solution.py:28
  34.1 90.7 %collective-permute-start.131 = (f32[2,128,512]{2,1,0:T(8,128)S(1)}, f32[2,128,512]{2,1,0:T(8,128)S(1)}, u32[]{:S(2)}, u32[]{:S(2)}) collective-permute-start(f32[2,128,512]{2,1,0:T(8,128)S(1)} %bitcast.249), channel_id=1, source_target_pairs={{0,8},{8,0},{16,24},{24,16},{1,9},{9,1},{17,25},{25,17},{2,10},{10... | collective-permute-start | bytes 1572872 | tf_op jit(solution)/shard_map/ppermute | solution.py:28
  40.1 85.2 %collective-permute-start.132 = (f32[512,128]{1,0:T(8,128)S(1)}, f32[512,128]{1,0:T(8,128)S(1)}, u32[]{:S(2)}, u32[]{:S(2)}) collective-permute-start(f32[512,128]{1,0:T(8,128)S(1)} %get-tuple-element.1024), channel_id=1, source_target_pairs={{0,24},{8,16},{16,8},{24,0},{1,25},{9,17},{17,9},{25,1},{2,26},{10... | collective-permute-start | bytes 786440 | tf_op jit(solution)/shard_map/ppermute | solution.py:28
  83.4 41.9 %collective-permute-start.133 = (f32[512,128]{1,0:T(8,128)S(1)}, f32[512,128]{1,0:T(8,128)S(1)}, u32[]{:S(2)}, u32[]{:S(2)}) collective-permute-start(f32[512,128]{1,0:T(8,128)S(1)} %get-tuple-element.1023), channel_id=1, source_target_pairs={{0,16},{8,24},{16,0},{24,8},{1,17},{9,25},{17,1},{25,9},{2,18},{10... | collective-permute-start | bytes 786440 | tf_op jit(solution)/shard_map/ppermute | solution.py:28
  105.7 27.1 %collective-permute-start.134 = (f32[512,128]{1,0:T(8,128)S(1)}, f32[512,128]{1,0:T(8,128)S(1)}, u32[]{:S(2)}, u32[]{:S(2)}) collective-permute-start(f32[512,128]{1,0:T(8,128)S(1)} %get-tuple-element.1022), channel_id=1, source_target_pairs={{0,8},{8,0},{16,24},{24,16},{1,9},{9,1},{17,25},{25,17},{2,10},{10... | collective-permute-start | bytes 786440 | tf_op jit(solution)/shard_map/ppermute | solution.py:28
  134.6 16.6 %collective-permute-start.135 = (f32[512,128]{0,1:T(8,128)S(1)}, f32[512,128]{0,1:T(8,128)S(1)}, u32[]{:S(2)}, u32[]{:S(2)}) collective-permute-start(f32[512,128]{0,1:T(8,128)S(1)} %fusion.4), channel_id=1, source_target_pairs={{0,24},{8,16},{16,8},{24,0},{1,25},{9,17},{17,9},{25,1},{2,26},{10... | collective-permute-start | bytes 786440 | tf_op jit(solution)/shard_map/ppermute | solution.py:28
  158.3 93.7 %collective-permute-start.121 = (f32[128,512]{1,0:T(8,128)S(1)}, f32[128,512]{1,0:T(8,128)S(1)}, u32[]{:S(2)}, u32[]{:S(2)}) collective-permute-start(f32[128,512]{1,0:T(8,128)S(1)} %get-tuple-element.1009), channel_id=1, source_target_pairs={{7,6},{15,14},{23,22},{31,30},{39,38},{47,46},{55,54},{63,62},{71,... | collective-permute-start | bytes 786440 | tf_op jit(solution)/shard_map/cond/branch_7_fun/ppermute | solution.py:70
  176.4 94.7 %collective-permute-start.122 = (f32[128,512]{1,0:T(8,128)S(1)}, f32[128,512]{1,0:T(8,128)S(1)}, u32[]{:S(2)}, u32[]{:S(2)}) collective-permute-start(f32[128,512]{1,0:T(8,128)S(1)} %get-tuple-element.1008), channel_id=1, source_target_pairs={{7,5},{15,13},{23,21},{31,29},{39,37},{47,45},{55,53},{63,61},{71,... | collective-permute-start | bytes 786440 | tf_op jit(solution)/shard_map/cond/branch_7_fun/ppermute | solution.py:70
  194.8 94.6 %collective-permute-start.123 = (f32[128,512]{1,0:T(8,128)S(1)}, f32[128,512]{1,0:T(8,128)}, u32[]{:S(2)}, u32[]{:S(2)}) collective-permute-start(f32[128,512]{1,0:T(8,128)S(1)} %get-tuple-element.1007), channel_id=1, source_target_pairs={{7,4},{15,12},{23,20},{31,28},{39,36},{47,44},{55,52},{63,60},{71,... | collective-permute-start | bytes 786440 | tf_op jit(solution)/shard_map/cond/branch_7_fun/ppermute | solution.py:70
  213.8 75.6 %collective-permute-start.124 = (f32[128,512]{1,0:T(8,128)S(1)}, f32[128,512]{1,0:T(8,128)}, u32[]{:S(2)}, u32[]{:S(2)}) collective-permute-start(f32[128,512]{1,0:T(8,128)S(1)} %get-tuple-element.1006), channel_id=1, source_target_pairs={{7,3},{15,11},{23,19},{31,27},{39,35},{47,43},{55,51},{63,59},{71,... | collective-permute-start | bytes 786440 | tf_op jit(solution)/shard_map/cond/branch_7_fun/ppermute | solution.py:70
  232.9 56.5 %collective-permute-start.125 = (f32[128,512]{1,0:T(8,128)S(1)}, f32[128,512]{1,0:T(8,128)}, u32[]{:S(2)}, u32[]{:S(2)}) collective-permute-start(f32[128,512]{1,0:T(8,128)S(1)} %get-tuple-element.1005), channel_id=1, source_target_pairs={{7,2},{15,10},{23,18},{31,26},{39,34},{47,42},{55,50},{63,58},{71,... | collective-permute-start | bytes 786440 | tf_op jit(solution)/shard_map/cond/branch_7_fun/ppermute | solution.py:70
  252.0 37.4 %collective-permute-start.126 = (f32[128,512]{1,0:T(8,128)S(1)}, f32[128,512]{1,0:T(8,128)}, u32[]{:S(2)}, u32[]{:S(2)}) collective-permute-start(f32[128,512]{1,0:T(8,128)S(1)} %get-tuple-element.1004), channel_id=1, source_target_pairs={{7,1},{15,9},{23,17},{31,25},{39,33},{47,41},{55,49},{63,57},{71,6... | collective-permute-start | bytes 786440 | tf_op jit(solution)/shard_map/cond/branch_7_fun/ppermute | solution.py:70
  271.1 35.7 %collective-permute-start.127 = (f32[128,512]{1,0:T(8,128)S(1)}, f32[128,512]{1,0:T(8,128)}, u32[]{:S(2)}, u32[]{:S(2)}) collective-permute-start(f32[128,512]{1,0:T(8,128)S(1)} %get-tuple-element.1003), channel_id=1, source_target_pairs={{7,0},{15,8},{23,16},{31,24},{39,32},{47,40},{55,48},{63,56},{71,6... | collective-permute-start | bytes 786440 | tf_op jit(solution)/shard_map/cond/branch_7_fun/ppermute | solution.py:70
  311.5 16.2 %collective-permute-start.138 = (f32[512,128]{1,0:T(8,128)}, f32[512,128]{1,0:T(8,128)S(1)}, u32[]{:S(2)}, u32[]{:S(2)}) collective-permute-start(f32[512,128]{1,0:T(8,128)} %get-tuple-element.1021), channel_id=1, source_target_pairs={{0,24},{8,16},{16,8},{24,0},{1,25},{9,17},{17,9},{25,1},{2,26},{10... | collective-permute-start | bytes 786440 | tf_op jit(solution)/shard_map/ppermute | solution.py:28
  332.6 19.2 %collective-permute-start.141 = (f32[512,128]{0,1:T(8,128)S(1)}, f32[512,128]{0,1:T(8,128)S(1)}, u32[]{:S(2)}, u32[]{:S(2)}) collective-permute-start(f32[512,128]{0,1:T(8,128)S(1)} %fusion.3), channel_id=1, source_target_pairs={{0,24},{8,16},{16,8},{24,0},{1,25},{9,17},{17,9},{25,1},{2,26},{10... | collective-permute-start | bytes 786440 | tf_op jit(solution)/shard_map/ppermute | solution.py:28
  337.3 14.6 %collective-permute-start.142 = (f32[512,128]{0,1:T(8,128)S(1)}, f32[512,128]{0,1:T(8,128)S(1)}, u32[]{:S(2)}, u32[]{:S(2)}) collective-permute-start(f32[512,128]{0,1:T(8,128)S(1)} %fusion.3), channel_id=1, source_target_pairs={{0,16},{8,24},{16,0},{24,8},{1,17},{9,25},{17,1},{25,9},{2,18},{10... | collective-permute-start | bytes 786440 | tf_op jit(solution)/shard_map/ppermute | solution.py:28
  340.0 17.5 %collective-permute-start.143 = (f32[512,128]{0,1:T(8,128)S(1)}, f32[512,128]{0,1:T(8,128)}, u32[]{:S(2)}, u32[]{:S(2)}) collective-permute-start(f32[512,128]{0,1:T(8,128)S(1)} %fusion.3), channel_id=1, source_target_pairs={{0,8},{8,0},{16,24},{24,16},{1,9},{9,1},{17,25},{25,17},{2,10},{10... | collective-permute-start | bytes 786440 | tf_op jit(solution)/shard_map/ppermute | solution.py:28
  379.7 47.5 %collective-permute-start.144 = (f32[1024,512]{1,0:T(8,128)}, f32[1024,512]{1,0:T(8,128)S(1)}, u32[]{:S(2)}, u32[]{:S(2)}) collective-permute-start(f32[1024,512]{1,0:T(8,128)} %bitcast_multiply_fusion.1), channel_id=1, source_target_pairs={{0,32},{32,0},{64,96},{96,64},{128,160},{160,128},{192,224},{224,1... | collective-permute-start | bytes 6291464 | tf_op jit(solution)/shard_map/ppermute | solution.py:28
  392.5 32.4 %collective-permute-start.128 = (s32[8,4]{1,0:T(8,128)S(1)}, s32[8,4]{1,0:T(8,128)S(1)}, u32[]{:S(2)}, u32[]{:S(2)}) collective-permute-start(s32[8,4]{1,0:T(8,128)S(1)} %get-tuple-element.897), channel_id=1, source_target_pairs={{0,64},{32,96},{64,0},{96,32},{128,192},{160,224},{192,128},{224,1... | collective-permute-start | bytes 392 | tf_op jit(solution)/shard_map/ppermute | solution.py:28
  406.7 20.3 %collective-permute-start.150 = (s32[8,4]{1,0:T(8,128)S(1)}, s32[8,4]{1,0:T(8,128)S(1)}, u32[]{:S(2)}, u32[]{:S(2)}) collective-permute-start(s32[8,4]{1,0:T(8,128)S(1)} %get-tuple-element.897), channel_id=1, source_target_pairs={{0,384},{32,416},{64,448},{96,480},{128,256},{160,288},{192,320},{... | collective-permute-start | bytes 392 | tf_op jit(solution)/shard_map/ppermute | solution.py:28
  409.0 18.2 %collective-permute-start.148 = (s32[8,4]{1,0:T(8,128)S(1)}, s32[8,4]{1,0:T(8,128)S(1)}, u32[]{:S(2)}, u32[]{:S(2)}) collective-permute-start(s32[8,4]{1,0:T(8,128)S(1)} %get-tuple-element.897), channel_id=1, source_target_pairs={{0,256},{32,288},{64,320},{96,352},{128,384},{160,416},{192,448},{... | collective-permute-start | bytes 392 | tf_op jit(solution)/shard_map/ppermute | solution.py:28
  413.4 167.3 %collective-permute-start.149 = (s32[8,4]{1,0:T(8,128)S(1)}, s32[8,4]{1,0:T(8,128)S(1)}, u32[]{:S(2)}, u32[]{:S(2)}) collective-permute-start(s32[8,4]{1,0:T(8,128)S(1)} %get-tuple-element.897), channel_id=1, source_target_pairs={{0,128},{32,160},{64,192},{96,224},{128,0},{160,32},{192,64},{224,... | collective-permute-start | bytes 392 | tf_op jit(solution)/shard_map/ppermute | solution.py:28
  434.4 47.3 %collective-permute-start.6 = (f32[14,128,128]{2,1,0:T(8,128)S(1)}, f32[14,128,128]{2,1,0:T(8,128)S(1)}, u32[]{:S(2)}, u32[]{:S(2)}) collective-permute-start(f32[14,128,128]{2,1,0:T(8,128)S(1)} %branch_7_fun.2), channel_id=1, source_target_pairs={{0,64},{32,96},{64,0},{96,32},{128,192},{160,224},{192,128},{224,1... | collective-permute-start | bytes 2752520 | tf_op jit(solution)/shard_map/cond/branch_7_fun/ppermute | solution.py:28
  486.9 99.2 %collective-permute-start.145 = (f32[256,512]{1,0:T(8,128)S(1)}, f32[256,512]{1,0:T(8,128)S(1)}, u32[]{:S(2)}, u32[]{:S(2)}) collective-permute-start(f32[256,512]{1,0:T(8,128)S(1)} %get-tuple-element.1016), channel_id=1, source_target_pairs={{0,128},{32,160},{64,192},{96,224},{128,0},{160,32},{192,64},{224,... | collective-permute-start | bytes 1572872 | tf_op jit(solution)/shard_map/ppermute | solution.py:28
  572.7 25.0 %collective-permute-start.146 = (f32[256,512]{1,0:T(8,128)S(1)}, f32[256,512]{1,0:T(8,128)S(1)}, u32[]{:S(2)}, u32[]{:S(2)}) collective-permute-start(f32[256,512]{1,0:T(8,128)S(1)} %get-tuple-element.1018), channel_id=1, source_target_pairs={{0,256},{32,288},{64,320},{96,352},{128,384},{160,416},{192,448},{... | collective-permute-start | bytes 1572872 | tf_op jit(solution)/shard_map/ppermute | solution.py:28
  576.0 28.0 %collective-permute-start.147 = (f32[256,512]{1,0:T(8,128)S(1)}, f32[256,512]{1,0:T(8,128)S(1)}, u32[]{:S(2)}, u32[]{:S(2)}) collective-permute-start(f32[256,512]{1,0:T(8,128)S(1)} %get-tuple-element.1017), channel_id=1, source_target_pairs={{0,384},{32,416},{64,448},{96,480},{128,256},{160,288},{192,320},{... | collective-permute-start | bytes 1572872 | tf_op jit(solution)/shard_map/ppermute | solution.py:28
  605.4 32.2 %collective-permute-start.151 = (f32[256,512]{1,0:T(8,128)S(1)}, f32[256,512]{1,0:T(8,128)S(1)}, u32[]{:S(2)}, u32[]{:S(2)}) collective-permute-start(f32[256,512]{1,0:T(8,128)S(1)} %get-tuple-element.1011), channel_id=1, source_target_pairs={{0,128},{32,160},{64,192},{96,224},{128,0},{160,32},{192,64},{224,... | collective-permute-start | bytes 1572872 | tf_op jit(solution)/shard_map/ppermute | solution.py:28
  624.1 25.0 %collective-permute-start.152 = (f32[256,512]{1,0:T(8,128)S(1)}, f32[256,512]{1,0:T(8,128)S(1)}, u32[]{:S(2)}, u32[]{:S(2)}) collective-permute-start(f32[256,512]{1,0:T(8,128)S(1)} %get-tuple-element.1015), channel_id=1, source_target_pairs={{0,256},{32,288},{64,320},{96,352},{128,384},{160,416},{192,448},{... | collective-permute-start | bytes 1572872 | tf_op jit(solution)/shard_map/ppermute | solution.py:28
  627.4 28.0 %collective-permute-start.153 = (f32[256,512]{1,0:T(8,128)S(1)}, f32[256,512]{1,0:T(8,128)S(1)}, u32[]{:S(2)}, u32[]{:S(2)}) collective-permute-start(f32[256,512]{1,0:T(8,128)S(1)} %get-tuple-element.1010), channel_id=1, source_target_pairs={{0,384},{32,416},{64,448},{96,480},{128,256},{160,288},{192,320},{... | collective-permute-start | bytes 1572872 | tf_op jit(solution)/shard_map/ppermute | solution.py:28
  (22 other events, 297.2 us)
Sparse Core Ops, SparseCore 0:
  26.7 97.9 all-gather.2
  308.7 66.1 all-gather.4

commit v3 on v2

--- a/solution.py
+++ b/solution.py
@@ -56,21 +56,8 @@
     return pick(got, row ^ source)
 
 
-def spread(panel, col, source):
-    count = lax.axis_size("col")
-    share = panel.shape[0] // count
-
-    def branch(origin, value):
-        def part(t):
-            return value[t * share : (t + 1) * share]
-
-        order = sorted((t for t in range(count) if t != origin), key=lambda t: -abs(t - origin))
-        total = jnp.where(col == origin, part(origin), 0.0)
-        for t in order:
-            total = jnp.where(col == t, lax.ppermute(part(t), "col", [(origin, t)]), total)
-        return total
-
-    return lax.switch(source, [functools.partial(branch, p) for p in range(count)], panel)
+def spread(panel, source):
+    return lax.psum(jnp.where(lax.axis_index("col") == source, panel, 0.0), "col")
 
 
 def blocks_of(rows, cols):
@@ -166,23 +153,18 @@
     mask1 = lax.dynamic_slice(pattern[1].astype(jnp.float32) * a1[:, None] * a1[None, :], *here)
     kept = lax.dynamic_slice(a1[:, None] * a1[None, :], *here)
 
-    share = spread(matrix, col, q0)
-    share, inverse_part, matrix, mine = lax.optimization_barrier(
-        (share, inverses[0], matrix, lists[0])
-    )
-    left = lax.all_gather(share, "col", axis=0, tiled=True)
-    mine = lax.dynamic_slice(mine, *here)
+    left = spread(matrix, q0)
+    mine = lax.dynamic_slice(lists[0], *here)
     theirs = xor_send(mine, "layer", 2)
     listed = [mine] + [xor_send(mine, "layer", 4 * k) for k in (1, 2, 3)]
-    inv = jnp.concatenate(gather_row(inverse_part, row), axis=1)
+    inv = jnp.concatenate(gather_row(inverses[0], row), axis=1)
     candidate = lax.dynamic_slice_in_dim(matrix, (q0 % 2) * half, half, 0)
     scaled = matmul(inv[0], exchange_row(candidate, row, q0 // 2))
     right = jnp.concatenate(gather_row(scaled, row), axis=1)
+    right, theirs, listed = lax.optimization_barrier((right, theirs, listed))
     matrix = matrix - by_blocks(matmul(left, right), mask0)
 
-    share = spread(matrix, col, q1)
-    share, matrix = lax.optimization_barrier((share, matrix))
-    left = lax.all_gather(share, "col", axis=0, tiled=True)
+    left = spread(matrix, q1)
     candidate = lax.dynamic_slice_in_dim(matrix, (q1 % 2) * half, half, 0)
     scaled = matmul(inv[1], exchange_row(candidate, row, q1 // 2))
     right = jnp.concatenate(gather_row(scaled, row), axis=1)

time: 676 us -> 534 us (0.79)
  the two profiles are of different devices: /device:TPU:24 before, /device:TPU:224 now
where the time goes in v3:
time: 534 us; the launch traced here: 533 us
  waiting for transfers between devices  360 us (67%)
  starting transfers between devices  107 us (20%)
  between operations  21.5 us (4%)
  other arithmetic  14.2 us (3%)
  matrix products  13 us (2%)
  local copies, waits for them, and re-layouts  12.4 us (2%)
    psum x2, waiting for transfers between devices, spread(): lax.psum(jnp.where(lax.axis_index('col') == source, panel, 0.0), 'col')  187 us
    ppermute x27, waiting for transfers between devices, xor_send(): return lax.ppermute(value, axis, pairs)  174 us
    ppermute x27, starting transfers between devices, xor_send(): return lax.ppermute(value, axis, pairs)  107 us
    dot_general x4, matrix products, matmul(): jnp.dot(left_side, right_side, precision=lax.Precision.HIGH, preferred_el...  13 us
  transfers between devices with their start and end apart: 29, of which 20 were waited for; matrix products, arithmetic and copies ran while one was open for 3% of the time, Pallas kernels for 0%

profile of v3, /device:TPU:224, one launch (start us, length us, event | category | flops | bytes accessed | tf_op | source)
XLA Modules:
  0.0 532.9 jit_solution(14532997795531475382)
XLA Ops:
  6.5 4.8 collective-permute-start.16
  16.7 8.2 %collective-permute-start.25 = (s32[8,4]{0,1:T(4,128)S(1)}, s32[8,4]{0,1:T(4,128)S(1)}, u32[]{:S(2)}, u32[]{:S(2)}) collective-permute-start(s32[8,4]{0,1:T(4,128)S(1)} %bitcast.262), channel_id=1, source_target_pairs={{0,64},{32,96},{64,0},{96,32},{128,192},{160,224},{192,128},{224,1... | collective-permute-start | bytes 392 | tf_op jit(solution)/shard_map/ppermute | solution.py:28
  24.9 3.5 collective-permute-start.26
  30.3 3.1 bitcast_select_fusion.32
  37.5 4.7 collective-permute-start.19
  49.1 2.9 collective-permute-done.19
  52.0 2.8 collective-permute-done.20
  56.2 4.7 collective-permute-start.22
  69.1 4.8 collective-permute-start.27
  76.8 3.8 collective-permute-done.28
  80.6 88.1 %all-reduce.3.cloned.1.call-done = f32[1024,512]{1,0:T(8,128)} async-done(((f32[1024,512]{1,0:T(8,128)}), f32[1024,512]{1,0:T(8,128)}) %all-reduce.3.cloned.1.call-update) | async-done | bytes 2097168 | tf_op jit(solution)/shard_map/psum | solution.py:60
  168.7 5.4 %broadcast_select_fusion = (f32[1024,512]{1,0:T(8,128)}, f32[1024,512]{1,0:T(8,128)S(1)}) fusion(pred[]{:T(512)S(6)} %eq.116, f32[8,512]{1,0:T(8,128)S(1)} %broadcast_bitcast_fusion.3, f32[1024,512]{1,0:T(8,128)} %all-reduce.3.cloned.1.call-done, f32[512,512]{0,1:T(8,128)S(1)} %pad_maximum_fusion.1, f32[1,1024,512]{2,1,0:T(8,128)} %param.22), kind=kOutput, calls=%fused_computation.117 | convolution fusion | flops 1612185600 | bytes 9453569 | tf_op jit(solution)/shard_map/dot_general | solution.py:18
  176.8 4.5 collective-permute-start.29
  181.3 2.9 collective-permute-start.30
  194.8 4.2 collective-permute-start.32
  199.0 2.9 collective-permute-start.33
  205.5 3.3 collective-permute-done.33
  211.6 98.5 %all-reduce.5.cloned.1.call-done = f32[1024,512]{1,0:T(8,128)} async-done(((f32[1024,512]{1,0:T(8,128)}), f32[1024,512]{1,0:T(8,128)}) %all-reduce.5.cloned.1.call-update) | async-done | bytes 2097168 | tf_op jit(solution)/shard_map/psum | solution.py:60
  310.0 4.8 bitcast_multiply_fusion.1
  321.1 3.4 fusion
  326.1 121.2 %conditional.1 = (f32[4,256,512]{2,1,0:T(8,128)}) conditional(s32[]{:T(128)} %clamp.43, f32[1024,512]{1,0:T(8,128)} %fusion, (pred[8,4]{0,1:T(4,128)(4,1)S(1)}, s32[32,1]{1,0:T(8,128)S(1)}, pred[8,4]{0,1:T(4,128)(4,1)S(1)}, s32[32,1]{1,0:T(8,128)S(1)}, f32[1024,512]{1,0:T(8,128)S(1)}) %tuple.235, ...), branch_computations={%region_6.7_spmd, %region_7.8_spmd, %region_8.9_spmd, %region_9.10... | conditional | flops 256 | bytes 16779276 | solution.py:131
  328.3 9.2 %collective-permute-start.9 = (f32[20,128,128]{2,1,0:T(8,128)S(1)}, f32[20,128,128]{2,1,0:T(8,128)S(1)}, u32[]{:S(2)}, u32[]{:S(2)}) collective-permute-start(f32[20,128,128]{2,1,0:T(8,128)S(1)} %branch_10_fun.2), channel_id=1, source_target_pairs={{0,64},{32,96},{64,0},{96,32},{128,192},{160,224},{192,128},{224,1... | collective-permute-start | bytes 3932168 | tf_op jit(solution)/shard_map/cond/branch_10_fun/ppermute | solution.py:28
  337.9 106.0 %collective-permute-done.9.packed = f32[20,128,128]{2,1,0:T(8,128)S(1)} collective-permute-done((f32[20,128,128]{2,1,0:T(8,128)S(1)}, f32[20,128,128]{2,1,0:T(8,128)S(1)}, u32[]{:S(2)}, u32[]{:S(2)}) %collective-permute-start.9) | collective-permute-done | bytes 1310752 | tf_op jit(solution)/shard_map/cond/branch_10_fun/ppermute | solution.py:28
  443.8 3.5 branch_10_fun.3
  450.7 13.3 %collective-permute-start.37 = (f32[256,512]{1,0:T(8,128)S(1)}, f32[256,512]{1,0:T(8,128)S(1)}, u32[]{:S(2)}, u32[]{:S(2)}) collective-permute-start(f32[256,512]{1,0:T(8,128)S(1)} %get-tuple-element.791), channel_id=1, source_target_pairs={{0,256},{32,288},{64,320},{96,352},{128,384},{160,416},{192,448},{... | collective-permute-start | bytes 1572872 | tf_op jit(solution)/shard_map/ppermute | solution.py:28
  466.4 18.8 %collective-permute-done.37 = f32[256,512]{1,0:T(8,128)S(1)} collective-permute-done((f32[256,512]{1,0:T(8,128)S(1)}, f32[256,512]{1,0:T(8,128)S(1)}, u32[]{:S(2)}, u32[]{:S(2)}) %collective-permute-start.37) | collective-permute-done | bytes 524320 | tf_op jit(solution)/shard_map/ppermute | solution.py:28
  485.2 6.4 %collective-permute-done.38 = f32[256,512]{1,0:T(8,128)S(1)} collective-permute-done((f32[256,512]{1,0:T(8,128)S(1)}, f32[256,512]{1,0:T(8,128)S(1)}, u32[]{:S(2)}, u32[]{:S(2)}) %collective-permute-start.38) | collective-permute-done | bytes 524320 | tf_op jit(solution)/shard_map/ppermute | solution.py:28
  494.9 2.9 collective-permute-start.40
  497.8 5.6 %collective-permute-start.41 = (f32[256,512]{1,0:T(8,128)S(1)}, f32[256,512]{1,0:T(8,128)S(1)}, u32[]{:S(2)}, u32[]{:S(2)}) collective-permute-start(f32[256,512]{1,0:T(8,128)S(1)} %get-tuple-element.783), channel_id=1, source_target_pairs={{0,384},{32,416},{64,448},{96,480},{128,256},{160,288},{192,320},{... | collective-permute-start | bytes 1572872 | tf_op jit(solution)/shard_map/ppermute | solution.py:28
  503.7 6.0 %collective-permute-done.39 = f32[256,512]{1,0:T(8,128)S(1)} collective-permute-done((f32[256,512]{1,0:T(8,128)S(1)}, f32[256,512]{1,0:T(8,128)S(1)}, u32[]{:S(2)}, u32[]{:S(2)}) %collective-permute-start.39) | collective-permute-done | bytes 524320 | tf_op jit(solution)/shard_map/ppermute | solution.py:28
  509.8 7.7 %collective-permute-done.40 = f32[256,512]{1,0:T(8,128)S(1)} collective-permute-done((f32[256,512]{1,0:T(8,128)S(1)}, f32[256,512]{1,0:T(8,128)S(1)}, u32[]{:S(2)}, u32[]{:S(2)}) %collective-permute-start.40) | collective-permute-done | bytes 524320 | tf_op jit(solution)/shard_map/ppermute | solution.py:28
  517.6 7.1 %collective-permute-done.41 = f32[256,512]{1,0:T(8,128)S(1)} collective-permute-done((f32[256,512]{1,0:T(8,128)S(1)}, f32[256,512]{1,0:T(8,128)S(1)}, u32[]{:S(2)}, u32[]{:S(2)}) %collective-permute-start.41) | collective-permute-done | bytes 524320 | tf_op jit(solution)/shard_map/ppermute | solution.py:28
  (141 shorter events, 63.8 us)
Async XLA Ops:
  6.5 10.0 %copy-start = (s32[1,32,32]{2,1,0:T(8,128)S(1)}, s32[1,32,32]{2,1,0:T(8,128)}, u32[]{:S(2)}) copy-start(s32[1,32,32]{2,1,0:T(8,128)} %param.26) | copy-start | bytes 12292
  6.5 162.1 %all-reduce.3.cloned.1.call-start = ((), (), s32[]{:S(2)}) async-start(), calls=%async_computation | async-start | bytes 4194304 | tf_op jit(solution)/shard_map/psum | solution.py:60
  6.5 31.0 %collective-permute-start.16 = (f32[2,128,512]{2,1,0:T(8,128)}, f32[2,128,512]{2,1,0:T(8,128)S(1)}, u32[]{:S(2)}, u32[]{:S(2)}) collective-permute-start(f32[2,128,512]{2,1,0:T(8,128)} %bitcast.259), channel_id=1, source_target_pairs={{0,24},{8,16},{16,8},{24,0},{1,25},{9,17},{17,9},{25,1},{2,26},{10... | collective-permute-start | bytes 1572872 | tf_op jit(solution)/shard_map/ppermute | solution.py:28
  11.3 30.9 %collective-permute-start.17 = (f32[2,128,512]{2,1,0:T(8,128)}, f32[2,128,512]{2,1,0:T(8,128)}, u32[]{:S(2)}, u32[]{:S(2)}) collective-permute-start(f32[2,128,512]{2,1,0:T(8,128)} %bitcast.260), channel_id=1, source_target_pairs={{0,16},{8,24},{16,0},{24,8},{1,17},{9,25},{17,1},{25,9},{2,18},{10... | collective-permute-start | bytes 1572872 | tf_op jit(solution)/shard_map/ppermute | solution.py:28
  14.1 30.9 %collective-permute-start.18 = (f32[2,128,512]{2,1,0:T(8,128)}, f32[2,128,512]{2,1,0:T(8,128)}, u32[]{:S(2)}, u32[]{:S(2)}) collective-permute-start(f32[2,128,512]{2,1,0:T(8,128)} %bitcast.261), channel_id=1, source_target_pairs={{0,8},{8,0},{16,24},{24,16},{1,9},{9,1},{17,25},{25,17},{2,10},{10... | collective-permute-start | bytes 1572872 | tf_op jit(solution)/shard_map/ppermute | solution.py:28
  16.7 60.1 %collective-permute-start.25 = (s32[8,4]{0,1:T(4,128)S(1)}, s32[8,4]{0,1:T(4,128)S(1)}, u32[]{:S(2)}, u32[]{:S(2)}) collective-permute-start(s32[8,4]{0,1:T(4,128)S(1)} %bitcast.262), channel_id=1, source_target_pairs={{0,64},{32,96},{64,0},{96,32},{128,192},{160,224},{192,128},{224,1... | collective-permute-start | bytes 392 | tf_op jit(solution)/shard_map/ppermute | solution.py:28
  24.9 51.9 %collective-permute-start.26 = (s32[8,4]{0,1:T(4,128)S(1)}, s32[8,4]{0,1:T(4,128)S(1)}, u32[]{:S(2)}, u32[]{:S(2)}) collective-permute-start(s32[8,4]{0,1:T(4,128)S(1)} %bitcast.263), channel_id=1, source_target_pairs={{0,128},{32,160},{64,192},{96,224},{128,0},{160,32},{192,64},{224,... | collective-permute-start | bytes 392 | tf_op jit(solution)/shard_map/ppermute | solution.py:28
  33.5 13.9 %copy-start.16 = (f32[1,2,128,512]{3,2,1,0:T(8,128)S(1)}, f32[1,2,128,512]{3,2,1,0:T(8,128)}, u32[]{:S(2)}) copy-start(f32[1,2,128,512]{3,2,1,0:T(8,128)} %param.23) | copy-start | bytes 1572868
  33.5 276.5 %all-reduce.5.cloned.1.call-start = ((), (), s32[]{:S(2)}) async-start(), calls=%async_computation.1 | async-start | bytes 4194304 | tf_op jit(solution)/shard_map/psum | solution.py:60
  37.5 14.5 %collective-permute-start.19 = (f32[512,128]{1,0:T(8,128)S(1)}, f32[512,128]{1,0:T(8,128)S(1)}, u32[]{:S(2)}, u32[]{:S(2)}) collective-permute-start(f32[512,128]{1,0:T(8,128)S(1)} %get-tuple-element.797), channel_id=1, source_target_pairs={{0,24},{8,16},{16,8},{24,0},{1,25},{9,17},{17,9},{25,1},{2,26},{10... | collective-permute-start | bytes 786440 | tf_op jit(solution)/shard_map/ppermute | solution.py:28
  42.2 12.6 %collective-permute-start.20 = (f32[512,128]{1,0:T(8,128)S(1)}, f32[512,128]{1,0:T(8,128)S(1)}, u32[]{:S(2)}, u32[]{:S(2)}) collective-permute-start(f32[512,128]{1,0:T(8,128)S(1)} %get-tuple-element.796), channel_id=1, source_target_pairs={{0,16},{8,24},{16,0},{24,8},{1,17},{9,25},{17,1},{25,9},{2,18},{10... | collective-permute-start | bytes 786440 | tf_op jit(solution)/shard_map/ppermute | solution.py:28
  44.9 10.5 %collective-permute-start.21 = (f32[512,128]{1,0:T(8,128)S(1)}, f32[512,128]{1,0:T(8,128)S(1)}, u32[]{:S(2)}, u32[]{:S(2)}) collective-permute-start(f32[512,128]{1,0:T(8,128)S(1)} %get-tuple-element.795), channel_id=1, source_target_pairs={{0,8},{8,0},{16,24},{24,16},{1,9},{9,1},{17,25},{25,17},{2,10},{10... | collective-permute-start | bytes 786440 | tf_op jit(solution)/shard_map/ppermute | solution.py:28
  56.2 12.9 %collective-permute-start.22 = (f32[512,128]{0,1:T(8,128)S(1)}, f32[512,128]{0,1:T(8,128)S(1)}, u32[]{:S(2)}, u32[]{:S(2)}) collective-permute-start(f32[512,128]{0,1:T(8,128)S(1)} %fusion.4), channel_id=1, source_target_pairs={{0,24},{8,16},{16,8},{24,0},{1,25},{9,17},{17,9},{25,1},{2,26},{10... | collective-permute-start | bytes 786440 | tf_op jit(solution)/shard_map/ppermute | solution.py:28
  60.9 13.0 %collective-permute-start.23 = (f32[512,128]{0,1:T(8,128)S(1)}, f32[512,128]{0,1:T(8,128)S(1)}, u32[]{:S(2)}, u32[]{:S(2)}) collective-permute-start(f32[512,128]{0,1:T(8,128)S(1)} %fusion.4), channel_id=1, source_target_pairs={{0,16},{8,24},{16,0},{24,8},{1,17},{9,25},{17,1},{25,9},{2,18},{10... | collective-permute-start | bytes 786440 | tf_op jit(solution)/shard_map/ppermute | solution.py:28
  63.6 12.9 %collective-permute-start.24 = (f32[512,128]{0,1:T(8,128)S(1)}, f32[512,128]{0,1:T(8,128)S(1)}, u32[]{:S(2)}, u32[]{:S(2)}) collective-permute-start(f32[512,128]{0,1:T(8,128)S(1)} %fusion.4), channel_id=1, source_target_pairs={{0,8},{8,0},{16,24},{24,16},{1,9},{9,1},{17,25},{25,17},{2,10},{10... | collective-permute-start | bytes 786440 | tf_op jit(solution)/shard_map/ppermute | solution.py:28
  69.1 7.7 %collective-permute-start.27 = (s32[8,4]{0,1:T(4,128)S(1)}, s32[8,4]{0,1:T(4,128)S(1)}, u32[]{:S(2)}, u32[]{:S(2)}) collective-permute-start(s32[8,4]{0,1:T(4,128)S(1)} %bitcast.264), channel_id=1, source_target_pairs={{0,256},{32,288},{64,320},{96,352},{128,384},{160,416},{192,448},{... | collective-permute-start | bytes 392 | tf_op jit(solution)/shard_map/ppermute | solution.py:28
  73.9 6.7 %collective-permute-start.28 = (s32[8,4]{0,1:T(4,128)S(1)}, s32[8,4]{0,1:T(4,128)S(1)}, u32[]{:S(2)}, u32[]{:S(2)}) collective-permute-start(s32[8,4]{0,1:T(4,128)S(1)} %bitcast.265), channel_id=1, source_target_pairs={{0,384},{32,416},{64,448},{96,480},{128,256},{160,288},{192,320},{... | collective-permute-start | bytes 392 | tf_op jit(solution)/shard_map/ppermute | solution.py:28
  176.8 12.7 %collective-permute-start.29 = (f32[512,128]{1,0:T(8,128)}, f32[512,128]{1,0:T(8,128)S(1)}, u32[]{:S(2)}, u32[]{:S(2)}) collective-permute-start(f32[512,128]{1,0:T(8,128)} %get-tuple-element.794), channel_id=1, source_target_pairs={{0,24},{8,16},{16,8},{24,0},{1,25},{9,17},{17,9},{25,1},{2,26},{10... | collective-permute-start | bytes 786440 | tf_op jit(solution)/shard_map/ppermute | solution.py:28
  181.3 10.5 %collective-permute-start.30 = (f32[512,128]{1,0:T(8,128)S(1)}, f32[512,128]{1,0:T(8,128)S(1)}, u32[]{:S(2)}, u32[]{:S(2)}) collective-permute-start(f32[512,128]{1,0:T(8,128)S(1)} %get-tuple-element.793), channel_id=1, source_target_pairs={{0,16},{8,24},{16,0},{24,8},{1,17},{9,25},{17,1},{25,9},{2,18},{10... | collective-permute-start | bytes 786440 | tf_op jit(solution)/shard_map/ppermute | solution.py:28
  184.1 8.7 %collective-permute-start.31 = (f32[512,128]{1,0:T(8,128)S(1)}, f32[512,128]{1,0:T(8,128)S(1)}, u32[]{:S(2)}, u32[]{:S(2)}) collective-permute-start(f32[512,128]{1,0:T(8,128)S(1)} %get-tuple-element.792), channel_id=1, source_target_pairs={{0,8},{8,0},{16,24},{24,16},{1,9},{9,1},{17,25},{25,17},{2,10},{10... | collective-permute-start | bytes 786440 | tf_op jit(solution)/shard_map/ppermute | solution.py:28
  194.8 10.6 %collective-permute-start.32 = (f32[512,128]{0,1:T(8,128)S(1)}, f32[512,128]{0,1:T(8,128)S(1)}, u32[]{:S(2)}, u32[]{:S(2)}) collective-permute-start(f32[512,128]{0,1:T(8,128)S(1)} %fusion.3), channel_id=1, source_target_pairs={{0,24},{8,16},{16,8},{24,0},{1,25},{9,17},{17,9},{25,1},{2,26},{10... | collective-permute-start | bytes 786440 | tf_op jit(solution)/shard_map/ppermute | solution.py:28
  199.0 9.8 %collective-permute-start.33 = (f32[512,128]{0,1:T(8,128)S(1)}, f32[512,128]{0,1:T(8,128)S(1)}, u32[]{:S(2)}, u32[]{:S(2)}) collective-permute-start(f32[512,128]{0,1:T(8,128)S(1)} %fusion.3), channel_id=1, source_target_pairs={{0,16},{8,24},{16,0},{24,8},{1,17},{9,25},{17,1},{25,9},{2,18},{10... | collective-permute-start | bytes 786440 | tf_op jit(solution)/shard_map/ppermute | solution.py:28
  201.9 8.4 %collective-permute-start.34 = (f32[512,128]{0,1:T(8,128)S(1)}, f32[512,128]{0,1:T(8,128)}, u32[]{:S(2)}, u32[]{:S(2)}) collective-permute-start(f32[512,128]{0,1:T(8,128)S(1)} %fusion.3), channel_id=1, source_target_pairs={{0,8},{8,0},{16,24},{24,16},{1,9},{9,1},{17,25},{25,17},{2,10},{10... | collective-permute-start | bytes 786440 | tf_op jit(solution)/shard_map/ppermute | solution.py:28
  314.8 6.3 %collective-permute-start.35 = (f32[1024,512]{1,0:T(8,128)}, f32[1024,512]{1,0:T(8,128)S(1)}, u32[]{:S(2)}, u32[]{:S(2)}) collective-permute-start(f32[1024,512]{1,0:T(8,128)} %bitcast_multiply_fusion.1), channel_id=1, source_target_pairs={{0,32},{32,0},{64,96},{96,64},{128,160},{160,128},{192,224},{224,1... | collective-permute-start | bytes 6291464 | tf_op jit(solution)/shard_map/ppermute | solution.py:28
  328.3 115.5 %collective-permute-start.9 = (f32[20,128,128]{2,1,0:T(8,128)S(1)}, f32[20,128,128]{2,1,0:T(8,128)S(1)}, u32[]{:S(2)}, u32[]{:S(2)}) collective-permute-start(f32[20,128,128]{2,1,0:T(8,128)S(1)} %branch_10_fun.2), channel_id=1, source_target_pairs={{0,64},{32,96},{64,0},{96,32},{128,192},{160,224},{192,128},{224,1... | collective-permute-start | bytes 3932168 | tf_op jit(solution)/shard_map/cond/branch_10_fun/ppermute | solution.py:28
  448.8 17.6 %collective-permute-start.36 = (f32[256,512]{1,0:T(8,128)S(1)}, f32[256,512]{1,0:T(8,128)S(1)}, u32[]{:S(2)}, u32[]{:S(2)}) collective-permute-start(f32[256,512]{1,0:T(8,128)S(1)} %get-tuple-element.789), channel_id=1, source_target_pairs={{0,128},{32,160},{64,192},{96,224},{128,0},{160,32},{192,64},{224,... | collective-permute-start | bytes 1572872 | tf_op jit(solution)/shard_map/ppermute | solution.py:28
  450.7 34.5 %collective-permute-start.37 = (f32[256,512]{1,0:T(8,128)S(1)}, f32[256,512]{1,0:T(8,128)S(1)}, u32[]{:S(2)}, u32[]{:S(2)}) collective-permute-start(f32[256,512]{1,0:T(8,128)S(1)} %get-tuple-element.791), channel_id=1, source_target_pairs={{0,256},{32,288},{64,320},{96,352},{128,384},{160,416},{192,448},{... | collective-permute-start | bytes 1572872 | tf_op jit(solution)/shard_map/ppermute | solution.py:28
  464.0 27.6 %collective-permute-start.38 = (f32[256,512]{1,0:T(8,128)S(1)}, f32[256,512]{1,0:T(8,128)S(1)}, u32[]{:S(2)}, u32[]{:S(2)}) collective-permute-start(f32[256,512]{1,0:T(8,128)S(1)} %get-tuple-element.790), channel_id=1, source_target_pairs={{0,384},{32,416},{64,448},{96,480},{128,256},{160,288},{192,320},{... | collective-permute-start | bytes 1572872 | tf_op jit(solution)/shard_map/ppermute | solution.py:28
  493.0 16.8 %collective-permute-start.39 = (f32[256,512]{1,0:T(8,128)S(1)}, f32[256,512]{1,0:T(8,128)S(1)}, u32[]{:S(2)}, u32[]{:S(2)}) collective-permute-start(f32[256,512]{1,0:T(8,128)S(1)} %get-tuple-element.784), channel_id=1, source_target_pairs={{0,128},{32,160},{64,192},{96,224},{128,0},{160,32},{192,64},{224,... | collective-permute-start | bytes 1572872 | tf_op jit(solution)/shard_map/ppermute | solution.py:28
  494.9 22.6 %collective-permute-start.40 = (f32[256,512]{1,0:T(8,128)S(1)}, f32[256,512]{1,0:T(8,128)S(1)}, u32[]{:S(2)}, u32[]{:S(2)}) collective-permute-start(f32[256,512]{1,0:T(8,128)S(1)} %get-tuple-element.788), channel_id=1, source_target_pairs={{0,256},{32,288},{64,320},{96,352},{128,384},{160,416},{192,448},{... | collective-permute-start | bytes 1572872 | tf_op jit(solution)/shard_map/ppermute | solution.py:28
  497.8 26.8 %collective-permute-start.41 = (f32[256,512]{1,0:T(8,128)S(1)}, f32[256,512]{1,0:T(8,128)S(1)}, u32[]{:S(2)}, u32[]{:S(2)}) collective-permute-start(f32[256,512]{1,0:T(8,128)S(1)} %get-tuple-element.783), channel_id=1, source_target_pairs={{0,384},{32,416},{64,448},{96,480},{128,256},{160,288},{192,320},{... | collective-permute-start | bytes 1572872 | tf_op jit(solution)/shard_map/ppermute | solution.py:28
  503.4 22.6 %copy-start.1 = (s32[1,32,32]{2,1,0:T(8,128)S(1)}, s32[1,32,32]{2,1,0:T(8,128)}, u32[]{:S(2)}) copy-start(s32[1,32,32]{2,1,0:T(8,128)} %param.26) | copy-start | bytes 12292
  (7 other events, 21.5 us)
Sparse Core Ops, SparseCore 0:
  33.6 134.9 all-reduce.2
  174.2 135.7 all-reduce.4

commit v4 on v3

--- a/solution.py
+++ b/solution.py
@@ -12,6 +12,7 @@
 BLK = 128
 PB = P_SIZE // BLK
 STEP = 2
+Y_GROUPS = [[first + 4 * k for k in range(4)] for first in range(4)]
 
 
 def matmul(left_side, right_side):
@@ -56,8 +57,8 @@
     return pick(got, row ^ source)
 
 
-def spread(panel, source):
-    return lax.psum(jnp.where(lax.axis_index("col") == source, panel, 0.0), "col")
+def own_panel(panel, source):
+    return jnp.where(lax.axis_index("col") == source, panel, 0.0)
 
 
 def blocks_of(rows, cols):
@@ -153,21 +154,27 @@
     mask1 = lax.dynamic_slice(pattern[1].astype(jnp.float32) * a1[:, None] * a1[None, :], *here)
     kept = lax.dynamic_slice(a1[:, None] * a1[None, :], *here)
 
-    left = spread(matrix, q0)
-    mine = lax.dynamic_slice(lists[0], *here)
+    panel, matrix = lax.optimization_barrier((own_panel(matrix, q0), matrix))
+    left = lax.psum(panel, "col")
+    candidate = lax.dynamic_slice_in_dim(matrix, (q0 % 2) * half, half, 0)
+    pivot, inverse_part = lax.optimization_barrier(
+        (exchange_row(candidate, row, q0 // 2), inverses[0])
+    )
+    inv = jnp.concatenate(gather_row(inverse_part, row), axis=1)
+    scaled = matmul(inv[0], pivot)
+    right = jnp.concatenate(gather_row(scaled, row), axis=1)
+    matrix = matrix - by_blocks(matmul(left, right), mask0)
+
+    panel, matrix = lax.optimization_barrier((own_panel(matrix, q1), matrix))
+    left = lax.psum(panel, "col")
+    candidate = lax.dynamic_slice_in_dim(matrix, (q1 % 2) * half, half, 0)
+    pivot, listed = lax.optimization_barrier((exchange_row(candidate, row, q1 // 2), lists[0]))
+    scaled = matmul(inv[1], pivot)
+    right = jnp.concatenate(gather_row(scaled, row), axis=1)
+    mine = lax.dynamic_slice(listed, *here)
     theirs = xor_send(mine, "layer", 2)
-    listed = [mine] + [xor_send(mine, "layer", 4 * k) for k in (1, 2, 3)]
-    inv = jnp.concatenate(gather_row(inverses[0], row), axis=1)
-    candidate = lax.dynamic_slice_in_dim(matrix, (q0 % 2) * half, half, 0)
-    scaled = matmul(inv[0], exchange_row(candidate, row, q0 // 2))
-    right = jnp.concatenate(gather_row(scaled, row), axis=1)
-    right, theirs, listed = lax.optimization_barrier((right, theirs, listed))
-    matrix = matrix - by_blocks(matmul(left, right), mask0)
-
-    left = spread(matrix, q1)
-    candidate = lax.dynamic_slice_in_dim(matrix, (q1 % 2) * half, half, 0)
-    scaled = matmul(inv[1], exchange_row(candidate, row, q1 // 2))
-    right = jnp.concatenate(gather_row(scaled, row), axis=1)
+    listed = lax.all_gather(mine, "layer", axis_index_groups=Y_GROUPS)
+    left, right, theirs, listed = lax.optimization_barrier((left, right, theirs, listed))
     acc = by_blocks(matrix - by_blocks(matmul(left, right), mask1), kept)
 
     def bit(values, b):
@@ -178,23 +185,20 @@
     acc = listed_exchange(acc, bit(mine, 1) * kept > 0, bit(theirs, 1) * kept > 0, 2)
 
     yy = layer // 4
-    qrows = rows // 4
     qb = rb // 4
-    quarters = acc.reshape(4, qrows, cols)
-
-    def own(q):
-        return lax.dynamic_index_in_dim(quarters, q, 0, keepdims=False)
-
-    held = [own(yy)] + [xor_send(own(yy ^ k), "layer", 4 * k) for k in (1, 2, 3)]
-    w = [lax.dynamic_slice_in_dim(values, yy * qb, qb, 0) for values in listed]
+
+    def turn(value):
+        return lax.all_to_all(
+            value.reshape(4, -1, cols), "layer", 0, 0, axis_index_groups=Y_GROUPS, tiled=True
+        )
+
+    held = turn(acc)
+    held = [held[k] for k in range(4)]
+    w = lax.dynamic_slice_in_dim(listed, yy * qb, qb, 1)
     for b in (2, 3):
         d = b - 1
         held = [held[k] + by_blocks(held[k ^ d], bit(w[k], b)) for k in range(4)]
-    back = [held[0]] + [xor_send(held[k], "layer", 4 * k) for k in (1, 2, 3)]
-    out = jnp.zeros((4, qrows, cols), jnp.float32)
-    for k in range(4):
-        out = lax.dynamic_update_index_in_dim(out, back[k], yy ^ k, 0)
-    return out.reshape(1, rows, cols)
+    return turn(jnp.stack(held)).reshape(1, rows, cols)
 
 
 def solution(mesh):

time: 534 us -> 494 us (0.925)
  the two profiles are of different devices: /device:TPU:224 before, /device:TPU:24 now
where the time goes in v4:
time: 494 us; the launch traced here: 489 us
  waiting for transfers between devices  314 us (64%)
  starting transfers between devices  71.5 us (14%)
  blocking collectives  38.1 us (8%)
  between operations  21.7 us (4%)
  other arithmetic  15.1 us (3%)
  matrix products  12.8 us (3%)
  local copies, waits for them, and re-layouts  12 us (2%)
    psum x2, waiting for transfers between devices, body(): left = lax.psum(panel, 'col')  172 us
    ppermute x18, waiting for transfers between devices, xor_send(): return lax.ppermute(value, axis, pairs)  118 us
    ppermute x18, starting transfers between devices, xor_send(): return lax.ppermute(value, axis, pairs)  65.6 us
    all_to_all x1, blocking collectives, turn(): lax.all_to_all(value.reshape(4, -1, cols), 'layer', 0, 0, axis_index_grou...  28 us
    all_to_all x1, waiting for transfers between devices, turn(): lax.all_to_all(value.reshape(4, -1, cols), 'layer', 0, 0, axis_index_grou...  23.6 us
    dot_general x4, matrix products, matmul(): jnp.dot(left_side, right_side, precision=lax.Precision.HIGH, preferred_el...  12.8 us
    all_gather x1, blocking collectives, body(): listed = lax.all_gather(mine, 'layer', axis_index_groups=Y_GROUPS)  10.1 us
  transfers between devices with their start and end apart: 21, of which 14 were waited for; matrix products, arithmetic and copies ran while one was open for 3% of the time, Pallas kernels for 0%

profile of v4, /device:TPU:24, one launch (start us, length us, event | category | flops | bytes accessed | tf_op | source)
XLA Modules:
  0.0 489.5 jit_solution(18401905498707780399)
XLA Ops:
  10.7 3.3 broadcast_select_fusion.1
  15.0 4.8 collective-permute-start.16
  19.8 2.7 collective-permute-start.17
  25.8 5.8 %collective-permute-done.16 = f32[512,128]{1,0:T(8,128)S(1)} collective-permute-done((f32[512,128]{1,0:T(8,128)}, f32[512,128]{1,0:T(8,128)S(1)}, u32[]{:S(2)}, u32[]{:S(2)}) %collective-permute-start.16) | collective-permute-done | bytes 262176 | tf_op jit(solution)/shard_map/ppermute | solution.py:29
  35.9 3.7 collective-permute-start.19
  39.6 2.7 collective-permute-start.20
  42.3 3.4 collective-permute-start.21
  46.8 16.0 %collective-permute-done.19 = f32[2,128,512]{2,1,0:T(8,128)S(1)} collective-permute-done((f32[2,128,512]{2,1,0:T(8,128)S(1)}, f32[2,128,512]{2,1,0:T(8,128)S(1)}, u32[]{:S(2)}, u32[]{:S(2)}) %collective-permute-start.19) | collective-permute-done | bytes 524320 | tf_op jit(solution)/shard_map/ppermute | solution.py:29
  62.7 2.5 collective-permute-done.21
  67.8 3.7 collective-permute-start.22
  71.5 2.7 collective-permute-start.23
  74.2 3.4 collective-permute-start.24
  78.5 3.1 collective-permute-done.22
  85.1 85.6 %all-reduce.3.cloned.1.call-done = f32[1024,512]{1,0:T(8,128)} async-done(((f32[1024,512]{1,0:T(8,128)}), f32[1024,512]{1,0:T(8,128)}) %all-reduce.3.cloned.1.call-update) | async-done | bytes 2097168 | tf_op jit(solution)/shard_map/psum | solution.py:158
  170.7 5.4 %broadcast_select_fusion = (f32[1024,512]{1,0:T(8,128)}, f32[1024,512]{1,0:T(8,128)S(1)}) fusion(pred[]{:T(512)S(6)} %eq.100, f32[1024,512]{1,0:T(8,128)} %bitcast.278, f32[8,512]{1,0:T(8,128)S(1)} %broadcast_bitcast_fusion.3, f32[1024,512]{1,0:T(8,128)} %all-reduce.3.cloned.1.call-done, f32[512,128]{0,1:T(8,128)S(1)} %get-tuple-element.888, ...), kind=kOutput, calls=%fused_computation.117 | convolution fusion | flops 1612972032 | bytes 9453569 | tf_op jit(solution)/shard_map/dot_general | solution.py:19
  178.8 4.6 collective-permute-start.25
  183.4 2.8 collective-permute-start.26
  196.5 4.0 collective-permute-start.28
  200.5 2.8 collective-permute-start.29
  203.3 3.0 collective-permute-start.30
  207.2 7.6 %collective-permute-start.31 = (s32[8,4]{1,0:T(8,128)S(1)}, s32[8,4]{1,0:T(8,128)S(1)}, u32[]{:S(2)}, u32[]{:S(2)}) collective-permute-start(s32[8,4]{1,0:T(8,128)S(1)} %get-tuple-element.868), channel_id=1, source_target_pairs={{0,64},{32,96},{64,0},{96,32},{128,192},{160,224},{192,128},{224,1... | collective-permute-start | bytes 392 | tf_op jit(solution)/shard_map/ppermute | solution.py:29
  214.9 10.1 %all-gather.1 = s32[4,8,4]{1,2,0:T(4,128)S(1)} all-gather(s32[1,8,4]{1,2,0:T(4,128)S(1)} %bitcast.302), channel_id=2, replica_groups={{0,128,256,384},{32,160,288,416},{64,192,320,448},{96,224,352,480},{1,1..., dimensions={0}, use_global_device_ids=true | all-gather | bytes 640 | tf_op jit(solution)/shard_map/all_gather | solution.py:176
  225.3 86.9 %all-reduce.5.cloned.1.call-done = f32[1024,512]{1,0:T(8,128)} async-done(((f32[1024,512]{1,0:T(8,128)}), f32[1024,512]{1,0:T(8,128)}) %all-reduce.5.cloned.1.call-update) | async-done | bytes 2097168 | tf_op jit(solution)/shard_map/psum | solution.py:169
  312.1 4.8 bitcast_multiply_fusion.1
  324.1 3.4 fusion
  327.6 93.9 %conditional.1 = (f32[1024,512]{1,0:T(8,128)}) conditional(s32[]{:T(128)} %clamp.35, f32[1024,512]{1,0:T(8,128)} %fusion, (pred[8,4]{1,0:T(8,128)(4,1)S(1)}, s32[32,1]{1,0:T(8,128)S(1)}, pred[8,4]{1,0:T(8,128)(4,1)S(1)}, s32[32,1]{1,0:T(8,128)S(1)}, f32[1024,512]{1,0:T(8,128)}) %tuple.69, ...), branch_computations={%region_6.7_spmd, %region_7.8_spmd, %region_8.9_spmd, %region_9.10... | conditional | flops 256 | bytes 12584816 | solution.py:132
  330.2 6.9 %collective-permute-start.7 = (f32[16,128,128]{2,1,0:T(8,128)S(1)}, f32[16,128,128]{2,1,0:T(8,128)}, u32[]{:S(2)}, u32[]{:S(2)}) collective-permute-start(f32[16,128,128]{2,1,0:T(8,128)S(1)} %branch_8_fun.2), channel_id=1, source_target_pairs={{0,64},{32,96},{64,0},{96,32},{128,192},{160,224},{192,128},{224,1... | collective-permute-start | bytes 3145736 | tf_op jit(solution)/shard_map/cond/branch_8_fun/ppermute | solution.py:29
  337.3 81.0 %collective-permute-done.7.packed = f32[16,128,128]{2,1,0:T(8,128)} collective-permute-done((f32[16,128,128]{2,1,0:T(8,128)S(1)}, f32[16,128,128]{2,1,0:T(8,128)}, u32[]{:S(2)}, u32[]{:S(2)}) %collective-permute-start.7) | collective-permute-done | bytes 1048608 | tf_op jit(solution)/shard_map/cond/branch_8_fun/ppermute | solution.py:29
  418.3 3.2 branch_8_fun.3
  421.5 5.8 %all-to-all-start = ((f32[4,256,512]{2,1,0:T(8,128)}), f32[4,256,512]{2,1,0:T(8,128)S(1)}, u32[]{:S(2)}, u32[]{:S(2)}) async-start(f32[4,256,512]{2,1,0:T(8,128)} %bitcast.50), calls=%async_computation | async-start | bytes 4194304 | tf_op jit(solution)/shard_map/all_to_all | solution.py:191
  428.1 23.6 %all-to-all-done = f32[4,256,512]{2,1,0:T(8,128)S(1)} async-done(((f32[4,256,512]{2,1,0:T(8,128)}), f32[4,256,512]{2,1,0:T(8,128)S(1)}, u32[]{:S(2)}, u32[]{:S(2)}) %all-to-all-start) | async-done | bytes 2097184 | tf_op jit(solution)/shard_map/all_to_all | solution.py:191
  453.3 28.0 %all_to_all.10 = f32[4,256,512]{2,1,0:T(8,128)S(1)} all-to-all(f32[4,256,512]{2,1,0:T(8,128)S(1)} %pad_maximum_fusion.1), channel_id=1, replica_groups={{0,128,256,384},{32,160,288,416},{64,192,320,448},{96,224,352,480},{1,1..., dimensions={0} | all-to-all | bytes 4194304 | tf_op jit(solution)/shard_map/all_to_all | solution.py:191
  (128 shorter events, 40.6 us)
Async XLA Ops:
  6.5 164.1 %all-reduce.3.cloned.1.call-start = ((), (), s32[]{:S(2)}) async-start(), calls=%async_computation.2 | async-start | bytes 4194304 | tf_op jit(solution)/shard_map/psum | solution.py:158
  10.7 3.3 copy-start
  15.0 20.8 %copy-start.2 = (f32[1,2,128,512]{3,2,1,0:T(8,128)S(1)}, f32[1,2,128,512]{3,2,1,0:T(8,128)}, u32[]{:S(2)}) copy-start(f32[1,2,128,512]{3,2,1,0:T(8,128)} %param.23) | copy-start | bytes 1572868
  15.0 31.7 %copy-start.5 = (s32[2,32,32]{2,1,0:T(8,128)S(1)}, s32[2,32,32]{2,1,0:T(8,128)}, u32[]{:S(2)}) copy-start(s32[2,32,32]{2,1,0:T(8,128)} %param.24) | copy-start | bytes 24580
  15.0 16.5 %collective-permute-start.16 = (f32[512,128]{1,0:T(8,128)}, f32[512,128]{1,0:T(8,128)S(1)}, u32[]{:S(2)}, u32[]{:S(2)}) collective-permute-start(f32[512,128]{1,0:T(8,128)} %get-tuple-element.882), channel_id=1, source_target_pairs={{0,24},{8,16},{16,8},{24,0},{1,25},{9,17},{17,9},{25,1},{2,26},{10... | collective-permute-start | bytes 786440 | tf_op jit(solution)/shard_map/ppermute | solution.py:29
  19.8 12.8 %collective-permute-start.17 = (f32[512,128]{1,0:T(8,128)}, f32[512,128]{1,0:T(8,128)S(1)}, u32[]{:S(2)}, u32[]{:S(2)}) collective-permute-start(f32[512,128]{1,0:T(8,128)} %get-tuple-element.881), channel_id=1, source_target_pairs={{0,16},{8,24},{16,0},{24,8},{1,17},{9,25},{17,1},{25,9},{2,18},{10... | collective-permute-start | bytes 786440 | tf_op jit(solution)/shard_map/ppermute | solution.py:29
  22.6 12.2 %collective-permute-start.18 = (f32[512,128]{1,0:T(8,128)S(1)}, f32[512,128]{1,0:T(8,128)}, u32[]{:S(2)}, u32[]{:S(2)}) collective-permute-start(f32[512,128]{1,0:T(8,128)S(1)} %get-tuple-element.880), channel_id=1, source_target_pairs={{0,8},{8,0},{16,24},{24,16},{1,9},{9,1},{17,25},{25,17},{2,10},{10... | collective-permute-start | bytes 786440 | tf_op jit(solution)/shard_map/ppermute | solution.py:29
  25.0 287.1 %all-reduce.5.cloned.1.call-start = ((), (), s32[]{:S(2)}) async-start(), calls=%async_computation.3 | async-start | bytes 4194304 | tf_op jit(solution)/shard_map/psum | solution.py:169
  35.9 26.9 %collective-permute-start.19 = (f32[2,128,512]{2,1,0:T(8,128)S(1)}, f32[2,128,512]{2,1,0:T(8,128)S(1)}, u32[]{:S(2)}, u32[]{:S(2)}) collective-permute-start(f32[2,128,512]{2,1,0:T(8,128)S(1)} %bitcast.290), channel_id=1, source_target_pairs={{0,24},{8,16},{16,8},{24,0},{1,25},{9,17},{17,9},{25,1},{2,26},{10... | collective-permute-start | bytes 1572872 | tf_op jit(solution)/shard_map/ppermute | solution.py:29
  39.6 23.1 %collective-permute-start.20 = (f32[2,128,512]{2,1,0:T(8,128)S(1)}, f32[2,128,512]{2,1,0:T(8,128)S(1)}, u32[]{:S(2)}, u32[]{:S(2)}) collective-permute-start(f32[2,128,512]{2,1,0:T(8,128)S(1)} %bitcast.291), channel_id=1, source_target_pairs={{0,16},{8,24},{16,0},{24,8},{1,17},{9,25},{17,1},{25,9},{2,18},{10... | collective-permute-start | bytes 1572872 | tf_op jit(solution)/shard_map/ppermute | solution.py:29
  42.3 22.9 %collective-permute-start.21 = (f32[2,128,512]{2,1,0:T(8,128)S(1)}, f32[2,128,512]{2,1,0:T(8,128)S(1)}, u32[]{:S(2)}, u32[]{:S(2)}) collective-permute-start(f32[2,128,512]{2,1,0:T(8,128)S(1)} %bitcast.292), channel_id=1, source_target_pairs={{0,8},{8,0},{16,24},{24,16},{1,9},{9,1},{17,25},{25,17},{2,10},{10... | collective-permute-start | bytes 1572872 | tf_op jit(solution)/shard_map/ppermute | solution.py:29
  65.8 1.3 copy-start.1
  67.8 13.8 %collective-permute-start.22 = (f32[512,128]{0,1:T(8,128)S(1)}, f32[512,128]{0,1:T(8,128)S(1)}, u32[]{:S(2)}, u32[]{:S(2)}) collective-permute-start(f32[512,128]{0,1:T(8,128)S(1)} %fusion.4), channel_id=1, source_target_pairs={{0,24},{8,16},{16,8},{24,0},{1,25},{9,17},{17,9},{25,1},{2,26},{10... | collective-permute-start | bytes 786440 | tf_op jit(solution)/shard_map/ppermute | solution.py:29
  71.5 11.8 %collective-permute-start.23 = (f32[512,128]{0,1:T(8,128)S(1)}, f32[512,128]{0,1:T(8,128)S(1)}, u32[]{:S(2)}, u32[]{:S(2)}) collective-permute-start(f32[512,128]{0,1:T(8,128)S(1)} %fusion.4), channel_id=1, source_target_pairs={{0,16},{8,24},{16,0},{24,8},{1,17},{9,25},{17,1},{25,9},{2,18},{10... | collective-permute-start | bytes 786440 | tf_op jit(solution)/shard_map/ppermute | solution.py:29
  74.2 10.7 %collective-permute-start.24 = (f32[512,128]{0,1:T(8,128)S(1)}, f32[512,128]{0,1:T(8,128)S(1)}, u32[]{:S(2)}, u32[]{:S(2)}) collective-permute-start(f32[512,128]{0,1:T(8,128)S(1)} %fusion.4), channel_id=1, source_target_pairs={{0,8},{8,0},{16,24},{24,16},{1,9},{9,1},{17,25},{25,17},{2,10},{10... | collective-permute-start | bytes 786440 | tf_op jit(solution)/shard_map/ppermute | solution.py:29
  178.8 12.3 %collective-permute-start.25 = (f32[512,128]{1,0:T(8,128)}, f32[512,128]{1,0:T(8,128)S(1)}, u32[]{:S(2)}, u32[]{:S(2)}) collective-permute-start(f32[512,128]{1,0:T(8,128)} %get-tuple-element.875), channel_id=1, source_target_pairs={{0,24},{8,16},{16,8},{24,0},{1,25},{9,17},{17,9},{25,1},{2,26},{10... | collective-permute-start | bytes 786440 | tf_op jit(solution)/shard_map/ppermute | solution.py:29
  183.4 9.8 %collective-permute-start.26 = (f32[512,128]{1,0:T(8,128)S(1)}, f32[512,128]{1,0:T(8,128)S(1)}, u32[]{:S(2)}, u32[]{:S(2)}) collective-permute-start(f32[512,128]{1,0:T(8,128)S(1)} %get-tuple-element.874), channel_id=1, source_target_pairs={{0,16},{8,24},{16,0},{24,8},{1,17},{9,25},{17,1},{25,9},{2,18},{10... | collective-permute-start | bytes 786440 | tf_op jit(solution)/shard_map/ppermute | solution.py:29
  186.2 8.3 %collective-permute-start.27 = (f32[512,128]{1,0:T(8,128)S(1)}, f32[512,128]{1,0:T(8,128)S(1)}, u32[]{:S(2)}, u32[]{:S(2)}) collective-permute-start(f32[512,128]{1,0:T(8,128)S(1)} %get-tuple-element.873), channel_id=1, source_target_pairs={{0,8},{8,0},{16,24},{24,16},{1,9},{9,1},{17,25},{25,17},{2,10},{10... | collective-permute-start | bytes 786440 | tf_op jit(solution)/shard_map/ppermute | solution.py:29
  196.5 28.5 %collective-permute-start.28 = (f32[512,128]{0,1:T(8,128)S(1)}, f32[512,128]{0,1:T(8,128)S(1)}, u32[]{:S(2)}, u32[]{:S(2)}) collective-permute-start(f32[512,128]{0,1:T(8,128)S(1)} %fusion.3), channel_id=1, source_target_pairs={{0,24},{8,16},{16,8},{24,0},{1,25},{9,17},{17,9},{25,1},{2,26},{10... | collective-permute-start | bytes 786440 | tf_op jit(solution)/shard_map/ppermute | solution.py:29
  200.5 24.5 %collective-permute-start.29 = (f32[512,128]{0,1:T(8,128)S(1)}, f32[512,128]{0,1:T(8,128)S(1)}, u32[]{:S(2)}, u32[]{:S(2)}) collective-permute-start(f32[512,128]{0,1:T(8,128)S(1)} %fusion.3), channel_id=1, source_target_pairs={{0,16},{8,24},{16,0},{24,8},{1,17},{9,25},{17,1},{25,9},{2,18},{10... | collective-permute-start | bytes 786440 | tf_op jit(solution)/shard_map/ppermute | solution.py:29
  203.3 21.7 %collective-permute-start.30 = (f32[512,128]{0,1:T(8,128)S(1)}, f32[512,128]{0,1:T(8,128)S(1)}, u32[]{:S(2)}, u32[]{:S(2)}) collective-permute-start(f32[512,128]{0,1:T(8,128)S(1)} %fusion.3), channel_id=1, source_target_pairs={{0,8},{8,0},{16,24},{24,16},{1,9},{9,1},{17,25},{25,17},{2,10},{10... | collective-permute-start | bytes 786440 | tf_op jit(solution)/shard_map/ppermute | solution.py:29
  207.2 18.1 %collective-permute-start.31 = (s32[8,4]{1,0:T(8,128)S(1)}, s32[8,4]{1,0:T(8,128)S(1)}, u32[]{:S(2)}, u32[]{:S(2)}) collective-permute-start(s32[8,4]{1,0:T(8,128)S(1)} %get-tuple-element.868), channel_id=1, source_target_pairs={{0,64},{32,96},{64,0},{96,32},{128,192},{160,224},{192,128},{224,1... | collective-permute-start | bytes 392 | tf_op jit(solution)/shard_map/ppermute | solution.py:29
  316.9 7.2 %collective-permute-start.32 = (f32[1024,512]{1,0:T(8,128)}, f32[1024,512]{1,0:T(8,128)S(1)}, u32[]{:S(2)}, u32[]{:S(2)}) collective-permute-start(f32[1024,512]{1,0:T(8,128)} %bitcast_multiply_fusion.1), channel_id=1, source_target_pairs={{0,32},{32,0},{64,96},{96,64},{128,160},{160,128},{192,224},{224,1... | collective-permute-start | bytes 6291464 | tf_op jit(solution)/shard_map/ppermute | solution.py:29
  330.2 88.0 %collective-permute-start.7 = (f32[16,128,128]{2,1,0:T(8,128)S(1)}, f32[16,128,128]{2,1,0:T(8,128)}, u32[]{:S(2)}, u32[]{:S(2)}) collective-permute-start(f32[16,128,128]{2,1,0:T(8,128)S(1)} %branch_8_fun.2), channel_id=1, source_target_pairs={{0,64},{32,96},{64,0},{96,32},{128,192},{160,224},{192,128},{224,1... | collective-permute-start | bytes 3145736 | tf_op jit(solution)/shard_map/cond/branch_8_fun/ppermute | solution.py:29
  421.4 5.9 %copy-start.11 = (f32[2,4]{1,0:T(2,128)S(1)}, f32[2,4]{1,0:T(2,128)}, u32[]{:S(2)}) copy-start(f32[2,4]{1,0:T(2,128)} %get-tuple-element.913) | copy-start | bytes 100
  421.4 5.9 %copy-start.6 = (f32[1,2,4,128]{3,2,1,0:T(4,128)S(1)}, f32[1,2,4,128]{3,2,1,0:T(4,128)}, u32[]{:S(2)}) copy-start(f32[1,2,4,128]{3,2,1,0:T(4,128)} %broadcast_bitcast_fusion.6) | copy-start | bytes 12292
  421.5 6.0 %copy-start.10 = (f32[2,4]{1,0:T(2,128)S(1)}, f32[2,4]{1,0:T(2,128)}, u32[]{:S(2)}) copy-start(f32[2,4]{1,0:T(2,128)} %get-tuple-element.903) | copy-start | bytes 100
  421.5 6.0 %copy-start.9 = (f32[2,4]{1,0:T(2,128)S(1)}, f32[2,4]{1,0:T(2,128)}, u32[]{:S(2)}) copy-start(f32[2,4]{1,0:T(2,128)} %get-tuple-element.904) | copy-start | bytes 100
  421.5 6.1 %copy-start.8 = (s32[1,2,4]{1,2,0:T(4,128)S(1)}, s32[1,2,4]{1,2,0:T(4,128)}, u32[]{:S(2)}) copy-start(s32[1,2,4]{1,2,0:T(4,128)} %get-tuple-element.895) | copy-start | bytes 100
  421.5 6.2 %copy-start.7 = (s32[1,2,4]{1,2,0:T(4,128)S(1)}, s32[1,2,4]{1,2,0:T(4,128)}, u32[]{:S(2)}) copy-start(s32[1,2,4]{1,2,0:T(4,128)} %get-tuple-element.893) | copy-start | bytes 100
  421.5 30.2 %all-to-all-start = ((f32[4,256,512]{2,1,0:T(8,128)}), f32[4,256,512]{2,1,0:T(8,128)S(1)}, u32[]{:S(2)}, u32[]{:S(2)}) async-start(f32[4,256,512]{2,1,0:T(8,128)} %bitcast.50), calls=%async_computation | async-start | bytes 4194304 | tf_op jit(solution)/shard_map/all_to_all | solution.py:191
Sparse Core Ops, SparseCore 0:
  25.1 145.4 all-reduce.2
  176.2 135.8 all-reduce.4

commit v5 on v4

--- a/solution.py
+++ b/solution.py
@@ -47,18 +47,26 @@
     return [pick(got, row ^ q) for q in range(4)]
 
 
-def exchange_row(candidate, row, source):
-    quarter = candidate.shape[1] // 4
-
-    def part(q):
-        return lax.dynamic_slice_in_dim(candidate, q * quarter, quarter, 1)
+def exchange_row(candidates, row, sources):
+    part_rows = candidates.shape[1] // 4
+
+    def part(r):
+        return lax.dynamic_slice_in_dim(candidates, r * part_rows, part_rows, 1)
 
     got = [part(row)] + [xor_send(part(row ^ k), "row", k) for k in (1, 2, 3)]
-    return pick(got, row ^ source)
-
-
-def own_panel(panel, source):
-    return jnp.where(lax.axis_index("col") == source, panel, 0.0)
+    return [pick([g[i] for g in got], row ^ source) for i, source in enumerate(sources)]
+
+
+def spread_part(value, col, source):
+    for bit in (4, 2, 1):
+        got = lax.cond(
+            ((col ^ source) & (bit - 1)) == 0,
+            lambda held, bit=bit: xor_send(held, "col", bit),
+            lambda held: held,
+            value,
+        )
+        value = jnp.where(((col ^ source) & bit) != 0, got, value)
+    return value
 
 
 def blocks_of(rows, cols):
@@ -142,7 +150,6 @@
     rb, cb = rows // BLK, cols // BLK
     row_first, col_first = row * rb, col * cb
     half = rows // 2
-    quarter = cols // 4
 
     panels = jnp.arange(F // P_SIZE)
     alive0 = (panels != q0).astype(jnp.float32)
@@ -154,28 +161,50 @@
     mask1 = lax.dynamic_slice(pattern[1].astype(jnp.float32) * a1[:, None] * a1[None, :], *here)
     kept = lax.dynamic_slice(a1[:, None] * a1[None, :], *here)
 
-    panel, matrix = lax.optimization_barrier((own_panel(matrix, q0), matrix))
-    left = lax.psum(panel, "col")
-    candidate = lax.dynamic_slice_in_dim(matrix, (q0 % 2) * half, half, 0)
-    pivot, inverse_part = lax.optimization_barrier(
-        (exchange_row(candidate, row, q0 // 2), inverses[0])
-    )
+    mask_c = lax.dynamic_slice(
+        pattern[0].astype(jnp.float32) * a0[:, None] * a0[None, :],
+        (row_first, q1 * PB),
+        (rb, PB),
+    )
+    mask_r = lax.dynamic_slice(
+        pattern[0].astype(jnp.float32) * a0[:, None] * a0[None, :],
+        (q1 * PB, col_first),
+        (PB, cb),
+    )
+
+    panel0 = jnp.where(col == q0, matrix, 0.0)
+    panel1 = jnp.where(col == q1, matrix, 0.0)
+    panel0, panel1, matrix = lax.optimization_barrier((panel0, panel1, matrix))
+    left0, column1 = lax.psum((panel0, panel1), "col")
+
+    candidates = jnp.stack(
+        [
+            lax.dynamic_slice_in_dim(matrix, (q0 % 2) * half, half, 0),
+            lax.dynamic_slice_in_dim(matrix, (q1 % 2) * half, half, 0),
+        ]
+    )
+    part0, part1, inverse_part, listed = lax.optimization_barrier(
+        (*exchange_row(candidates, row, (q0 // 2, q1 // 2)), inverses[0], lists[0])
+    )
+    rows01 = jnp.concatenate(gather_row(jnp.stack([part0, part1]), row), axis=1)
     inv = jnp.concatenate(gather_row(inverse_part, row), axis=1)
-    scaled = matmul(inv[0], pivot)
-    right = jnp.concatenate(gather_row(scaled, row), axis=1)
-    matrix = matrix - by_blocks(matmul(left, right), mask0)
-
-    panel, matrix = lax.optimization_barrier((own_panel(matrix, q1), matrix))
-    left = lax.psum(panel, "col")
-    candidate = lax.dynamic_slice_in_dim(matrix, (q1 % 2) * half, half, 0)
-    pivot, listed = lax.optimization_barrier((exchange_row(candidate, row, q1 // 2), lists[0]))
-    scaled = matmul(inv[1], pivot)
-    right = jnp.concatenate(gather_row(scaled, row), axis=1)
+    x_part = spread_part(part0, col, q1)
+    y_part = spread_part(part1, col, q0)
+    crossed = jnp.concatenate(gather_row(jnp.stack([x_part, y_part]), row), axis=1)
     mine = lax.dynamic_slice(listed, *here)
     theirs = xor_send(mine, "layer", 2)
     listed = lax.all_gather(mine, "layer", axis_index_groups=Y_GROUPS)
-    left, right, theirs, listed = lax.optimization_barrier((left, right, theirs, listed))
-    acc = by_blocks(matrix - by_blocks(matmul(left, right), mask1), kept)
+
+    right0 = matmul(inv[0], rows01[0])
+    right0x = matmul(inv[0], crossed[0])
+    right1 = matmul(inv[1], rows01[1] - by_blocks(matmul(crossed[1], right0), mask_r))
+    right0, right0x, right1, theirs, listed, left0, column1 = lax.optimization_barrier(
+        (right0, right0x, right1, theirs, listed, left0, column1)
+    )
+
+    left1 = column1 - by_blocks(matmul(left0, right0x), mask_c)
+    matrix = matrix - by_blocks(matmul(left0, right0), mask0)
+    acc = by_blocks(matrix - by_blocks(matmul(left1, right1), mask1), kept)
 
     def bit(values, b):
         return (values // 2**b % 2).astype(jnp.float32)

time: 494 us -> 477 us (0.966)
  the two profiles are of different devices: /device:TPU:24 before, /device:TPU:6 now
where the time goes in v5:
time: 477 us; the launch traced here: 475 us
  waiting for transfers between devices  200 us (42%)
  starting transfers between devices  154 us (32%)
  blocking collectives  38 us (8%)
  other arithmetic  26.1 us (5%)
  between operations  24 us (5%)
  matrix products  15.1 us (3%)
  local copies, waits for them, and re-layouts  13.5 us (3%)
    ppermute x17, starting transfers between devices, xor_send(): return lax.ppermute(value, axis, pairs)  151 us
    ppermute x17, waiting for transfers between devices, xor_send(): return lax.ppermute(value, axis, pairs)  145 us
    psum x1, waiting for transfers between devices, body(): left0, column1 = lax.psum((panel0, panel1), 'col')  31 us
    all_to_all x1, blocking collectives, turn(): lax.all_to_all(value.reshape(4, -1, cols), 'layer', 0, 0, axis_index_grou...  26.9 us
    all_to_all x1, waiting for transfers between devices, turn(): lax.all_to_all(value.reshape(4, -1, cols), 'layer', 0, 0, axis_index_grou...  24.5 us
    dot_general x7, matrix products, matmul(): jnp.dot(left_side, right_side, precision=lax.Precision.HIGH, preferred_el...  15.1 us
    all_gather x1, blocking collectives, body(): listed = lax.all_gather(mine, 'layer', axis_index_groups=Y_GROUPS)  11.1 us
  transfers between devices with their start and end apart: 19, of which 8 were waited for; matrix products, arithmetic and copies ran while one was open for 6% of the time, Pallas kernels for 0%

profile of v5, /device:TPU:6, one launch (start us, length us, event | category | flops | bytes accessed | tf_op | source)
XLA Modules:
  0.0 475.5 jit_solution(15287759374956876645)
XLA Ops:
  13.2 4.4 broadcast_select_fusion
  19.1 2.7 collective-permute-start.22
  21.8 8.4 %collective-permute-start.21 = (f32[2,128,512]{2,1,0:T(8,128)}, f32[2,128,512]{2,1,0:T(8,128)}, u32[]{:S(2)}, u32[]{:S(2)}) collective-permute-start(f32[2,128,512]{2,1,0:T(8,128)} %get-tuple-element.912), channel_id=1, source_target_pairs={{0,16},{8,24},{16,0},{24,8},{1,17},{9,25},{17,1},{25,9},{2,18},{10... | collective-permute-start | bytes 1572872 | tf_op jit(solution)/shard_map/ppermute | solution.py:29
  38.9 7.0 %collective-permute-done.21 = f32[2,128,512]{2,1,0:T(8,128)} collective-permute-done((f32[2,128,512]{2,1,0:T(8,128)}, f32[2,128,512]{2,1,0:T(8,128)}, u32[]{:S(2)}, u32[]{:S(2)}) %collective-permute-start.21) | collective-permute-done | bytes 524320 | tf_op jit(solution)/shard_map/ppermute | solution.py:29
  46.0 5.7 %collective-permute-done.20 = f32[2,128,512]{2,1,0:T(8,128)S(1)} collective-permute-done((f32[2,128,512]{2,1,0:T(8,128)}, f32[2,128,512]{2,1,0:T(8,128)S(1)}, u32[]{:S(2)}, u32[]{:S(2)}) %collective-permute-start.20) | collective-permute-done | bytes 524320 | tf_op jit(solution)/shard_map/ppermute | solution.py:29
  54.9 5.5 %collective-permute-start.26 = (f32[2,128,512]{2,1,0:T(8,128)}, f32[2,128,512]{2,1,0:T(8,128)S(1)}, u32[]{:S(2)}, u32[]{:S(2)}) collective-permute-start(f32[2,128,512]{2,1,0:T(8,128)} %pad_maximum_fusion.4), channel_id=1, source_target_pairs={{0,24},{8,16},{16,8},{24,0},{1,25},{9,17},{17,9},{25,1},{2,26},{10... | collective-permute-start | bytes 1572872 | tf_op jit(solution)/shard_map/ppermute | solution.py:29
  62.3 2.8 collective-permute-start.28
  68.3 56.7 %collective-permute-start.30 = (f32[128,512]{1,0:T(8,128)}, f32[128,512]{1,0:T(8,128)}, u32[]{:S(2)}, u32[]{:S(2)}) collective-permute-start(f32[128,512]{1,0:T(8,128)} %broadcast_select_fusion.3), channel_id=1, source_target_pairs={{0,1},{1,0},{2,3},{3,2},{4,5},{5,4},{6,7},{7,6},{8,9},{9,8},{10,11... | collective-permute-start | bytes 786440 | tf_op jit(solution)/shard_map/cond/branch_1_fun/ppermute | solution.py:29
  127.2 39.2 %collective-permute-start.29 = (f32[128,512]{1,0:T(8,128)}, f32[128,512]{1,0:T(8,128)S(1)}, u32[]{:S(2)}, u32[]{:S(2)}) collective-permute-start(f32[128,512]{1,0:T(8,128)} %broadcast_select_fusion.5), channel_id=1, source_target_pairs={{0,1},{1,0},{2,3},{3,2},{4,5},{5,4},{6,7},{7,6},{8,9},{9,8},{10,11... | collective-permute-start | bytes 786440 | tf_op jit(solution)/shard_map/cond/branch_1_fun/ppermute | solution.py:29
  167.3 11.1 %all-gather.1 = s32[4,8,4]{1,2,0:T(4,128)S(1)} all-gather(s32[1,8,4]{1,2,0:T(4,128)S(1)} %bitcast.357), channel_id=2, replica_groups={{0,128,256,384},{32,160,288,416},{64,192,320,448},{96,224,352,480},{1,1..., dimensions={0}, use_global_device_ids=true | all-gather | bytes 640 | tf_op jit(solution)/shard_map/all_gather | solution.py:196
  178.4 2.6 collective-permute-start.23
  182.0 4.3 collective-permute-start.24
  186.4 2.9 collective-permute-start.25
  189.3 8.0 %collective-permute-start.34 = (s32[8,4]{1,0:T(8,128)S(1)}, s32[8,4]{1,0:T(8,128)S(1)}, u32[]{:S(2)}, u32[]{:S(2)}) collective-permute-start(s32[8,4]{1,0:T(8,128)S(1)} %get-tuple-element.894), channel_id=1, source_target_pairs={{0,64},{32,96},{64,0},{96,32},{128,192},{160,224},{192,128},{224,1... | collective-permute-start | bytes 392 | tf_op jit(solution)/shard_map/ppermute | solution.py:29
  197.4 2.5 collective-permute-start.31
  202.6 3.4 collective-permute-done.23
  208.0 2.3 collective-permute-start.33
  212.1 12.4 %collective-permute-done.31 = f32[2,128,512]{2,1,0:T(8,128)S(1)} collective-permute-done((f32[2,128,512]{2,1,0:T(8,128)S(1)}, f32[2,128,512]{2,1,0:T(8,128)S(1)}, u32[]{:S(2)}, u32[]{:S(2)}) %collective-permute-start.31) | collective-permute-done | bytes 524320 | tf_op jit(solution)/shard_map/ppermute | solution.py:29
  224.5 3.6 collective-permute-done.33
  230.0 2.0 fusion.5
  232.1 2.1 fusion.7
  234.2 31.0 %all-reduce.3.cloned.1.call-done = (f32[1024,512]{1,0:T(8,128)}, f32[1024,512]{1,0:T(8,128)}) async-done(((f32[1024,512]{1,0:T(8,128)}, f32[1024,512]{1,0:T(8,128)}), (f32[1024,512]{1,0:T(8,128)}, f32[1024,512]{1,0:T(8,128)})) %all-reduce.3.cloned.1.call-update) | async-done | bytes 4194320 | tf_op jit(solution)/shard_map/psum | solution.py:178
  265.2 3.6 fusion.69
  271.9 3.5 bitcast_multiply_fusion.1
  282.5 3.4 fusion
  285.9 123.8 %conditional.9 = (f32[1024,512]{1,0:T(8,128)}) conditional(s32[]{:T(128)} %clamp.3, f32[1024,512]{1,0:T(8,128)} %fusion, (pred[8,4]{1,0:T(8,128)(4,1)S(1)}, s32[32,1]{1,0:T(8,128)S(1)}, pred[8,4]{1,0:T(8,128)(4,1)S(1)}, s32[32,1]{1,0:T(8,128)S(1)}, f32[1024,512]{1,0:T(8,128)}) %tuple.89, (pred[8,4]{1,0:T(8,128)(4,1)S(1)}, ...), branch_computations={%region_14.15_spmd, %region_15.16_spmd, %region_16.17_spmd, %regio... | conditional | flops 256 | bytes 12584816 | solution.py:140
  288.8 5.2 %collective-permute-start.12 = (f32[18,128,128]{2,1,0:T(8,128)S(1)}, f32[18,128,128]{2,1,0:T(8,128)}, u32[]{:S(2)}, u32[]{:S(2)}) collective-permute-start(f32[18,128,128]{2,1,0:T(8,128)S(1)} %branch_9_fun.2), channel_id=1, source_target_pairs={{0,64},{32,96},{64,0},{96,32},{128,192},{160,224},{192,128},{224,1... | collective-permute-start | bytes 3538952 | tf_op jit(solution)/shard_map/cond/branch_9_fun/ppermute | solution.py:29
  294.2 112.4 %collective-permute-done.12.packed = f32[18,128,128]{2,1,0:T(8,128)} collective-permute-done((f32[18,128,128]{2,1,0:T(8,128)S(1)}, f32[18,128,128]{2,1,0:T(8,128)}, u32[]{:S(2)}, u32[]{:S(2)}) %collective-permute-start.12) | collective-permute-done | bytes 1179680 | tf_op jit(solution)/shard_map/cond/branch_9_fun/ppermute | solution.py:29
  406.6 3.2 branch_9_fun.3
  409.8 3.6 all-to-all-start
  414.2 24.5 %all-to-all-done = f32[4,256,512]{2,1,0:T(8,128)S(1)} async-done(((f32[4,256,512]{2,1,0:T(8,128)}), f32[4,256,512]{2,1,0:T(8,128)S(1)}, u32[]{:S(2)}, u32[]{:S(2)}) %all-to-all-start) | async-done | bytes 2097184 | tf_op jit(solution)/shard_map/all_to_all | solution.py:220
  440.4 26.9 %all_to_all.10 = f32[4,256,512]{2,1,0:T(8,128)S(1)} all-to-all(f32[4,256,512]{2,1,0:T(8,128)S(1)} %pad_maximum_fusion.3), channel_id=1, replica_groups={{0,128,256,384},{32,160,288,416},{64,192,320,448},{96,224,352,480},{1,1..., dimensions={0} | all-to-all | bytes 4194304 | tf_op jit(solution)/shard_map/all_to_all | solution.py:220
  (158 shorter events, 47.2 us)
Async XLA Ops:
  6.5 258.6 %all-reduce.3.cloned.1.call-start = ((), (), s32[]{:S(2)}) async-start(), calls=%async_computation.2 | async-start | bytes 8388608 | tf_op jit(solution)/shard_map/psum | solution.py:178
  13.2 4.4 copy-start
  19.1 19.9 %collective-permute-start.22 = (f32[2,128,512]{2,1,0:T(8,128)}, f32[2,128,512]{2,1,0:T(8,128)}, u32[]{:S(2)}, u32[]{:S(2)}) collective-permute-start(f32[2,128,512]{2,1,0:T(8,128)} %get-tuple-element.913), channel_id=1, source_target_pairs={{0,8},{8,0},{16,24},{24,16},{1,9},{9,1},{17,25},{25,17},{2,10},{10... | collective-permute-start | bytes 1572872 | tf_op jit(solution)/shard_map/ppermute | solution.py:29
  21.8 24.1 %collective-permute-start.21 = (f32[2,128,512]{2,1,0:T(8,128)}, f32[2,128,512]{2,1,0:T(8,128)}, u32[]{:S(2)}, u32[]{:S(2)}) collective-permute-start(f32[2,128,512]{2,1,0:T(8,128)} %get-tuple-element.912), channel_id=1, source_target_pairs={{0,16},{8,24},{16,0},{24,8},{1,17},{9,25},{17,1},{25,9},{2,18},{10... | collective-permute-start | bytes 1572872 | tf_op jit(solution)/shard_map/ppermute | solution.py:29
  30.2 5.1 %copy-start.9 = (s32[2,32,32]{2,1,0:T(8,128)S(1)}, s32[2,32,32]{2,1,0:T(8,128)}, u32[]{:S(2)}) copy-start(s32[2,32,32]{2,1,0:T(8,128)} %param.32) | copy-start | bytes 24580
  30.2 21.5 %collective-permute-start.20 = (f32[2,128,512]{2,1,0:T(8,128)}, f32[2,128,512]{2,1,0:T(8,128)S(1)}, u32[]{:S(2)}, u32[]{:S(2)}) collective-permute-start(f32[2,128,512]{2,1,0:T(8,128)} %get-tuple-element.911), channel_id=1, source_target_pairs={{0,24},{8,16},{16,8},{24,0},{1,25},{9,17},{17,9},{25,1},{2,26},{10... | collective-permute-start | bytes 1572872 | tf_op jit(solution)/shard_map/ppermute | solution.py:29
  54.9 131.5 %collective-permute-start.26 = (f32[2,128,512]{2,1,0:T(8,128)}, f32[2,128,512]{2,1,0:T(8,128)S(1)}, u32[]{:S(2)}, u32[]{:S(2)}) collective-permute-start(f32[2,128,512]{2,1,0:T(8,128)} %pad_maximum_fusion.4), channel_id=1, source_target_pairs={{0,24},{8,16},{16,8},{24,0},{1,25},{9,17},{17,9},{25,1},{2,26},{10... | collective-permute-start | bytes 1572872 | tf_op jit(solution)/shard_map/ppermute | solution.py:29
  60.4 128.9 %collective-permute-start.27 = (f32[2,128,512]{2,1,0:T(8,128)}, f32[2,128,512]{2,1,0:T(8,128)}, u32[]{:S(2)}, u32[]{:S(2)}) collective-permute-start(f32[2,128,512]{2,1,0:T(8,128)} %pad_maximum_fusion.4), channel_id=1, source_target_pairs={{0,16},{8,24},{16,0},{24,8},{1,17},{9,25},{17,1},{25,9},{2,18},{10... | collective-permute-start | bytes 1572872 | tf_op jit(solution)/shard_map/ppermute | solution.py:29
  62.3 135.0 %collective-permute-start.28 = (f32[2,128,512]{2,1,0:T(8,128)}, f32[2,128,512]{2,1,0:T(8,128)}, u32[]{:S(2)}, u32[]{:S(2)}) collective-permute-start(f32[2,128,512]{2,1,0:T(8,128)} %pad_maximum_fusion.4), channel_id=1, source_target_pairs={{0,8},{8,0},{16,24},{24,16},{1,9},{9,1},{17,25},{25,17},{2,10},{10... | collective-permute-start | bytes 1572872 | tf_op jit(solution)/shard_map/ppermute | solution.py:29
  68.3 110.0 %collective-permute-start.30 = (f32[128,512]{1,0:T(8,128)}, f32[128,512]{1,0:T(8,128)}, u32[]{:S(2)}, u32[]{:S(2)}) collective-permute-start(f32[128,512]{1,0:T(8,128)} %broadcast_select_fusion.3), channel_id=1, source_target_pairs={{0,1},{1,0},{2,3},{3,2},{4,5},{5,4},{6,7},{7,6},{8,9},{9,8},{10,11... | collective-permute-start | bytes 786440 | tf_op jit(solution)/shard_map/cond/branch_1_fun/ppermute | solution.py:29
  127.2 54.8 %collective-permute-start.29 = (f32[128,512]{1,0:T(8,128)}, f32[128,512]{1,0:T(8,128)S(1)}, u32[]{:S(2)}, u32[]{:S(2)}) collective-permute-start(f32[128,512]{1,0:T(8,128)} %broadcast_select_fusion.5), channel_id=1, source_target_pairs={{0,1},{1,0},{2,3},{3,2},{4,5},{5,4},{6,7},{7,6},{8,9},{9,8},{10,11... | collective-permute-start | bytes 786440 | tf_op jit(solution)/shard_map/cond/branch_1_fun/ppermute | solution.py:29
  167.3 19.1 %copy-start.5 = (f32[1,2,128,512]{3,2,1,0:T(8,128)S(1)}, f32[1,2,128,512]{3,2,1,0:T(8,128)}, u32[]{:S(2)}) copy-start(f32[1,2,128,512]{3,2,1,0:T(8,128)} %param.31) | copy-start | bytes 1572868
  178.4 27.7 %collective-permute-start.23 = (f32[2,128,512]{2,1,0:T(8,128)}, f32[2,128,512]{2,1,0:T(8,128)S(1)}, u32[]{:S(2)}, u32[]{:S(2)}) collective-permute-start(f32[2,128,512]{2,1,0:T(8,128)} %bitcast.344), channel_id=1, source_target_pairs={{0,24},{8,16},{16,8},{24,0},{1,25},{9,17},{17,9},{25,1},{2,26},{10... | collective-permute-start | bytes 1572872 | tf_op jit(solution)/shard_map/ppermute | solution.py:29
  182.0 25.9 %collective-permute-start.24 = (f32[2,128,512]{2,1,0:T(8,128)}, f32[2,128,512]{2,1,0:T(8,128)S(1)}, u32[]{:S(2)}, u32[]{:S(2)}) collective-permute-start(f32[2,128,512]{2,1,0:T(8,128)} %bitcast.345), channel_id=1, source_target_pairs={{0,16},{8,24},{16,0},{24,8},{1,17},{9,25},{17,1},{25,9},{2,18},{10... | collective-permute-start | bytes 1572872 | tf_op jit(solution)/shard_map/ppermute | solution.py:29
  186.4 23.9 %collective-permute-start.25 = (f32[2,128,512]{2,1,0:T(8,128)S(1)}, f32[2,128,512]{2,1,0:T(8,128)S(1)}, u32[]{:S(2)}, u32[]{:S(2)}) collective-permute-start(f32[2,128,512]{2,1,0:T(8,128)S(1)} %bitcast.346), channel_id=1, source_target_pairs={{0,8},{8,0},{16,24},{24,16},{1,9},{9,1},{17,25},{25,17},{2,10},{10... | collective-permute-start | bytes 1572872 | tf_op jit(solution)/shard_map/ppermute | solution.py:29
  189.3 44.8 %collective-permute-start.34 = (s32[8,4]{1,0:T(8,128)S(1)}, s32[8,4]{1,0:T(8,128)S(1)}, u32[]{:S(2)}, u32[]{:S(2)}) collective-permute-start(s32[8,4]{1,0:T(8,128)S(1)} %get-tuple-element.894), channel_id=1, source_target_pairs={{0,64},{32,96},{64,0},{96,32},{128,192},{160,224},{192,128},{224,1... | collective-permute-start | bytes 392 | tf_op jit(solution)/shard_map/ppermute | solution.py:29
  197.4 27.2 %collective-permute-start.31 = (f32[2,128,512]{2,1,0:T(8,128)S(1)}, f32[2,128,512]{2,1,0:T(8,128)S(1)}, u32[]{:S(2)}, u32[]{:S(2)}) collective-permute-start(f32[2,128,512]{2,1,0:T(8,128)S(1)} %pad_maximum_fusion.5), channel_id=1, source_target_pairs={{0,24},{8,16},{16,8},{24,0},{1,25},{9,17},{17,9},{25,1},{2,26},{10... | collective-permute-start | bytes 1572872 | tf_op jit(solution)/shard_map/ppermute | solution.py:29
  206.0 18.5 %collective-permute-start.32 = (f32[2,128,512]{2,1,0:T(8,128)S(1)}, f32[2,128,512]{2,1,0:T(8,128)S(1)}, u32[]{:S(2)}, u32[]{:S(2)}) collective-permute-start(f32[2,128,512]{2,1,0:T(8,128)S(1)} %pad_maximum_fusion.5), channel_id=1, source_target_pairs={{0,16},{8,24},{16,0},{24,8},{1,17},{9,25},{17,1},{25,9},{2,18},{10... | collective-permute-start | bytes 1572872 | tf_op jit(solution)/shard_map/ppermute | solution.py:29
  208.0 20.2 %collective-permute-start.33 = (f32[2,128,512]{2,1,0:T(8,128)S(1)}, f32[2,128,512]{2,1,0:T(8,128)S(1)}, u32[]{:S(2)}, u32[]{:S(2)}) collective-permute-start(f32[2,128,512]{2,1,0:T(8,128)S(1)} %pad_maximum_fusion.5), channel_id=1, source_target_pairs={{0,8},{8,0},{16,24},{24,16},{1,9},{9,1},{17,25},{25,17},{2,10},{10... | collective-permute-start | bytes 1572872 | tf_op jit(solution)/shard_map/ppermute | solution.py:29
  265.2 3.6 copy-start.1
  265.2 3.6 copy-start.2
  268.8 1.9 copy-start.4
  270.7 1.2 copy-start.3
  275.4 7.1 %collective-permute-start.35 = (f32[1024,512]{1,0:T(8,128)}, f32[1024,512]{1,0:T(8,128)S(1)}, u32[]{:S(2)}, u32[]{:S(2)}) collective-permute-start(f32[1024,512]{1,0:T(8,128)} %bitcast_multiply_fusion.1), channel_id=1, source_target_pairs={{0,32},{32,0},{64,96},{96,64},{128,160},{160,128},{192,224},{224,1... | collective-permute-start | bytes 6291464 | tf_op jit(solution)/shard_map/ppermute | solution.py:29
  288.8 117.8 %collective-permute-start.12 = (f32[18,128,128]{2,1,0:T(8,128)S(1)}, f32[18,128,128]{2,1,0:T(8,128)}, u32[]{:S(2)}, u32[]{:S(2)}) collective-permute-start(f32[18,128,128]{2,1,0:T(8,128)S(1)} %branch_9_fun.2), channel_id=1, source_target_pairs={{0,64},{32,96},{64,0},{96,32},{128,192},{160,224},{192,128},{224,1... | collective-permute-start | bytes 3538952 | tf_op jit(solution)/shard_map/cond/branch_9_fun/ppermute | solution.py:29
  409.8 3.7 copy-start.15
  409.8 3.7 copy-start.10
  409.8 3.8 copy-start.14
  409.8 3.8 copy-start.13
  409.8 3.9 copy-start.12
  409.8 4.0 copy-start.11
  409.8 28.9 %all-to-all-start = ((f32[4,256,512]{2,1,0:T(8,128)}), f32[4,256,512]{2,1,0:T(8,128)S(1)}, u32[]{:S(2)}, u32[]{:S(2)}) async-start(f32[4,256,512]{2,1,0:T(8,128)} %bitcast.66), calls=%async_computation | async-start | bytes 4194304 | tf_op jit(solution)/shard_map/all_to_all | solution.py:220
  (1 other events, 0.8 us)
Sparse Core Ops, SparseCore 0:
  32.3 232.8 all-reduce.2

commit v6 on v5

--- a/solution.py
+++ b/solution.py
@@ -11,7 +11,7 @@
 P_SIZE = 512
 BLK = 128
 PB = P_SIZE // BLK
-STEP = 2
+SIZES = (3, 6, 8, *range(9, 25), 26, 28, 30, 32)
 Y_GROUPS = [[first + 4 * k for k in range(4)] for first in range(4)]
 
 
@@ -69,31 +69,45 @@
     return value
 
 
-def blocks_of(rows, cols):
-    return [(i, j) for i in range(rows // BLK) for j in range(cols // BLK)]
-
-
-def pack_kernel(slots, value, packed):
-    for b, (i, j) in enumerate(blocks_of(*value.shape)):
+def over_blocks(shape, step):
+    per_row = shape[1] // BLK
+
+    def one(b, _):
+        row_start = pl.multiple_of(b // per_row * BLK, BLK)
+        col_start = pl.multiple_of(b % per_row * BLK, BLK)
+        step(b, (pl.ds(row_start, BLK), pl.ds(col_start, BLK)))
+        return 0
+
+    lax.fori_loop(0, shape[0] // BLK * per_row, one, 0)
+
+
+def pack_kernel(taken, slots, value, other, packed, merged):
+    def step(b, at):
+        merged[at] = value[at]
+
+        @pl.when(taken[b] > 0)
+        def _():
+            merged[at] = merged[at] + other[at]
+
         slot = slots[b]
 
         @pl.when(slot >= 0)
         def _():
-            packed[slot] = value[i * BLK : (i + 1) * BLK, j * BLK : (j + 1) * BLK]
+            packed[slot] = merged[at]
+
+    over_blocks(value.shape, step)
 
 
 def add_kernel(slots, value, packed, out):
-    for b, (i, j) in enumerate(blocks_of(*value.shape)):
+    def step(b, at):
+        out[at] = value[at]
         slot = slots[b]
-        at = (slice(i * BLK, (i + 1) * BLK), slice(j * BLK, (j + 1) * BLK))
 
         @pl.when(slot >= 0)
         def _():
-            out[at] = value[at] + packed[slot]
-
-        @pl.when(slot < 0)
-        def _():
-            out[at] = value[at]
+            out[at] = out[at] + packed[slot]
+
+    over_blocks(value.shape, step)
 
 
 SMEM = pl.BlockSpec(memory_space=pltpu.SMEM)
@@ -101,14 +115,17 @@
 PARAMS = pltpu.CompilerParams(vmem_limit_bytes=24 * 2**20)
 
 
-def pack(slots, value, size):
+def pack(taken, slots, value, other, size):
     return pl.pallas_call(
         pack_kernel,
-        out_shape=jax.ShapeDtypeStruct((size, BLK, BLK), jnp.float32),
-        in_specs=[SMEM, VMEM],
-        out_specs=VMEM,
+        out_shape=(
+            jax.ShapeDtypeStruct((size, BLK, BLK), jnp.float32),
+            jax.ShapeDtypeStruct(value.shape, jnp.float32),
+        ),
+        in_specs=[SMEM, SMEM, VMEM, VMEM],
+        out_specs=(VMEM, VMEM),
         compiler_params=PARAMS,
-    )(slots, value)
+    )(taken, slots, value, other)
 
 
 def add_packed(slots, value, packed):
@@ -126,18 +143,22 @@
     return jnp.where(flat > 0, jnp.cumsum(flat) - 1, -1), jnp.sum(flat)
 
 
-def listed_exchange(acc, wanted_here, wanted_there, mask):
+def listed_exchange(value, other, taken, wanted_here, wanted_there, mask):
     to_send, n_send = slots_of(wanted_there)
     to_add, n_add = slots_of(wanted_here)
-    most = to_send.shape[0]
-
-    def branch(size, value):
-        packed = pack(to_send, value, size)
-        return add_packed(to_add, value, xor_send(packed, "layer", mask))
-
-    choices = [lambda value: value]
-    choices += [functools.partial(branch, s) for s in range(STEP, most + 1, STEP)]
-    return lax.switch((jnp.maximum(n_send, n_add) + STEP - 1) // STEP, choices, acc)
+    taken_flat = taken.reshape(-1).astype(jnp.int32)
+
+    def alone(value, other):
+        return value + by_blocks(other, taken)
+
+    def branch(size, value, other):
+        packed, merged = pack(taken_flat, to_send, value, other, size)
+        return add_packed(to_add, merged, xor_send(packed, "layer", mask))
+
+    choices = [alone] + [functools.partial(branch, size) for size in SIZES]
+    needed = jnp.maximum(n_send, n_add)
+    index = (needed > jnp.array((0, *SIZES), jnp.int32)).sum().astype(jnp.int32)
+    return lax.switch(index, choices, value, other)
 
 
 def body(front, inverses, pattern, order, lists):
@@ -174,25 +195,26 @@
 
     panel0 = jnp.where(col == q0, matrix, 0.0)
     panel1 = jnp.where(col == q1, matrix, 0.0)
-    panel0, panel1, matrix = lax.optimization_barrier((panel0, panel1, matrix))
+    panel0, panel1, matrix, listed = lax.optimization_barrier((panel0, panel1, matrix, lists[0]))
     left0, column1 = lax.psum((panel0, panel1), "col")
+    mine = lax.dynamic_slice(listed, *here)
+    theirs = xor_send(mine, "layer", 2)
+    theirs, matrix = lax.optimization_barrier((theirs, matrix))
 
     candidates = jnp.stack(
         [
-            lax.dynamic_slice_in_dim(matrix, (q0 % 2) * half, half, 0),
-            lax.dynamic_slice_in_dim(matrix, (q1 % 2) * half, half, 0),
+            lax.dynamic_slice_in_dim(matrix, (q0 & 1) * half, half, 0),
+            lax.dynamic_slice_in_dim(matrix, (q1 & 1) * half, half, 0),
         ]
     )
-    part0, part1, inverse_part, listed = lax.optimization_barrier(
-        (*exchange_row(candidates, row, (q0 // 2, q1 // 2)), inverses[0], lists[0])
+    part0, part1, inverse_part = lax.optimization_barrier(
+        (*exchange_row(candidates, row, (q0 >> 1, q1 >> 1)), inverses[0])
     )
     rows01 = jnp.concatenate(gather_row(jnp.stack([part0, part1]), row), axis=1)
     inv = jnp.concatenate(gather_row(inverse_part, row), axis=1)
     x_part = spread_part(part0, col, q1)
     y_part = spread_part(part1, col, q0)
     crossed = jnp.concatenate(gather_row(jnp.stack([x_part, y_part]), row), axis=1)
-    mine = lax.dynamic_slice(listed, *here)
-    theirs = xor_send(mine, "layer", 2)
     listed = lax.all_gather(mine, "layer", axis_index_groups=Y_GROUPS)
 
     right0 = matmul(inv[0], rows01[0])
@@ -209,9 +231,14 @@
     def bit(values, b):
         return (values // 2**b % 2).astype(jnp.float32)
 
-    acc = acc + by_blocks(xor_send(acc, "layer", 1), bit(mine, 0))
-
-    acc = listed_exchange(acc, bit(mine, 1) * kept > 0, bit(theirs, 1) * kept > 0, 2)
+    acc = listed_exchange(
+        acc,
+        xor_send(acc, "layer", 1),
+        bit(mine, 0),
+        bit(mine, 1) * kept > 0,
+        bit(theirs, 1) * kept > 0,
+        2,
+    )
 
     yy = layer // 4
     qb = rb // 4

time: 477 us -> 451 us (0.945)
  the two profiles are of different devices: /device:TPU:6 before, /device:TPU:229 now
where the time goes in v6:
time: 451 us; the launch traced here: 450 us
  waiting for transfers between devices  186 us (41%)
  starting transfers between devices  151 us (33%)
  blocking collectives  38.8 us (9%)
  between operations  21.6 us (5%)
  other arithmetic  19.2 us (4%)
  matrix products  15.3 us (3%)
  local copies, waits for them, and re-layouts  10.3 us (2%)
  Pallas kernels  7.5 us (2%)
    ppermute x17, waiting for transfers between devices, xor_send(): return lax.ppermute(value, axis, pairs)  152 us
    ppermute x17, starting transfers between devices, xor_send(): return lax.ppermute(value, axis, pairs)  148 us
    all_to_all x1, blocking collectives, turn(): lax.all_to_all(value.reshape(4, -1, cols), 'layer', 0, 0, axis_index_grou...  29.2 us
    all_to_all x1, waiting for transfers between devices, turn(): lax.all_to_all(value.reshape(4, -1, cols), 'layer', 0, 0, axis_index_grou...  24.8 us
    dot_general x7, matrix products, matmul(): jnp.dot(left_side, right_side, precision=lax.Precision.HIGH, preferred_el...  15.3 us
    all_gather x1, blocking collectives, body(): listed = lax.all_gather(mine, 'layer', axis_index_groups=Y_GROUPS)  9.62 us
  transfers between devices with their start and end apart: 19, of which 10 were waited for; matrix products, arithmetic and copies ran while one was open for 5% of the time, Pallas kernels for 0%

profile of v6, /device:TPU:229, one launch (start us, length us, event | category | flops | bytes accessed | tf_op | source)
XLA Modules:
  0.0 450.0 jit_solution(17370478673839944265)
XLA Ops:
  10.8 4.3 broadcast_select_fusion
  15.8 8.1 %collective-permute-start.27 = (s32[8,4]{1,0:T(8,128)S(1)}, s32[8,4]{1,0:T(8,128)S(1)}, u32[]{:S(2)}, u32[]{:S(2)}) collective-permute-start(s32[8,4]{1,0:T(8,128)S(1)} %get-tuple-element.1647), channel_id=1, source_target_pairs={{0,64},{32,96},{64,0},{96,32},{128,192},{160,224},{192,128},{224,1... | collective-permute-start | bytes 392 | tf_op jit(solution)/shard_map/ppermute | solution.py:29
  30.5 2.8 collective-permute-start.30
  33.3 2.4 collective-permute-start.29
  35.7 3.1 collective-permute-start.28
  41.8 9.6 %all-gather.1 = s32[4,8,4]{1,2,0:T(4,128)S(1)} all-gather(s32[1,8,4]{1,2,0:T(4,128)S(1)} %bitcast.385), channel_id=2, replica_groups={{0,128,256,384},{32,160,288,416},{64,192,320,448},{96,224,352,480},{1,1..., dimensions={0}, use_global_device_ids=true | all-gather | bytes 640 | tf_op jit(solution)/shard_map/all_gather | solution.py:218
  51.6 3.9 collective-permute-done.29
  55.5 4.7 %collective-permute-done.28 = f32[2,128,512]{2,1,0:T(8,128)} collective-permute-done((f32[2,128,512]{2,1,0:T(8,128)}, f32[2,128,512]{2,1,0:T(8,128)}, u32[]{:S(2)}, u32[]{:S(2)}) %collective-permute-start.28) | collective-permute-done | bytes 524320 | tf_op jit(solution)/shard_map/ppermute | solution.py:29
  64.3 53.3 %collective-permute-start.38 = (f32[128,512]{1,0:T(8,128)S(1)}, f32[128,512]{1,0:T(8,128)S(1)}, u32[]{:S(2)}, u32[]{:S(2)}) collective-permute-start(f32[128,512]{1,0:T(8,128)S(1)} %broadcast_select_fusion.3), channel_id=1, source_target_pairs={{0,1},{1,0},{2,3},{3,2},{4,5},{5,4},{6,7},{7,6},{8,9},{9,8},{10,11... | collective-permute-start | bytes 786440 | tf_op jit(solution)/shard_map/cond/branch_1_fun/ppermute | solution.py:29
  121.0 26.6 %collective-permute-start.37 = (f32[128,512]{1,0:T(8,128)S(1)}, f32[128,512]{1,0:T(8,128)S(1)}, u32[]{:S(2)}, u32[]{:S(2)}) collective-permute-start(f32[128,512]{1,0:T(8,128)S(1)} %broadcast_select_fusion.5), channel_id=1, source_target_pairs={{0,1},{1,0},{2,3},{3,2},{4,5},{5,4},{6,7},{7,6},{8,9},{9,8},{10,11... | collective-permute-start | bytes 786440 | tf_op jit(solution)/shard_map/cond/branch_1_fun/ppermute | solution.py:29
  149.8 6.4 %collective-permute-start.35 = (f32[2,128,512]{2,1,0:T(8,128)S(1)}, f32[2,128,512]{2,1,0:T(8,128)S(1)}, u32[]{:S(2)}, u32[]{:S(2)}) collective-permute-start(f32[2,128,512]{2,1,0:T(8,128)S(1)} %pad_maximum_fusion.4), channel_id=1, source_target_pairs={{0,16},{8,24},{16,0},{24,8},{1,17},{9,25},{17,1},{25,9},{2,18},{10... | collective-permute-start | bytes 1572872 | tf_op jit(solution)/shard_map/ppermute | solution.py:29
  156.1 2.8 collective-permute-start.36
  159.0 3.1 collective-permute-start.31
  162.1 3.1 collective-permute-start.32
  165.3 5.3 %collective-permute-done.34 = f32[2,128,512]{2,1,0:T(8,128)S(1)} collective-permute-done((f32[2,128,512]{2,1,0:T(8,128)S(1)}, f32[2,128,512]{2,1,0:T(8,128)S(1)}, u32[]{:S(2)}, u32[]{:S(2)}) %collective-permute-start.34) | collective-permute-done | bytes 524320 | tf_op jit(solution)/shard_map/ppermute | solution.py:29
  170.6 7.4 %collective-permute-start.33 = (f32[2,128,512]{2,1,0:T(8,128)S(1)}, f32[2,128,512]{2,1,0:T(8,128)S(1)}, u32[]{:S(2)}, u32[]{:S(2)}) collective-permute-start(f32[2,128,512]{2,1,0:T(8,128)S(1)} %bitcast.374), channel_id=1, source_target_pairs={{0,8},{8,0},{16,24},{24,16},{1,9},{9,1},{17,25},{25,17},{2,10},{10... | collective-permute-start | bytes 1572872 | tf_op jit(solution)/shard_map/ppermute | solution.py:29
  178.0 4.4 collective-permute-start.39
  184.9 8.2 %collective-permute-done.31 = f32[2,128,512]{2,1,0:T(8,128)S(1)} collective-permute-done((f32[2,128,512]{2,1,0:T(8,128)}, f32[2,128,512]{2,1,0:T(8,128)S(1)}, u32[]{:S(2)}, u32[]{:S(2)}) %collective-permute-start.31) | collective-permute-done | bytes 524320 | tf_op jit(solution)/shard_map/ppermute | solution.py:29
  193.1 7.6 %collective-permute-start.41 = (f32[2,128,512]{2,1,0:T(8,128)S(1)}, f32[2,128,512]{2,1,0:T(8,128)S(1)}, u32[]{:S(2)}, u32[]{:S(2)}) collective-permute-start(f32[2,128,512]{2,1,0:T(8,128)S(1)} %pad_maximum_fusion.5), channel_id=1, source_target_pairs={{0,8},{8,0},{16,24},{24,16},{1,9},{9,1},{17,25},{25,17},{2,10},{10... | collective-permute-start | bytes 1572872 | tf_op jit(solution)/shard_map/ppermute | solution.py:29
  202.5 11.9 %collective-permute-done.39 = f32[2,128,512]{2,1,0:T(8,128)S(1)} collective-permute-done((f32[2,128,512]{2,1,0:T(8,128)S(1)}, f32[2,128,512]{2,1,0:T(8,128)S(1)}, u32[]{:S(2)}, u32[]{:S(2)}) %collective-permute-start.39) | collective-permute-done | bytes 524320 | tf_op jit(solution)/shard_map/ppermute | solution.py:29
  214.4 8.5 %collective-permute-done.41 = f32[2,128,512]{2,1,0:T(8,128)S(1)} collective-permute-done((f32[2,128,512]{2,1,0:T(8,128)S(1)}, f32[2,128,512]{2,1,0:T(8,128)S(1)}, u32[]{:S(2)}, u32[]{:S(2)}) %collective-permute-start.41) | collective-permute-done | bytes 524320 | tf_op jit(solution)/shard_map/ppermute | solution.py:29
  228.9 8.6 %all-reduce.3.cloned.1.call-done = (f32[1024,512]{1,0:T(8,128)}, f32[1024,512]{1,0:T(8,128)}) async-done(((f32[1024,512]{1,0:T(8,128)}, f32[1024,512]{1,0:T(8,128)}), (f32[1024,512]{1,0:T(8,128)}, f32[1024,512]{1,0:T(8,128)})) %all-reduce.3.cloned.1.call-update) | async-done | bytes 4194320 | tf_op jit(solution)/shard_map/psum | solution.py:199
  237.5 3.6 fusion.70
  243.2 3.5 bitcast_multiply_fusion.1
  255.3 126.5 %conditional.9 = (f32[1024,512]{1,0:T(8,128)}) conditional(s32[]{:T(128)} %clamp.3, (f32[8,4]{1,0:T(8,128)S(1)}, f32[1024,512]{1,0:T(8,128)}, f32[1024,512]{1,0:T(8,128)}) %tuple.112, (pred[8,4]{1,0:T(8,128)(4,1)S(1)}, s32[32,1]{1,0:T(8,128)S(1)}, f32[8,4]{1,0:T(8,128)S(1)}, pred[8,4]{1,0:T(8,128)(4,1)S(1)}, ...), branch_computations={%region_15.16_spmd, %region_16.17_spmd, %region_17.18_spmd, %regio... | conditional | flops 1048576 | bytes 8391024 | solution.py:161
  255.6 4.6 %branch_15_fun.2 = (f32[20,128,128]{2,1,0:T(8,128)}, f32[1024,512]{1,0:T(8,128)S(1)}) custom-call(s32[32]{0:T(128)S(1)} %convert_element_type.360.taken, s32[32]{0:T(128)S(1)} %bitcast_select_fusion.28.slots, f32[1024,512]{1,0:T(8,128)} %get-tuple-element.1041.value, f32[1024,512]{1,0:T(8,128)} %get-tuple-element.1042.other), custom_call_target="tpu_custom_call" | custom-call | tf_op jit(solution)/shard_map/cond/branch_15_fun/pallas_call | solution.py:119
  260.3 10.4 %collective-permute-start.18 = (f32[20,128,128]{2,1,0:T(8,128)}, f32[20,128,128]{2,1,0:T(8,128)S(1)}, u32[]{:S(2)}, u32[]{:S(2)}) collective-permute-start(f32[20,128,128]{2,1,0:T(8,128)} %get-tuple-element.1044), channel_id=1, source_target_pairs={{0,64},{32,96},{64,0},{96,32},{128,192},{160,224},{192,128},{224,1... | collective-permute-start | bytes 3932168 | tf_op jit(solution)/shard_map/cond/branch_15_fun/ppermute | solution.py:29
  270.9 108.1 %collective-permute-done.18.packed = f32[20,128,128]{2,1,0:T(8,128)S(1)} collective-permute-done((f32[20,128,128]{2,1,0:T(8,128)}, f32[20,128,128]{2,1,0:T(8,128)S(1)}, u32[]{:S(2)}, u32[]{:S(2)}) %collective-permute-start.18) | collective-permute-done | bytes 1310752 | tf_op jit(solution)/shard_map/cond/branch_15_fun/ppermute | solution.py:29
  378.9 2.9 branch_15_fun.3
  381.8 3.6 all-to-all-start
  386.2 24.8 %all-to-all-done = f32[4,256,512]{2,1,0:T(8,128)S(1)} async-done(((f32[4,256,512]{2,1,0:T(8,128)}), f32[4,256,512]{2,1,0:T(8,128)S(1)}, u32[]{:S(2)}, u32[]{:S(2)}) %all-to-all-start) | async-done | bytes 2097184 | tf_op jit(solution)/shard_map/all_to_all | solution.py:247
  412.7 29.2 %all_to_all.10 = f32[4,256,512]{2,1,0:T(8,128)S(1)} all-to-all(f32[4,256,512]{2,1,0:T(8,128)S(1)} %pad_maximum_fusion.3), channel_id=1, replica_groups={{0,128,256,384},{32,160,288,416},{64,192,320,448},{96,224,352,480},{1,1..., dimensions={0} | all-to-all | bytes 4194304 | tf_op jit(solution)/shard_map/all_to_all | solution.py:247
  (159 shorter events, 44.5 us)
Async XLA Ops:
  6.5 231.0 %all-reduce.3.cloned.1.call-start = ((), (), s32[]{:S(2)}) async-start(), calls=%async_computation.2 | async-start | bytes 8388608 | tf_op jit(solution)/shard_map/psum | solution.py:199
  15.8 10.9 %copy-start.11 = (s32[2,32,32]{2,1,0:T(8,128)S(1)}, s32[2,32,32]{2,1,0:T(8,128)}, u32[]{:S(2)}) copy-start(s32[2,32,32]{2,1,0:T(8,128)} %param.40) | copy-start | bytes 24580
  15.8 13.2 %copy-start = (f32[1,1024,512]{2,1,0:T(8,128)S(1)}, f32[1,1024,512]{2,1,0:T(8,128)}, u32[]{:S(2)}) copy-start(f32[1,1024,512]{2,1,0:T(8,128)} %param.38) | copy-start | bytes 6291460
  15.8 13.2 %collective-permute-start.27 = (s32[8,4]{1,0:T(8,128)S(1)}, s32[8,4]{1,0:T(8,128)S(1)}, u32[]{:S(2)}, u32[]{:S(2)}) collective-permute-start(s32[8,4]{1,0:T(8,128)S(1)} %get-tuple-element.1647), channel_id=1, source_target_pairs={{0,64},{32,96},{64,0},{96,32},{128,192},{160,224},{192,128},{224,1... | collective-permute-start | bytes 392 | tf_op jit(solution)/shard_map/ppermute | solution.py:29
  30.5 21.1 %collective-permute-start.30 = (f32[2,128,512]{2,1,0:T(8,128)}, f32[2,128,512]{2,1,0:T(8,128)S(1)}, u32[]{:S(2)}, u32[]{:S(2)}) collective-permute-start(f32[2,128,512]{2,1,0:T(8,128)} %get-tuple-element.1666), channel_id=1, source_target_pairs={{0,8},{8,0},{16,24},{24,16},{1,9},{9,1},{17,25},{25,17},{2,10},{10... | collective-permute-start | bytes 1572872 | tf_op jit(solution)/shard_map/ppermute | solution.py:29
  33.3 22.2 %collective-permute-start.29 = (f32[2,128,512]{2,1,0:T(8,128)}, f32[2,128,512]{2,1,0:T(8,128)}, u32[]{:S(2)}, u32[]{:S(2)}) collective-permute-start(f32[2,128,512]{2,1,0:T(8,128)} %get-tuple-element.1665), channel_id=1, source_target_pairs={{0,16},{8,24},{16,0},{24,8},{1,17},{9,25},{17,1},{25,9},{2,18},{10... | collective-permute-start | bytes 1572872 | tf_op jit(solution)/shard_map/ppermute | solution.py:29
  35.7 24.5 %collective-permute-start.28 = (f32[2,128,512]{2,1,0:T(8,128)}, f32[2,128,512]{2,1,0:T(8,128)}, u32[]{:S(2)}, u32[]{:S(2)}) collective-permute-start(f32[2,128,512]{2,1,0:T(8,128)} %get-tuple-element.1664), channel_id=1, source_target_pairs={{0,24},{8,16},{16,8},{24,0},{1,25},{9,17},{17,9},{25,1},{2,26},{10... | collective-permute-start | bytes 1572872 | tf_op jit(solution)/shard_map/ppermute | solution.py:29
  51.6 8.6 %copy-start.10 = (f32[2,128,512]{2,1,0:T(8,128)}, f32[2,128,512]{2,1,0:T(8,128)S(1)}, u32[]{:S(2)}) copy-start(f32[2,128,512]{2,1,0:T(8,128)S(1)} %collective-permute-done.30) | copy-start | bytes 1572868
  64.3 94.7 %collective-permute-start.38 = (f32[128,512]{1,0:T(8,128)S(1)}, f32[128,512]{1,0:T(8,128)S(1)}, u32[]{:S(2)}, u32[]{:S(2)}) collective-permute-start(f32[128,512]{1,0:T(8,128)S(1)} %broadcast_select_fusion.3), channel_id=1, source_target_pairs={{0,1},{1,0},{2,3},{3,2},{4,5},{5,4},{6,7},{7,6},{8,9},{9,8},{10,11... | collective-permute-start | bytes 786440 | tf_op jit(solution)/shard_map/cond/branch_1_fun/ppermute | solution.py:29
  120.0 42.1 %copy-start.9 = (f32[1,2,128,512]{3,2,1,0:T(8,128)S(1)}, f32[1,2,128,512]{3,2,1,0:T(8,128)}, u32[]{:S(2)}) copy-start(f32[1,2,128,512]{3,2,1,0:T(8,128)} %param.39) | copy-start | bytes 1572868
  121.0 41.1 %collective-permute-start.37 = (f32[128,512]{1,0:T(8,128)S(1)}, f32[128,512]{1,0:T(8,128)S(1)}, u32[]{:S(2)}, u32[]{:S(2)}) collective-permute-start(f32[128,512]{1,0:T(8,128)S(1)} %broadcast_select_fusion.5), channel_id=1, source_target_pairs={{0,1},{1,0},{2,3},{3,2},{4,5},{5,4},{6,7},{7,6},{8,9},{9,8},{10,11... | collective-permute-start | bytes 786440 | tf_op jit(solution)/shard_map/cond/branch_1_fun/ppermute | solution.py:29
  147.7 22.9 %collective-permute-start.34 = (f32[2,128,512]{2,1,0:T(8,128)S(1)}, f32[2,128,512]{2,1,0:T(8,128)S(1)}, u32[]{:S(2)}, u32[]{:S(2)}) collective-permute-start(f32[2,128,512]{2,1,0:T(8,128)S(1)} %pad_maximum_fusion.4), channel_id=1, source_target_pairs={{0,24},{8,16},{16,8},{24,0},{1,25},{9,17},{17,9},{25,1},{2,26},{10... | collective-permute-start | bytes 1572872 | tf_op jit(solution)/shard_map/ppermute | solution.py:29
  149.8 28.3 %collective-permute-start.35 = (f32[2,128,512]{2,1,0:T(8,128)S(1)}, f32[2,128,512]{2,1,0:T(8,128)S(1)}, u32[]{:S(2)}, u32[]{:S(2)}) collective-permute-start(f32[2,128,512]{2,1,0:T(8,128)S(1)} %pad_maximum_fusion.4), channel_id=1, source_target_pairs={{0,16},{8,24},{16,0},{24,8},{1,17},{9,25},{17,1},{25,9},{2,18},{10... | collective-permute-start | bytes 1572872 | tf_op jit(solution)/shard_map/ppermute | solution.py:29
  156.1 26.3 %collective-permute-start.36 = (f32[2,128,512]{2,1,0:T(8,128)S(1)}, f32[2,128,512]{2,1,0:T(8,128)S(1)}, u32[]{:S(2)}, u32[]{:S(2)}) collective-permute-start(f32[2,128,512]{2,1,0:T(8,128)S(1)} %pad_maximum_fusion.4), channel_id=1, source_target_pairs={{0,8},{8,0},{16,24},{24,16},{1,9},{9,1},{17,25},{25,17},{2,10},{10... | collective-permute-start | bytes 1572872 | tf_op jit(solution)/shard_map/ppermute | solution.py:29
  159.0 34.1 %collective-permute-start.31 = (f32[2,128,512]{2,1,0:T(8,128)}, f32[2,128,512]{2,1,0:T(8,128)S(1)}, u32[]{:S(2)}, u32[]{:S(2)}) collective-permute-start(f32[2,128,512]{2,1,0:T(8,128)} %bitcast.372), channel_id=1, source_target_pairs={{0,24},{8,16},{16,8},{24,0},{1,25},{9,17},{17,9},{25,1},{2,26},{10... | collective-permute-start | bytes 1572872 | tf_op jit(solution)/shard_map/ppermute | solution.py:29
  162.1 38.6 %collective-permute-start.32 = (f32[2,128,512]{2,1,0:T(8,128)S(1)}, f32[2,128,512]{2,1,0:T(8,128)S(1)}, u32[]{:S(2)}, u32[]{:S(2)}) collective-permute-start(f32[2,128,512]{2,1,0:T(8,128)S(1)} %bitcast.373), channel_id=1, source_target_pairs={{0,16},{8,24},{16,0},{24,8},{1,17},{9,25},{17,1},{25,9},{2,18},{10... | collective-permute-start | bytes 1572872 | tf_op jit(solution)/shard_map/ppermute | solution.py:29
  170.6 30.1 %collective-permute-start.33 = (f32[2,128,512]{2,1,0:T(8,128)S(1)}, f32[2,128,512]{2,1,0:T(8,128)S(1)}, u32[]{:S(2)}, u32[]{:S(2)}) collective-permute-start(f32[2,128,512]{2,1,0:T(8,128)S(1)} %bitcast.374), channel_id=1, source_target_pairs={{0,8},{8,0},{16,24},{24,16},{1,9},{9,1},{17,25},{25,17},{2,10},{10... | collective-permute-start | bytes 1572872 | tf_op jit(solution)/shard_map/ppermute | solution.py:29
  178.0 36.3 %collective-permute-start.39 = (f32[2,128,512]{2,1,0:T(8,128)S(1)}, f32[2,128,512]{2,1,0:T(8,128)S(1)}, u32[]{:S(2)}, u32[]{:S(2)}) collective-permute-start(f32[2,128,512]{2,1,0:T(8,128)S(1)} %pad_maximum_fusion.5), channel_id=1, source_target_pairs={{0,24},{8,16},{16,8},{24,0},{1,25},{9,17},{17,9},{25,1},{2,26},{10... | collective-permute-start | bytes 1572872 | tf_op jit(solution)/shard_map/ppermute | solution.py:29
  182.4 31.9 %collective-permute-start.40 = (f32[2,128,512]{2,1,0:T(8,128)S(1)}, f32[2,128,512]{2,1,0:T(8,128)S(1)}, u32[]{:S(2)}, u32[]{:S(2)}) collective-permute-start(f32[2,128,512]{2,1,0:T(8,128)S(1)} %pad_maximum_fusion.5), channel_id=1, source_target_pairs={{0,16},{8,24},{16,0},{24,8},{1,17},{9,25},{17,1},{25,9},{2,18},{10... | collective-permute-start | bytes 1572872 | tf_op jit(solution)/shard_map/ppermute | solution.py:29
  193.1 29.8 %collective-permute-start.41 = (f32[2,128,512]{2,1,0:T(8,128)S(1)}, f32[2,128,512]{2,1,0:T(8,128)S(1)}, u32[]{:S(2)}, u32[]{:S(2)}) collective-permute-start(f32[2,128,512]{2,1,0:T(8,128)S(1)} %pad_maximum_fusion.5), channel_id=1, source_target_pairs={{0,8},{8,0},{16,24},{24,16},{1,9},{9,1},{17,25},{25,17},{2,10},{10... | collective-permute-start | bytes 1572872 | tf_op jit(solution)/shard_map/ppermute | solution.py:29
  237.5 3.6 copy-start.2
  237.5 3.6 copy-start.4
  243.1 9.8 %copy-start.18 = (s32[24]{0:T(128)S(1)}, s32[24]{0:T(128)}, u32[]{:S(2)}) copy-start(s32[24]{0:T(128)} %constant.257.clone) | copy-start | bytes 292
  246.7 8.7 %collective-permute-start.42 = (f32[1024,512]{1,0:T(8,128)}, f32[1024,512]{1,0:T(8,128)}, u32[]{:S(2)}, u32[]{:S(2)}) collective-permute-start(f32[1024,512]{1,0:T(8,128)} %bitcast_multiply_fusion.1), channel_id=1, source_target_pairs={{0,32},{32,0},{64,96},{96,64},{128,160},{160,128},{192,224},{224,1... | collective-permute-start | bytes 6291464 | tf_op jit(solution)/shard_map/ppermute | solution.py:29
  260.3 118.7 %collective-permute-start.18 = (f32[20,128,128]{2,1,0:T(8,128)}, f32[20,128,128]{2,1,0:T(8,128)S(1)}, u32[]{:S(2)}, u32[]{:S(2)}) collective-permute-start(f32[20,128,128]{2,1,0:T(8,128)} %get-tuple-element.1044), channel_id=1, source_target_pairs={{0,64},{32,96},{64,0},{96,32},{128,192},{160,224},{192,128},{224,1... | collective-permute-start | bytes 3932168 | tf_op jit(solution)/shard_map/cond/branch_15_fun/ppermute | solution.py:29
  381.8 3.7 copy-start.17
  381.8 3.7 copy-start.12
  381.8 3.8 copy-start.16
  381.8 3.8 copy-start.15
  381.8 3.9 copy-start.14
  381.8 4.0 copy-start.13
  381.8 29.2 %all-to-all-start = ((f32[4,256,512]{2,1,0:T(8,128)}), f32[4,256,512]{2,1,0:T(8,128)S(1)}, u32[]{:S(2)}, u32[]{:S(2)}) async-start(f32[4,256,512]{2,1,0:T(8,128)} %bitcast.80), calls=%async_computation | async-start | bytes 4194304 | tf_op jit(solution)/shard_map/all_to_all | solution.py:247
  (2 other events, 5.6 us)
Sparse Core Ops, SparseCore 0:
  24.0 213.4 all-reduce.2

commit v7 on v6

--- a/solution.py
+++ b/solution.py
@@ -83,29 +83,28 @@
 
 def pack_kernel(taken, slots, value, other, packed, merged):
     def step(b, at):
-        merged[at] = value[at]
-
-        @pl.when(taken[b] > 0)
-        def _():
-            merged[at] = merged[at] + other[at]
-
+        block = value[at] + other[at] * taken[b].astype(jnp.float32)
+        merged[at] = block
         slot = slots[b]
 
         @pl.when(slot >= 0)
         def _():
-            packed[slot] = merged[at]
+            packed[slot] = block
 
     over_blocks(value.shape, step)
 
 
 def add_kernel(slots, value, packed, out):
     def step(b, at):
-        out[at] = value[at]
         slot = slots[b]
 
         @pl.when(slot >= 0)
         def _():
-            out[at] = out[at] + packed[slot]
+            out[at] = value[at] + packed[slot]
+
+        @pl.when(slot < 0)
+        def _():
+            out[at] = value[at]
 
     over_blocks(value.shape, step)
 
@@ -143,21 +142,25 @@
     return jnp.where(flat > 0, jnp.cumsum(flat) - 1, -1), jnp.sum(flat)
 
 
-def listed_exchange(value, other, taken, wanted_here, wanted_there, mask):
+def plan_exchange(wanted_here, wanted_there):
     to_send, n_send = slots_of(wanted_there)
     to_add, n_add = slots_of(wanted_here)
-    taken_flat = taken.reshape(-1).astype(jnp.int32)
-
-    def alone(value, other):
-        return value + by_blocks(other, taken)
-
-    def branch(size, value, other):
-        packed, merged = pack(taken_flat, to_send, value, other, size)
-        return add_packed(to_add, merged, xor_send(packed, "layer", mask))
-
-    choices = [alone] + [functools.partial(branch, size) for size in SIZES]
     needed = jnp.maximum(n_send, n_add)
     index = (needed > jnp.array((0, *SIZES), jnp.int32)).sum().astype(jnp.int32)
+    return to_send, to_add, index
+
+
+def listed_exchange(value, other, taken, plan, mask):
+    to_send, to_add, index = plan
+
+    def alone(value, other):
+        return value + by_blocks(other, taken.reshape(-1, value.shape[1] // BLK).astype(jnp.float32))
+
+    def branch(size, value, other):
+        packed, merged = pack(taken, to_send, value, other, size)
+        return add_packed(to_add, merged, xor_send(packed, "layer", mask))
+
+    choices = [alone] + [functools.partial(branch, size) for size in SIZES]
     return lax.switch(index, choices, value, other)
 
 
@@ -220,25 +223,20 @@
     right0 = matmul(inv[0], rows01[0])
     right0x = matmul(inv[0], crossed[0])
     right1 = matmul(inv[1], rows01[1] - by_blocks(matmul(crossed[1], right0), mask_r))
-    right0, right0x, right1, theirs, listed, left0, column1 = lax.optimization_barrier(
-        (right0, right0x, right1, theirs, listed, left0, column1)
+    def bit(values, b):
+        return values // 2**b % 2
+
+    taken = bit(mine, 0).reshape(-1)
+    plan = plan_exchange(bit(mine, 1) * kept > 0, bit(theirs, 1) * kept > 0)
+    right0, right0x, right1, listed, taken, plan, left0, column1 = lax.optimization_barrier(
+        (right0, right0x, right1, listed, taken, plan, left0, column1)
     )
 
     left1 = column1 - by_blocks(matmul(left0, right0x), mask_c)
     matrix = matrix - by_blocks(matmul(left0, right0), mask0)
     acc = by_blocks(matrix - by_blocks(matmul(left1, right1), mask1), kept)
 
-    def bit(values, b):
-        return (values // 2**b % 2).astype(jnp.float32)
-
-    acc = listed_exchange(
-        acc,
-        xor_send(acc, "layer", 1),
-        bit(mine, 0),
-        bit(mine, 1) * kept > 0,
-        bit(theirs, 1) * kept > 0,
-        2,
-    )
+    acc = listed_exchange(acc, xor_send(acc, "layer", 1), taken, plan, 2)
 
     yy = layer // 4
     qb = rb // 4
@@ -253,7 +251,7 @@
     w = lax.dynamic_slice_in_dim(listed, yy * qb, qb, 1)
     for b in (2, 3):
         d = b - 1
-        held = [held[k] + by_blocks(held[k ^ d], bit(w[k], b)) for k in range(4)]
+        held = [held[k] + by_blocks(held[k ^ d], bit(w[k], b).astype(jnp.float32)) for k in range(4)]
     return turn(jnp.stack(held)).reshape(1, rows, cols)
 
 

time: 451 us -> 430 us (0.953)
  the two profiles are of different devices: /device:TPU:229 before, /device:TPU:24 now
where the time goes in v7:
time: 430 us; the launch traced here: 431 us
  waiting for transfers between devices  228 us (53%)
  starting transfers between devices  101 us (23%)
  blocking collectives  37.4 us (9%)
  between operations  21.8 us (5%)
  other arithmetic  17.1 us (4%)
  matrix products  11.8 us (3%)
  local copies, waits for them, and re-layouts  7.51 us (2%)
  Pallas kernels  5.57 us (1%)
    ppermute x19, waiting for transfers between devices, xor_send(): return lax.ppermute(value, axis, pairs)  192 us
    ppermute x19, starting transfers between devices, xor_send(): return lax.ppermute(value, axis, pairs)  97 us
    all_to_all x1, blocking collectives, turn(): lax.all_to_all(value.reshape(4, -1, cols), 'layer', 0, 0, axis_index_grou...  27.3 us
    all_to_all x1, waiting for transfers between devices, turn(): lax.all_to_all(value.reshape(4, -1, cols), 'layer', 0, 0, axis_index_grou...  22.9 us
    psum x1, waiting for transfers between devices, body(): left0, column1 = lax.psum((panel0, panel1), 'col')  13 us
    dot_general x7, matrix products, matmul(): jnp.dot(left_side, right_side, precision=lax.Precision.HIGH, preferred_el...  11.8 us
    all_gather x1, blocking collectives, body(): listed = lax.all_gather(mine, 'layer', axis_index_groups=Y_GROUPS)  10.1 us
  transfers between devices with their start and end apart: 21, of which 13 were waited for; matrix products, arithmetic and copies ran while one was open for 4% of the time, Pallas kernels for 0%

profile of v7, /device:TPU:24, one launch (start us, length us, event | category | flops | bytes accessed | tf_op | source)
XLA Modules:
  0.0 431.0 jit_solution(6620797104836633958)
XLA Ops:
  10.8 4.2 broadcast_select_fusion
  16.5 15.8 %collective-permute-start.27 = (s32[8,4]{1,0:T(8,128)S(1)}, s32[8,4]{1,0:T(8,128)S(1)}, u32[]{:S(2)}, u32[]{:S(2)}) collective-permute-start(s32[8,4]{1,0:T(8,128)S(1)} %get-tuple-element.492), channel_id=1, source_target_pairs={{0,64},{32,96},{64,0},{96,32},{128,192},{160,224},{192,128},{224,1... | collective-permute-start | bytes 392 | tf_op jit(solution)/shard_map/ppermute | solution.py:29
  38.2 10.1 %all-gather.1 = s32[4,8,4]{1,2,0:T(4,128)S(1)} all-gather(s32[1,8,4]{1,2,0:T(4,128)S(1)} %bitcast.294), channel_id=2, replica_groups={{0,128,256,384},{32,160,288,416},{64,192,320,448},{96,224,352,480},{1,1..., dimensions={0}, use_global_device_ids=true | all-gather | bytes 640 | tf_op jit(solution)/shard_map/all_gather | solution.py:221
  50.6 3.4 collective-permute-start.30
  54.0 4.6 %collective-permute-start.29 = (f32[2,128,512]{2,1,0:T(8,128)S(1)}, f32[2,128,512]{2,1,0:T(8,128)S(1)}, u32[]{:S(2)}, u32[]{:S(2)}) collective-permute-start(f32[2,128,512]{2,1,0:T(8,128)S(1)} %get-tuple-element.512), channel_id=1, source_target_pairs={{0,16},{8,24},{16,0},{24,8},{1,17},{9,25},{17,1},{25,9},{2,18},{10... | collective-permute-start | bytes 1572872 | tf_op jit(solution)/shard_map/ppermute | solution.py:29
  64.0 3.6 collective-permute-done.30
  67.6 9.2 %collective-permute-done.29 = f32[2,128,512]{2,1,0:T(8,128)S(1)} collective-permute-done((f32[2,128,512]{2,1,0:T(8,128)S(1)}, f32[2,128,512]{2,1,0:T(8,128)S(1)}, u32[]{:S(2)}, u32[]{:S(2)}) %collective-permute-start.29) | collective-permute-done | bytes 524320 | tf_op jit(solution)/shard_map/ppermute | solution.py:29
  76.8 6.2 %collective-permute-done.28 = f32[2,128,512]{2,1,0:T(8,128)S(1)} collective-permute-done((f32[2,128,512]{2,1,0:T(8,128)S(1)}, f32[2,128,512]{2,1,0:T(8,128)S(1)}, u32[]{:S(2)}, u32[]{:S(2)}) %collective-permute-start.28) | collective-permute-done | bytes 524320 | tf_op jit(solution)/shard_map/ppermute | solution.py:29
  83.2 31.2 %conditional.7 = (f32[128,512]{1,0:T(8,128)}) conditional(s32[]{:T(128)} %convert_element_type.106, f32[128,512]{1,0:T(8,128)S(1)} %get-tuple-element.474, f32[128,512]{1,0:T(8,128)S(1)} %get-tuple-element.474), branch_computations={%region_4.5_spmd, %region_5.6_spmd} | conditional | bytes 1048624 | solution.py:62
  83.2 4.3 collective-permute-start.2
  87.5 26.9 %collective-permute-done.2 = f32[128,512]{1,0:T(8,128)} collective-permute-done((f32[128,512]{1,0:T(8,128)S(1)}, f32[128,512]{1,0:T(8,128)}, u32[]{:S(2)}, u32[]{:S(2)}) %collective-permute-start.2) | collective-permute-done | bytes 262176 | tf_op jit(solution)/shard_map/cond/branch_1_fun/ppermute | solution.py:29
  115.4 20.6 %conditional.8 = (f32[128,512]{1,0:T(8,128)}) conditional(s32[]{:T(128)} %convert_element_type.105, f32[128,512]{1,0:T(8,128)S(1)} %broadcast_select_fusion.2, f32[128,512]{1,0:T(8,128)S(1)} %broadcast_select_fusion.2), branch_computations={%region_6.7_spmd, %region_7.8_spmd} | conditional | bytes 1048624 | solution.py:62
  117.3 18.7 %collective-permute-done.3 = f32[128,512]{1,0:T(8,128)} collective-permute-done((f32[128,512]{1,0:T(8,128)S(1)}, f32[128,512]{1,0:T(8,128)}, u32[]{:S(2)}, u32[]{:S(2)}) %collective-permute-start.3) | collective-permute-done | bytes 262176 | tf_op jit(solution)/shard_map/cond/branch_1_fun/ppermute | solution.py:29
  141.5 22.9 %collective-permute-start.37 = (f32[128,512]{1,0:T(8,128)S(1)}, f32[128,512]{1,0:T(8,128)S(1)}, u32[]{:S(2)}, u32[]{:S(2)}) collective-permute-start(f32[128,512]{1,0:T(8,128)S(1)} %broadcast_select_fusion.5), channel_id=1, source_target_pairs={{0,1},{1,0},{2,3},{3,2},{4,5},{5,4},{6,7},{7,6},{8,9},{9,8},{10,11... | collective-permute-start | bytes 786440 | tf_op jit(solution)/shard_map/cond/branch_1_fun/ppermute | solution.py:29
  164.5 3.3 collective-permute-start.34
  167.8 7.0 %collective-permute-start.35 = (f32[2,128,512]{2,1,0:T(8,128)S(1)}, f32[2,128,512]{2,1,0:T(8,128)S(1)}, u32[]{:S(2)}, u32[]{:S(2)}) collective-permute-start(f32[2,128,512]{2,1,0:T(8,128)S(1)} %pad_maximum_fusion.4), channel_id=1, source_target_pairs={{0,16},{8,24},{16,0},{24,8},{1,17},{9,25},{17,1},{25,9},{2,18},{10... | collective-permute-start | bytes 1572872 | tf_op jit(solution)/shard_map/ppermute | solution.py:29
  176.7 3.0 collective-permute-start.31
  179.8 4.8 %collective-permute-start.32 = (f32[2,128,512]{2,1,0:T(8,128)S(1)}, f32[2,128,512]{2,1,0:T(8,128)S(1)}, u32[]{:S(2)}, u32[]{:S(2)}) collective-permute-start(f32[2,128,512]{2,1,0:T(8,128)S(1)} %bitcast.282), channel_id=1, source_target_pairs={{0,16},{8,24},{16,0},{24,8},{1,17},{9,25},{17,1},{25,9},{2,18},{10... | collective-permute-start | bytes 1572872 | tf_op jit(solution)/shard_map/ppermute | solution.py:29
  184.8 13.3 %collective-permute-done.34 = f32[2,128,512]{2,1,0:T(8,128)S(1)} collective-permute-done((f32[2,128,512]{2,1,0:T(8,128)S(1)}, f32[2,128,512]{2,1,0:T(8,128)S(1)}, u32[]{:S(2)}, u32[]{:S(2)}) %collective-permute-start.34) | collective-permute-done | bytes 524320 | tf_op jit(solution)/shard_map/ppermute | solution.py:29
  200.2 3.2 collective-permute-start.39
  203.5 4.4 %collective-permute-start.40 = (f32[2,128,512]{2,1,0:T(8,128)S(1)}, f32[2,128,512]{2,1,0:T(8,128)S(1)}, u32[]{:S(2)}, u32[]{:S(2)}) collective-permute-start(f32[2,128,512]{2,1,0:T(8,128)S(1)} %pad_maximum_fusion.5), channel_id=1, source_target_pairs={{0,16},{8,24},{16,0},{24,8},{1,17},{9,25},{17,1},{25,9},{2,18},{10... | collective-permute-start | bytes 1572872 | tf_op jit(solution)/shard_map/ppermute | solution.py:29
  208.4 12.1 %collective-permute-done.31 = f32[2,128,512]{2,1,0:T(8,128)S(1)} collective-permute-done((f32[2,128,512]{2,1,0:T(8,128)S(1)}, f32[2,128,512]{2,1,0:T(8,128)S(1)}, u32[]{:S(2)}, u32[]{:S(2)}) %collective-permute-start.31) | collective-permute-done | bytes 524320 | tf_op jit(solution)/shard_map/ppermute | solution.py:29
  224.7 10.3 %collective-permute-done.39 = f32[2,128,512]{2,1,0:T(8,128)S(1)} collective-permute-done((f32[2,128,512]{2,1,0:T(8,128)S(1)}, f32[2,128,512]{2,1,0:T(8,128)S(1)}, u32[]{:S(2)}, u32[]{:S(2)}) %collective-permute-start.39) | collective-permute-done | bytes 524320 | tf_op jit(solution)/shard_map/ppermute | solution.py:29
  241.5 13.0 %all-reduce.3.cloned.1.call-done = (f32[1024,512]{1,0:T(8,128)}, f32[1024,512]{1,0:T(8,128)}) async-done(((f32[1024,512]{1,0:T(8,128)}, f32[1024,512]{1,0:T(8,128)}), (f32[1024,512]{1,0:T(8,128)}, f32[1024,512]{1,0:T(8,128)})) %all-reduce.3.cloned.1.call-update) | async-done | bytes 4194320 | tf_op jit(solution)/shard_map/psum | solution.py:202
  254.5 3.6 fusion.71
  265.3 3.2 collective-permute-done.42
  268.5 97.2 %conditional.9 = (f32[1024,512]{1,0:T(8,128)}) conditional(s32[]{:T(128)} %clamp.3, (s32[32]{0:T(128)S(1)}, f32[1024,512]{1,0:T(8,128)}, f32[1024,512]{1,0:T(8,128)S(1)}) %tuple.109, (s32[32]{0:T(128)S(1)}, s32[32]{0:T(128)S(1)}, f32[1024,512]{1,0:T(8,128)S(1)}, f32[1024,512]{1,0:T(8,128)}, ...), branch_computations={%region_15.16_spmd, %region_16.17_spmd, %region_17.18_spmd, %regio... | conditional | flops 1048608 | bytes 8388656 | solution.py:164
  271.2 5.3 %collective-permute-start.19 = (f32[21,128,128]{2,1,0:T(8,128)S(1)}, f32[21,128,128]{2,1,0:T(8,128)S(1)}, u32[]{:S(2)}, u32[]{:S(2)}) collective-permute-start(f32[21,128,128]{2,1,0:T(8,128)S(1)} %get-tuple-element.400), channel_id=1, source_target_pairs={{0,64},{32,96},{64,0},{96,32},{128,192},{160,224},{192,128},{224,1... | collective-permute-start | bytes 4128776 | tf_op jit(solution)/shard_map/cond/branch_16_fun/ppermute | solution.py:29
  276.6 86.3 %collective-permute-done.19.packed = f32[21,128,128]{2,1,0:T(8,128)S(1)} collective-permute-done((f32[21,128,128]{2,1,0:T(8,128)S(1)}, f32[21,128,128]{2,1,0:T(8,128)S(1)}, u32[]{:S(2)}, u32[]{:S(2)}) %collective-permute-start.19) | collective-permute-done | bytes 1376288 | tf_op jit(solution)/shard_map/cond/branch_16_fun/ppermute | solution.py:29
  365.7 4.5 %all-to-all-start = ((f32[4,256,512]{2,1,0:T(8,128)}), f32[4,256,512]{2,1,0:T(8,128)S(1)}, u32[]{:S(2)}, u32[]{:S(2)}) async-start(f32[4,256,512]{2,1,0:T(8,128)} %bitcast.269), calls=%async_computation | async-start | bytes 4194304 | tf_op jit(solution)/shard_map/all_to_all | solution.py:245
  371.0 22.9 %all-to-all-done = f32[4,256,512]{2,1,0:T(8,128)S(1)} async-done(((f32[4,256,512]{2,1,0:T(8,128)}), f32[4,256,512]{2,1,0:T(8,128)S(1)}, u32[]{:S(2)}, u32[]{:S(2)}) %all-to-all-start) | async-done | bytes 2097184 | tf_op jit(solution)/shard_map/all_to_all | solution.py:245
  395.6 27.3 %all_to_all.10 = f32[4,256,512]{2,1,0:T(8,128)S(1)} all-to-all(f32[4,256,512]{2,1,0:T(8,128)S(1)} %pad_maximum_fusion.3), channel_id=1, replica_groups={{0,128,256,384},{32,160,288,416},{64,192,320,448},{96,224,352,480},{1,1..., dimensions={0} | all-to-all | bytes 4194304 | tf_op jit(solution)/shard_map/all_to_all | solution.py:245
  (140 shorter events, 53.0 us)
Async XLA Ops:
  6.5 248.0 %all-reduce.3.cloned.1.call-start = ((), (), s32[]{:S(2)}) async-start(), calls=%async_computation.2 | async-start | bytes 8388608 | tf_op jit(solution)/shard_map/psum | solution.py:202
  16.5 21.5 %copy-start.5 = (s32[2,32,32]{2,1,0:T(8,128)S(1)}, s32[2,32,32]{2,1,0:T(8,128)}, u32[]{:S(2)}) copy-start(s32[2,32,32]{2,1,0:T(8,128)} %param.40) | copy-start | bytes 24580
  16.5 32.9 %copy-start = (f32[1,1024,512]{2,1,0:T(8,128)S(1)}, f32[1,1024,512]{2,1,0:T(8,128)}, u32[]{:S(2)}) copy-start(f32[1,1024,512]{2,1,0:T(8,128)} %param.38) | copy-start | bytes 6291460
  16.5 32.9 %collective-permute-start.27 = (s32[8,4]{1,0:T(8,128)S(1)}, s32[8,4]{1,0:T(8,128)S(1)}, u32[]{:S(2)}, u32[]{:S(2)}) collective-permute-start(s32[8,4]{1,0:T(8,128)S(1)} %get-tuple-element.492), channel_id=1, source_target_pairs={{0,64},{32,96},{64,0},{96,32},{128,192},{160,224},{192,128},{224,1... | collective-permute-start | bytes 392 | tf_op jit(solution)/shard_map/ppermute | solution.py:29
  49.6 13.6 %copy-start.6 = (s32[24]{0:T(128)S(1)}, s32[24]{0:T(128)}, u32[]{:S(2)}) copy-start(s32[24]{0:T(128)} %constant.211.clone) | copy-start | bytes 292
  50.6 17.0 %collective-permute-start.30 = (f32[2,128,512]{2,1,0:T(8,128)}, f32[2,128,512]{2,1,0:T(8,128)S(1)}, u32[]{:S(2)}, u32[]{:S(2)}) collective-permute-start(f32[2,128,512]{2,1,0:T(8,128)} %get-tuple-element.513), channel_id=1, source_target_pairs={{0,8},{8,0},{16,24},{24,16},{1,9},{9,1},{17,25},{25,17},{2,10},{10... | collective-permute-start | bytes 1572872 | tf_op jit(solution)/shard_map/ppermute | solution.py:29
  54.0 22.7 %collective-permute-start.29 = (f32[2,128,512]{2,1,0:T(8,128)S(1)}, f32[2,128,512]{2,1,0:T(8,128)S(1)}, u32[]{:S(2)}, u32[]{:S(2)}) collective-permute-start(f32[2,128,512]{2,1,0:T(8,128)S(1)} %get-tuple-element.512), channel_id=1, source_target_pairs={{0,16},{8,24},{16,0},{24,8},{1,17},{9,25},{17,1},{25,9},{2,18},{10... | collective-permute-start | bytes 1572872 | tf_op jit(solution)/shard_map/ppermute | solution.py:29
  58.7 24.3 %collective-permute-start.28 = (f32[2,128,512]{2,1,0:T(8,128)S(1)}, f32[2,128,512]{2,1,0:T(8,128)S(1)}, u32[]{:S(2)}, u32[]{:S(2)}) collective-permute-start(f32[2,128,512]{2,1,0:T(8,128)S(1)} %get-tuple-element.511), channel_id=1, source_target_pairs={{0,24},{8,16},{16,8},{24,0},{1,25},{9,17},{17,9},{25,1},{2,26},{10... | collective-permute-start | bytes 1572872 | tf_op jit(solution)/shard_map/ppermute | solution.py:29
  83.2 31.2 %collective-permute-start.2 = (f32[128,512]{1,0:T(8,128)S(1)}, f32[128,512]{1,0:T(8,128)}, u32[]{:S(2)}, u32[]{:S(2)}) collective-permute-start(f32[128,512]{1,0:T(8,128)S(1)} %param.5), channel_id=1, source_target_pairs={{0,4},{1,5},{2,6},{3,7},{4,0},{5,1},{6,2},{7,3},{8,12},{9,13},{10,... | collective-permute-start | bytes 786440 | tf_op jit(solution)/shard_map/cond/branch_1_fun/ppermute | solution.py:29
  115.4 20.6 %collective-permute-start.3 = (f32[128,512]{1,0:T(8,128)S(1)}, f32[128,512]{1,0:T(8,128)}, u32[]{:S(2)}, u32[]{:S(2)}) collective-permute-start(f32[128,512]{1,0:T(8,128)S(1)} %param.7), channel_id=1, source_target_pairs={{0,2},{1,3},{2,0},{3,1},{4,6},{5,7},{6,4},{7,5},{8,10},{9,11},{10,... | collective-permute-start | bytes 786440 | tf_op jit(solution)/shard_map/cond/branch_1_fun/ppermute | solution.py:29
  136.0 40.7 %copy-start.4 = (f32[1,2,128,512]{3,2,1,0:T(8,128)S(1)}, f32[1,2,128,512]{3,2,1,0:T(8,128)}, u32[]{:S(2)}) copy-start(f32[1,2,128,512]{3,2,1,0:T(8,128)} %param.39) | copy-start | bytes 1572868
  136.0 40.6 %collective-permute-start.38 = (f32[128,512]{1,0:T(8,128)S(1)}, f32[128,512]{1,0:T(8,128)S(1)}, u32[]{:S(2)}, u32[]{:S(2)}) collective-permute-start(f32[128,512]{1,0:T(8,128)S(1)} %broadcast_select_fusion.3), channel_id=1, source_target_pairs={{0,1},{1,0},{2,3},{3,2},{4,5},{5,4},{6,7},{7,6},{8,9},{9,8},{10,11... | collective-permute-start | bytes 786440 | tf_op jit(solution)/shard_map/cond/branch_1_fun/ppermute | solution.py:29
  141.5 38.3 %collective-permute-start.37 = (f32[128,512]{1,0:T(8,128)S(1)}, f32[128,512]{1,0:T(8,128)S(1)}, u32[]{:S(2)}, u32[]{:S(2)}) collective-permute-start(f32[128,512]{1,0:T(8,128)S(1)} %broadcast_select_fusion.5), channel_id=1, source_target_pairs={{0,1},{1,0},{2,3},{3,2},{4,5},{5,4},{6,7},{7,6},{8,9},{9,8},{10,11... | collective-permute-start | bytes 786440 | tf_op jit(solution)/shard_map/cond/branch_1_fun/ppermute | solution.py:29
  164.5 33.5 %collective-permute-start.34 = (f32[2,128,512]{2,1,0:T(8,128)S(1)}, f32[2,128,512]{2,1,0:T(8,128)S(1)}, u32[]{:S(2)}, u32[]{:S(2)}) collective-permute-start(f32[2,128,512]{2,1,0:T(8,128)S(1)} %pad_maximum_fusion.4), channel_id=1, source_target_pairs={{0,24},{8,16},{16,8},{24,0},{1,25},{9,17},{17,9},{25,1},{2,26},{10... | collective-permute-start | bytes 1572872 | tf_op jit(solution)/shard_map/ppermute | solution.py:29
  167.8 32.5 %collective-permute-start.35 = (f32[2,128,512]{2,1,0:T(8,128)S(1)}, f32[2,128,512]{2,1,0:T(8,128)S(1)}, u32[]{:S(2)}, u32[]{:S(2)}) collective-permute-start(f32[2,128,512]{2,1,0:T(8,128)S(1)} %pad_maximum_fusion.4), channel_id=1, source_target_pairs={{0,16},{8,24},{16,0},{24,8},{1,17},{9,25},{17,1},{25,9},{2,18},{10... | collective-permute-start | bytes 1572872 | tf_op jit(solution)/shard_map/ppermute | solution.py:29
  174.8 28.7 %collective-permute-start.36 = (f32[2,128,512]{2,1,0:T(8,128)S(1)}, f32[2,128,512]{2,1,0:T(8,128)S(1)}, u32[]{:S(2)}, u32[]{:S(2)}) collective-permute-start(f32[2,128,512]{2,1,0:T(8,128)S(1)} %pad_maximum_fusion.4), channel_id=1, source_target_pairs={{0,8},{8,0},{16,24},{24,16},{1,9},{9,1},{17,25},{25,17},{2,10},{10... | collective-permute-start | bytes 1572872 | tf_op jit(solution)/shard_map/ppermute | solution.py:29
  176.7 43.8 %collective-permute-start.31 = (f32[2,128,512]{2,1,0:T(8,128)S(1)}, f32[2,128,512]{2,1,0:T(8,128)S(1)}, u32[]{:S(2)}, u32[]{:S(2)}) collective-permute-start(f32[2,128,512]{2,1,0:T(8,128)S(1)} %bitcast.281), channel_id=1, source_target_pairs={{0,24},{8,16},{16,8},{24,0},{1,25},{9,17},{17,9},{25,1},{2,26},{10... | collective-permute-start | bytes 1572872 | tf_op jit(solution)/shard_map/ppermute | solution.py:29
  179.8 43.0 %collective-permute-start.32 = (f32[2,128,512]{2,1,0:T(8,128)S(1)}, f32[2,128,512]{2,1,0:T(8,128)S(1)}, u32[]{:S(2)}, u32[]{:S(2)}) collective-permute-start(f32[2,128,512]{2,1,0:T(8,128)S(1)} %bitcast.282), channel_id=1, source_target_pairs={{0,16},{8,24},{16,0},{24,8},{1,17},{9,25},{17,1},{25,9},{2,18},{10... | collective-permute-start | bytes 1572872 | tf_op jit(solution)/shard_map/ppermute | solution.py:29
  198.0 24.9 %collective-permute-start.33 = (f32[2,128,512]{2,1,0:T(8,128)S(1)}, f32[2,128,512]{2,1,0:T(8,128)S(1)}, u32[]{:S(2)}, u32[]{:S(2)}) collective-permute-start(f32[2,128,512]{2,1,0:T(8,128)S(1)} %bitcast.283), channel_id=1, source_target_pairs={{0,8},{8,0},{16,24},{24,16},{1,9},{9,1},{17,25},{25,17},{2,10},{10... | collective-permute-start | bytes 1572872 | tf_op jit(solution)/shard_map/ppermute | solution.py:29
  200.2 34.7 %collective-permute-start.39 = (f32[2,128,512]{2,1,0:T(8,128)S(1)}, f32[2,128,512]{2,1,0:T(8,128)S(1)}, u32[]{:S(2)}, u32[]{:S(2)}) collective-permute-start(f32[2,128,512]{2,1,0:T(8,128)S(1)} %pad_maximum_fusion.5), channel_id=1, source_target_pairs={{0,24},{8,16},{16,8},{24,0},{1,25},{9,17},{17,9},{25,1},{2,26},{10... | collective-permute-start | bytes 1572872 | tf_op jit(solution)/shard_map/ppermute | solution.py:29
  203.5 31.5 %collective-permute-start.40 = (f32[2,128,512]{2,1,0:T(8,128)S(1)}, f32[2,128,512]{2,1,0:T(8,128)S(1)}, u32[]{:S(2)}, u32[]{:S(2)}) collective-permute-start(f32[2,128,512]{2,1,0:T(8,128)S(1)} %pad_maximum_fusion.5), channel_id=1, source_target_pairs={{0,16},{8,24},{16,0},{24,8},{1,17},{9,25},{17,1},{25,9},{2,18},{10... | collective-permute-start | bytes 1572872 | tf_op jit(solution)/shard_map/ppermute | solution.py:29
  220.5 17.1 %collective-permute-start.41 = (f32[2,128,512]{2,1,0:T(8,128)S(1)}, f32[2,128,512]{2,1,0:T(8,128)S(1)}, u32[]{:S(2)}, u32[]{:S(2)}) collective-permute-start(f32[2,128,512]{2,1,0:T(8,128)S(1)} %pad_maximum_fusion.5), channel_id=1, source_target_pairs={{0,8},{8,0},{16,24},{24,16},{1,9},{9,1},{17,25},{25,17},{2,10},{10... | collective-permute-start | bytes 1572872 | tf_op jit(solution)/shard_map/ppermute | solution.py:29
  254.5 3.6 copy-start.2
  254.5 3.6 copy-start.3
  258.1 2.0 copy-start.1
  262.3 6.2 %collective-permute-start.42 = (f32[1024,512]{1,0:T(8,128)S(1)}, f32[1024,512]{1,0:T(8,128)}, u32[]{:S(2)}, u32[]{:S(2)}) collective-permute-start(f32[1024,512]{1,0:T(8,128)S(1)} %bitcast_multiply_fusion.1), channel_id=1, source_target_pairs={{0,32},{32,0},{64,96},{96,64},{128,160},{160,128},{192,224},{224,1... | collective-permute-start | bytes 6291464 | tf_op jit(solution)/shard_map/ppermute | solution.py:29
  271.2 91.7 %collective-permute-start.19 = (f32[21,128,128]{2,1,0:T(8,128)S(1)}, f32[21,128,128]{2,1,0:T(8,128)S(1)}, u32[]{:S(2)}, u32[]{:S(2)}) collective-permute-start(f32[21,128,128]{2,1,0:T(8,128)S(1)} %get-tuple-element.400), channel_id=1, source_target_pairs={{0,64},{32,96},{64,0},{96,32},{128,192},{160,224},{192,128},{224,1... | collective-permute-start | bytes 4128776 | tf_op jit(solution)/shard_map/cond/branch_16_fun/ppermute | solution.py:29
  365.7 28.2 %all-to-all-start = ((f32[4,256,512]{2,1,0:T(8,128)}), f32[4,256,512]{2,1,0:T(8,128)S(1)}, u32[]{:S(2)}, u32[]{:S(2)}) async-start(f32[4,256,512]{2,1,0:T(8,128)} %bitcast.269), calls=%async_computation | async-start | bytes 4194304 | tf_op jit(solution)/shard_map/all_to_all | solution.py:245
Sparse Core Ops, SparseCore 0:
  32.5 221.9 all-reduce.2

commit v8 on v7

--- a/solution.py
+++ b/solution.py
@@ -53,7 +53,9 @@
     def part(r):
         return lax.dynamic_slice_in_dim(candidates, r * part_rows, part_rows, 1)
 
-    got = [part(row)] + [xor_send(part(row ^ k), "row", k) for k in (1, 2, 3)]
+    near = xor_send(part(row ^ 1), "row", 1)
+    near, candidates = lax.optimization_barrier((near, candidates))
+    got = [part(row), near] + [xor_send(part(row ^ k), "row", k) for k in (2, 3)]
     return [pick([g[i] for g in got], row ^ source) for i, source in enumerate(sources)]
 
 
@@ -201,8 +203,6 @@
     panel0, panel1, matrix, listed = lax.optimization_barrier((panel0, panel1, matrix, lists[0]))
     left0, column1 = lax.psum((panel0, panel1), "col")
     mine = lax.dynamic_slice(listed, *here)
-    theirs = xor_send(mine, "layer", 2)
-    theirs, matrix = lax.optimization_barrier((theirs, matrix))
 
     candidates = jnp.stack(
         [
@@ -210,9 +210,10 @@
             lax.dynamic_slice_in_dim(matrix, (q1 & 1) * half, half, 0),
         ]
     )
-    part0, part1, inverse_part = lax.optimization_barrier(
-        (*exchange_row(candidates, row, (q0 >> 1, q1 >> 1)), inverses[0])
-    )
+    part0, part1, inverse_part, mine = lax.optimization_barrier(
+        (*exchange_row(candidates, row, (q0 >> 1, q1 >> 1)), inverses[0], mine)
+    )
+    theirs = xor_send(mine, "layer", 2)
     rows01 = jnp.concatenate(gather_row(jnp.stack([part0, part1]), row), axis=1)
     inv = jnp.concatenate(gather_row(inverse_part, row), axis=1)
     x_part = spread_part(part0, col, q1)

time: 430 us -> 425 us (0.988)
  the two profiles are of different devices: /device:TPU:24 before, /device:TPU:230 now
where the time goes in v8:
time: 425 us; the launch traced here: 420 us
  waiting for transfers between devices  201 us (47%)
  starting transfers between devices  111 us (26%)
  blocking collectives  38.4 us (9%)
  between operations  21.4 us (5%)
  other arithmetic  18.2 us (4%)
  matrix products  11.7 us (3%)
  local copies, waits for them, and re-layouts  11.3 us (3%)
  Pallas kernels  5.55 us (1%)
    ppermute x18, waiting for transfers between devices, xor_send(): return lax.ppermute(value, axis, pairs)  139 us
    ppermute x18, starting transfers between devices, xor_send(): return lax.ppermute(value, axis, pairs)  103 us
    psum x1, waiting for transfers between devices, body(): left0, column1 = lax.psum((panel0, panel1), 'col')  37 us
    all_to_all x1, blocking collectives, turn(): lax.all_to_all(value.reshape(4, -1, cols), 'layer', 0, 0, axis_index_grou...  27.4 us
    all_to_all x1, waiting for transfers between devices, turn(): lax.all_to_all(value.reshape(4, -1, cols), 'layer', 0, 0, axis_index_grou...  25.1 us
    dot_general x7, matrix products, matmul(): jnp.dot(left_side, right_side, precision=lax.Precision.HIGH, preferred_el...  11.7 us
    all_gather x1, blocking collectives, body(): listed = lax.all_gather(mine, 'layer', axis_index_groups=Y_GROUPS)  11.1 us
    all_to_all x1, starting transfers between devices, turn(): lax.all_to_all(value.reshape(4, -1, cols), 'layer', 0, 0, axis_index_grou...  8.87 us
  transfers between devices with their start and end apart: 20, of which 11 were waited for; matrix products, arithmetic and copies ran while one was open for 6% of the time, Pallas kernels for 0%

profile of v8, /device:TPU:230, one launch (start us, length us, event | category | flops | bytes accessed | tf_op | source)
XLA Modules:
  0.0 419.7 jit_solution(15783720430938731543)
XLA Ops:
  10.3 4.4 %broadcast_select_fusion = (f32[1024,512]{1,0:T(8,128)}, f32[1024,512]{1,0:T(8,128)}) fusion(pred[]{:T(512)S(6)} %eq.112, f32[1,1024,512]{2,1,0:T(8,128)} %param.38, pred[]{:T(512)S(6)} %eq.111), kind=kLoop, calls=%fused_computation.30 | loop fusion | flops 1048576 | bytes 6291458 | tf_op jit(solution)/shard_map/jit(_where)/select_n | solution.py:202
  15.9 2.9 collective-permute-start.27
  23.8 7.8 %collective-permute-done.27 = f32[2,128,512]{2,1,0:T(8,128)S(1)} collective-permute-done((f32[2,128,512]{2,1,0:T(8,128)S(1)}, f32[2,128,512]{2,1,0:T(8,128)S(1)}, u32[]{:S(2)}, u32[]{:S(2)}) %collective-permute-start.27) | collective-permute-done | bytes 524320 | tf_op jit(solution)/shard_map/ppermute | solution.py:29
  35.3 4.3 %collective-permute-start.29 = (f32[2,128,512]{2,1,0:T(8,128)S(1)}, f32[2,128,512]{2,1,0:T(8,128)S(1)}, u32[]{:S(2)}, u32[]{:S(2)}) collective-permute-start(f32[2,128,512]{2,1,0:T(8,128)S(1)} %get-tuple-element.513), channel_id=1, source_target_pairs={{0,16},{8,24},{16,0},{24,8},{1,17},{9,25},{17,1},{25,9},{2,18},{10... | collective-permute-start | bytes 1572872 | tf_op jit(solution)/shard_map/ppermute | solution.py:29
  43.2 16.8 %collective-permute-done.28 = f32[2,128,512]{2,1,0:T(8,128)S(1)} collective-permute-done((f32[2,128,512]{2,1,0:T(8,128)S(1)}, f32[2,128,512]{2,1,0:T(8,128)S(1)}, u32[]{:S(2)}, u32[]{:S(2)}) %collective-permute-start.28) | collective-permute-done | bytes 524320 | tf_op jit(solution)/shard_map/ppermute | solution.py:29
  64.5 3.1 collective-permute-start.34
  67.6 4.3 %collective-permute-start.35 = (f32[2,128,512]{2,1,0:T(8,128)}, f32[2,128,512]{2,1,0:T(8,128)S(1)}, u32[]{:S(2)}, u32[]{:S(2)}) collective-permute-start(f32[2,128,512]{2,1,0:T(8,128)} %pad_maximum_fusion.5), channel_id=1, source_target_pairs={{0,8},{8,0},{16,24},{24,16},{1,9},{9,1},{17,25},{25,17},{2,10},{10... | collective-permute-start | bytes 1572872 | tf_op jit(solution)/shard_map/ppermute | solution.py:29
  72.0 8.2 %collective-permute-start.41 = (s32[8,4]{1,0:T(8,128)S(1)}, s32[8,4]{1,0:T(8,128)S(1)}, u32[]{:S(2)}, u32[]{:S(2)}) collective-permute-start(s32[8,4]{1,0:T(8,128)S(1)} %dynamic_slice.45), channel_id=1, source_target_pairs={{0,64},{32,96},{64,0},{96,32},{128,192},{160,224},{192,128},{224,1... | collective-permute-start | bytes 392 | tf_op jit(solution)/shard_map/ppermute | solution.py:29
  81.8 50.3 %conditional.6 = (f32[128,512]{1,0:T(8,128)}) conditional(s32[]{:T(128)} %convert_element_type.103, f32[128,512]{1,0:T(8,128)S(1)} %broadcast_select_fusion.4, f32[128,512]{1,0:T(8,128)S(1)} %broadcast_select_fusion.4), branch_computations={%region_2.3_spmd, %region_3.4_spmd} | conditional | bytes 1048624 | solution.py:64
  81.8 38.5 %collective-permute-start.1 = (f32[128,512]{1,0:T(8,128)S(1)}, f32[128,512]{1,0:T(8,128)}, u32[]{:S(2)}, u32[]{:S(2)}) collective-permute-start(f32[128,512]{1,0:T(8,128)S(1)} %param.3), channel_id=1, source_target_pairs={{0,2},{1,3},{2,0},{3,1},{4,6},{5,7},{6,4},{7,5},{8,10},{9,11},{10,... | collective-permute-start | bytes 786440 | tf_op jit(solution)/shard_map/cond/branch_1_fun/ppermute | solution.py:29
  120.3 11.8 %collective-permute-done.1 = f32[128,512]{1,0:T(8,128)} collective-permute-done((f32[128,512]{1,0:T(8,128)S(1)}, f32[128,512]{1,0:T(8,128)}, u32[]{:S(2)}, u32[]{:S(2)}) %collective-permute-start.1) | collective-permute-done | bytes 262176 | tf_op jit(solution)/shard_map/cond/branch_1_fun/ppermute | solution.py:29
  137.7 11.1 %all-gather.1 = s32[4,8,4]{1,2,0:T(4,128)S(1)} all-gather(s32[1,8,4]{1,2,0:T(4,128)S(1)} %bitcast.294), channel_id=2, replica_groups={{0,128,256,384},{32,160,288,416},{64,192,320,448},{96,224,352,480},{1,1..., dimensions={0}, use_global_device_ids=true | all-gather | bytes 640 | tf_op jit(solution)/shard_map/all_gather | solution.py:222
  148.8 3.9 collective-permute-start.37
  156.3 2.5 collective-permute-start.30
  158.8 4.3 %collective-permute-start.31 = (f32[2,128,512]{2,1,0:T(8,128)S(1)}, f32[2,128,512]{2,1,0:T(8,128)S(1)}, u32[]{:S(2)}, u32[]{:S(2)}) collective-permute-start(f32[2,128,512]{2,1,0:T(8,128)S(1)} %bitcast.282), channel_id=1, source_target_pairs={{0,16},{8,24},{16,0},{24,8},{1,17},{9,25},{17,1},{25,9},{2,18},{10... | collective-permute-start | bytes 1572872 | tf_op jit(solution)/shard_map/ppermute | solution.py:29
  163.2 3.1 collective-permute-start.32
  166.3 2.5 collective-permute-start.38
  168.8 4.3 %collective-permute-start.39 = (f32[2,128,512]{2,1,0:T(8,128)S(1)}, f32[2,128,512]{2,1,0:T(8,128)S(1)}, u32[]{:S(2)}, u32[]{:S(2)}) collective-permute-start(f32[2,128,512]{2,1,0:T(8,128)S(1)} %pad_maximum_fusion.6), channel_id=1, source_target_pairs={{0,16},{8,24},{16,0},{24,8},{1,17},{9,25},{17,1},{25,9},{2,18},{10... | collective-permute-start | bytes 1572872 | tf_op jit(solution)/shard_map/ppermute | solution.py:29
  173.4 12.1 %collective-permute-done.30 = f32[2,128,512]{2,1,0:T(8,128)S(1)} collective-permute-done((f32[2,128,512]{2,1,0:T(8,128)S(1)}, f32[2,128,512]{2,1,0:T(8,128)S(1)}, u32[]{:S(2)}, u32[]{:S(2)}) %collective-permute-start.30) | collective-permute-done | bytes 524320 | tf_op jit(solution)/shard_map/ppermute | solution.py:29
  188.7 9.4 %collective-permute-done.38 = f32[2,128,512]{2,1,0:T(8,128)S(1)} collective-permute-done((f32[2,128,512]{2,1,0:T(8,128)S(1)}, f32[2,128,512]{2,1,0:T(8,128)S(1)}, u32[]{:S(2)}, u32[]{:S(2)}) %collective-permute-start.38) | collective-permute-done | bytes 524320 | tf_op jit(solution)/shard_map/ppermute | solution.py:29
  198.1 2.7 collective-permute-done.40
  206.0 37.0 %all-reduce.3.cloned.1.call-done = (f32[1024,512]{1,0:T(8,128)}, f32[1024,512]{1,0:T(8,128)}) async-done(((f32[1024,512]{1,0:T(8,128)}, f32[1024,512]{1,0:T(8,128)}), (f32[1024,512]{1,0:T(8,128)}, f32[1024,512]{1,0:T(8,128)})) %all-reduce.3.cloned.1.call-update) | async-done | bytes 4194320 | tf_op jit(solution)/shard_map/psum | solution.py:204
  242.9 3.6 fusion.68
  253.8 3.1 collective-permute-done.42
  256.9 91.0 %conditional.9 = (f32[1024,512]{1,0:T(8,128)}) conditional(s32[]{:T(128)} %clamp.3, (s32[32]{0:T(128)S(1)}, f32[1024,512]{1,0:T(8,128)}, f32[1024,512]{1,0:T(8,128)S(1)}) %tuple.109, (s32[32]{0:T(128)S(1)}, s32[32]{0:T(128)S(1)}, f32[1024,512]{1,0:T(8,128)S(1)}, f32[1024,512]{1,0:T(8,128)}, ...), branch_computations={%region_15.16_spmd, %region_16.17_spmd, %region_17.18_spmd, %regio... | conditional | flops 1048608 | bytes 8388656 | solution.py:166
  256.9 2.7 branch_12_fun.2
  259.6 10.1 %collective-permute-start.15 = (f32[17,128,128]{2,1,0:T(8,128)S(1)}, f32[17,128,128]{2,1,0:T(8,128)S(1)}, u32[]{:S(2)}, u32[]{:S(2)}) collective-permute-start(f32[17,128,128]{2,1,0:T(8,128)S(1)} %get-tuple-element.372), channel_id=1, source_target_pairs={{0,64},{32,96},{64,0},{96,32},{128,192},{160,224},{192,128},{224,1... | collective-permute-start | bytes 3342344 | tf_op jit(solution)/shard_map/cond/branch_12_fun/ppermute | solution.py:29
  269.7 75.3 %collective-permute-done.15.packed = f32[17,128,128]{2,1,0:T(8,128)S(1)} collective-permute-done((f32[17,128,128]{2,1,0:T(8,128)S(1)}, f32[17,128,128]{2,1,0:T(8,128)S(1)}, u32[]{:S(2)}, u32[]{:S(2)}) %collective-permute-start.15) | collective-permute-done | bytes 1114144 | tf_op jit(solution)/shard_map/cond/branch_12_fun/ppermute | solution.py:29
  345.0 2.8 branch_12_fun.3
  347.9 8.9 %all-to-all-start = ((f32[4,256,512]{2,1,0:T(8,128)}), f32[4,256,512]{2,1,0:T(8,128)S(1)}, u32[]{:S(2)}, u32[]{:S(2)}) async-start(f32[4,256,512]{2,1,0:T(8,128)} %bitcast.269), calls=%async_computation | async-start | bytes 4194304 | tf_op jit(solution)/shard_map/all_to_all | solution.py:246
  357.4 25.1 %all-to-all-done = f32[4,256,512]{2,1,0:T(8,128)S(1)} async-done(((f32[4,256,512]{2,1,0:T(8,128)}), f32[4,256,512]{2,1,0:T(8,128)S(1)}, u32[]{:S(2)}, u32[]{:S(2)}) %all-to-all-start) | async-done | bytes 2097184 | tf_op jit(solution)/shard_map/all_to_all | solution.py:246
  384.2 27.4 %all_to_all.10 = f32[4,256,512]{2,1,0:T(8,128)S(1)} all-to-all(f32[4,256,512]{2,1,0:T(8,128)S(1)} %pad_maximum_fusion.4), channel_id=1, replica_groups={{0,128,256,384},{32,160,288,416},{64,192,320,448},{96,224,352,480},{1,1..., dimensions={0} | all-to-all | bytes 4194304 | tf_op jit(solution)/shard_map/all_to_all | solution.py:246
  (144 shorter events, 46.6 us)
Async XLA Ops:
  6.5 236.4 %all-reduce.3.cloned.1.call-start = ((), (), s32[]{:S(2)}) async-start(), calls=%async_computation.2 | async-start | bytes 8388608 | tf_op jit(solution)/shard_map/psum | solution.py:204
  10.2 4.4 %copy-start = (f32[1,1024,512]{2,1,0:T(8,128)S(1)}, f32[1,1024,512]{2,1,0:T(8,128)}, u32[]{:S(2)}) copy-start(f32[1,1024,512]{2,1,0:T(8,128)} %param.38) | copy-start | bytes 6291460
  14.8 1.0 copy-start.2
  15.9 5.8 %copy-start.7 = (s32[2,32,32]{2,1,0:T(8,128)S(1)}, s32[2,32,32]{2,1,0:T(8,128)}, u32[]{:S(2)}) copy-start(s32[2,32,32]{2,1,0:T(8,128)} %param.40) | copy-start | bytes 24580
  15.9 5.9 %copy-start.3 = (f32[1,512,512]{2,1,0:T(8,128)S(1)}, f32[1,512,512]{2,1,0:T(8,128)}, u32[]{:S(2)}) copy-start(f32[1,512,512]{2,1,0:T(8,128)} %copy-done.2) | copy-start | bytes 3145732
  15.9 15.7 %collective-permute-start.27 = (f32[2,128,512]{2,1,0:T(8,128)S(1)}, f32[2,128,512]{2,1,0:T(8,128)S(1)}, u32[]{:S(2)}, u32[]{:S(2)}) collective-permute-start(f32[2,128,512]{2,1,0:T(8,128)S(1)} %fusion.10), channel_id=1, source_target_pairs={{0,8},{8,0},{16,24},{24,16},{1,9},{9,1},{17,25},{25,17},{2,10},{10... | collective-permute-start | bytes 1572872 | tf_op jit(solution)/shard_map/ppermute | solution.py:29
  32.9 27.1 %collective-permute-start.28 = (f32[2,128,512]{2,1,0:T(8,128)S(1)}, f32[2,128,512]{2,1,0:T(8,128)S(1)}, u32[]{:S(2)}, u32[]{:S(2)}) collective-permute-start(f32[2,128,512]{2,1,0:T(8,128)S(1)} %get-tuple-element.512), channel_id=1, source_target_pairs={{0,24},{8,16},{16,8},{24,0},{1,25},{9,17},{17,9},{25,1},{2,26},{10... | collective-permute-start | bytes 1572872 | tf_op jit(solution)/shard_map/ppermute | solution.py:29
  35.3 24.7 %collective-permute-start.29 = (f32[2,128,512]{2,1,0:T(8,128)S(1)}, f32[2,128,512]{2,1,0:T(8,128)S(1)}, u32[]{:S(2)}, u32[]{:S(2)}) collective-permute-start(f32[2,128,512]{2,1,0:T(8,128)S(1)} %get-tuple-element.513), channel_id=1, source_target_pairs={{0,16},{8,24},{16,0},{24,8},{1,17},{9,25},{17,1},{25,9},{2,18},{10... | collective-permute-start | bytes 1572872 | tf_op jit(solution)/shard_map/ppermute | solution.py:29
  62.1 101.1 %collective-permute-start.33 = (f32[2,128,512]{2,1,0:T(8,128)}, f32[2,128,512]{2,1,0:T(8,128)S(1)}, u32[]{:S(2)}, u32[]{:S(2)}) collective-permute-start(f32[2,128,512]{2,1,0:T(8,128)} %pad_maximum_fusion.5), channel_id=1, source_target_pairs={{0,24},{8,16},{16,8},{24,0},{1,25},{9,17},{17,9},{25,1},{2,26},{10... | collective-permute-start | bytes 1572872 | tf_op jit(solution)/shard_map/ppermute | solution.py:29
  64.5 101.8 %collective-permute-start.34 = (f32[2,128,512]{2,1,0:T(8,128)}, f32[2,128,512]{2,1,0:T(8,128)S(1)}, u32[]{:S(2)}, u32[]{:S(2)}) collective-permute-start(f32[2,128,512]{2,1,0:T(8,128)} %pad_maximum_fusion.5), channel_id=1, source_target_pairs={{0,16},{8,24},{16,0},{24,8},{1,17},{9,25},{17,1},{25,9},{2,18},{10... | collective-permute-start | bytes 1572872 | tf_op jit(solution)/shard_map/ppermute | solution.py:29
  67.6 101.2 %collective-permute-start.35 = (f32[2,128,512]{2,1,0:T(8,128)}, f32[2,128,512]{2,1,0:T(8,128)S(1)}, u32[]{:S(2)}, u32[]{:S(2)}) collective-permute-start(f32[2,128,512]{2,1,0:T(8,128)} %pad_maximum_fusion.5), channel_id=1, source_target_pairs={{0,8},{8,0},{16,24},{24,16},{1,9},{9,1},{17,25},{25,17},{2,10},{10... | collective-permute-start | bytes 1572872 | tf_op jit(solution)/shard_map/ppermute | solution.py:29
  72.0 76.9 %collective-permute-start.41 = (s32[8,4]{1,0:T(8,128)S(1)}, s32[8,4]{1,0:T(8,128)S(1)}, u32[]{:S(2)}, u32[]{:S(2)}) collective-permute-start(s32[8,4]{1,0:T(8,128)S(1)} %dynamic_slice.45), channel_id=1, source_target_pairs={{0,64},{32,96},{64,0},{96,32},{128,192},{160,224},{192,128},{224,1... | collective-permute-start | bytes 392 | tf_op jit(solution)/shard_map/ppermute | solution.py:29
  81.7 73.8 %copy-start.8 = (s32[24]{0:T(128)S(1)}, s32[24]{0:T(128)}, u32[]{:S(2)}) copy-start(s32[24]{0:T(128)} %constant.211.clone) | copy-start | bytes 292
  81.7 74.6 %copy-start.6 = (f32[1,2,128,512]{3,2,1,0:T(8,128)S(1)}, f32[1,2,128,512]{3,2,1,0:T(8,128)}, u32[]{:S(2)}) copy-start(f32[1,2,128,512]{3,2,1,0:T(8,128)} %param.39) | copy-start | bytes 1572868
  81.8 50.3 %collective-permute-start.1 = (f32[128,512]{1,0:T(8,128)S(1)}, f32[128,512]{1,0:T(8,128)}, u32[]{:S(2)}, u32[]{:S(2)}) collective-permute-start(f32[128,512]{1,0:T(8,128)S(1)} %param.3), channel_id=1, source_target_pairs={{0,2},{1,3},{2,0},{3,1},{4,6},{5,7},{6,4},{7,5},{8,10},{9,11},{10,... | collective-permute-start | bytes 786440 | tf_op jit(solution)/shard_map/cond/branch_1_fun/ppermute | solution.py:29
  134.8 21.5 %collective-permute-start.36 = (f32[128,512]{1,0:T(8,128)S(1)}, f32[128,512]{1,0:T(8,128)}, u32[]{:S(2)}, u32[]{:S(2)}) collective-permute-start(f32[128,512]{1,0:T(8,128)S(1)} %broadcast_select_fusion.5), channel_id=1, source_target_pairs={{0,1},{1,0},{2,3},{3,2},{4,5},{5,4},{6,7},{7,6},{8,9},{9,8},{10,11... | collective-permute-start | bytes 786440 | tf_op jit(solution)/shard_map/cond/branch_1_fun/ppermute | solution.py:29
  148.8 10.0 %collective-permute-start.37 = (f32[128,512]{1,0:T(8,128)S(1)}, f32[128,512]{1,0:T(8,128)S(1)}, u32[]{:S(2)}, u32[]{:S(2)}) collective-permute-start(f32[128,512]{1,0:T(8,128)S(1)} %broadcast_select_fusion.3), channel_id=1, source_target_pairs={{0,1},{1,0},{2,3},{3,2},{4,5},{5,4},{6,7},{7,6},{8,9},{9,8},{10,11... | collective-permute-start | bytes 786440 | tf_op jit(solution)/shard_map/cond/branch_1_fun/ppermute | solution.py:29
  156.3 29.2 %collective-permute-start.30 = (f32[2,128,512]{2,1,0:T(8,128)S(1)}, f32[2,128,512]{2,1,0:T(8,128)S(1)}, u32[]{:S(2)}, u32[]{:S(2)}) collective-permute-start(f32[2,128,512]{2,1,0:T(8,128)S(1)} %bitcast.281), channel_id=1, source_target_pairs={{0,24},{8,16},{16,8},{24,0},{1,25},{9,17},{17,9},{25,1},{2,26},{10... | collective-permute-start | bytes 1572872 | tf_op jit(solution)/shard_map/ppermute | solution.py:29
  158.8 29.2 %collective-permute-start.31 = (f32[2,128,512]{2,1,0:T(8,128)S(1)}, f32[2,128,512]{2,1,0:T(8,128)S(1)}, u32[]{:S(2)}, u32[]{:S(2)}) collective-permute-start(f32[2,128,512]{2,1,0:T(8,128)S(1)} %bitcast.282), channel_id=1, source_target_pairs={{0,16},{8,24},{16,0},{24,8},{1,17},{9,25},{17,1},{25,9},{2,18},{10... | collective-permute-start | bytes 1572872 | tf_op jit(solution)/shard_map/ppermute | solution.py:29
  163.2 25.2 %collective-permute-start.32 = (f32[2,128,512]{2,1,0:T(8,128)S(1)}, f32[2,128,512]{2,1,0:T(8,128)S(1)}, u32[]{:S(2)}, u32[]{:S(2)}) collective-permute-start(f32[2,128,512]{2,1,0:T(8,128)S(1)} %bitcast.283), channel_id=1, source_target_pairs={{0,8},{8,0},{16,24},{24,16},{1,9},{9,1},{17,25},{25,17},{2,10},{10... | collective-permute-start | bytes 1572872 | tf_op jit(solution)/shard_map/ppermute | solution.py:29
  166.3 31.8 %collective-permute-start.38 = (f32[2,128,512]{2,1,0:T(8,128)S(1)}, f32[2,128,512]{2,1,0:T(8,128)S(1)}, u32[]{:S(2)}, u32[]{:S(2)}) collective-permute-start(f32[2,128,512]{2,1,0:T(8,128)S(1)} %pad_maximum_fusion.6), channel_id=1, source_target_pairs={{0,24},{8,16},{16,8},{24,0},{1,25},{9,17},{17,9},{25,1},{2,26},{10... | collective-permute-start | bytes 1572872 | tf_op jit(solution)/shard_map/ppermute | solution.py:29
  168.8 29.3 %collective-permute-start.39 = (f32[2,128,512]{2,1,0:T(8,128)S(1)}, f32[2,128,512]{2,1,0:T(8,128)S(1)}, u32[]{:S(2)}, u32[]{:S(2)}) collective-permute-start(f32[2,128,512]{2,1,0:T(8,128)S(1)} %pad_maximum_fusion.6), channel_id=1, source_target_pairs={{0,16},{8,24},{16,0},{24,8},{1,17},{9,25},{17,1},{25,9},{2,18},{10... | collective-permute-start | bytes 1572872 | tf_op jit(solution)/shard_map/ppermute | solution.py:29
  185.5 15.3 %collective-permute-start.40 = (f32[2,128,512]{2,1,0:T(8,128)S(1)}, f32[2,128,512]{2,1,0:T(8,128)S(1)}, u32[]{:S(2)}, u32[]{:S(2)}) collective-permute-start(f32[2,128,512]{2,1,0:T(8,128)S(1)} %pad_maximum_fusion.6), channel_id=1, source_target_pairs={{0,8},{8,0},{16,24},{24,16},{1,9},{9,1},{17,25},{25,17},{2,10},{10... | collective-permute-start | bytes 1572872 | tf_op jit(solution)/shard_map/ppermute | solution.py:29
  242.9 3.6 copy-start.4
  242.9 3.6 copy-start.5
  246.5 2.0 copy-start.1
  250.7 6.2 %collective-permute-start.42 = (f32[1024,512]{1,0:T(8,128)S(1)}, f32[1024,512]{1,0:T(8,128)}, u32[]{:S(2)}, u32[]{:S(2)}) collective-permute-start(f32[1024,512]{1,0:T(8,128)S(1)} %bitcast_multiply_fusion.1), channel_id=1, source_target_pairs={{0,32},{32,0},{64,96},{96,64},{128,160},{160,128},{192,224},{224,1... | collective-permute-start | bytes 6291464 | tf_op jit(solution)/shard_map/ppermute | solution.py:29
  259.6 85.4 %collective-permute-start.15 = (f32[17,128,128]{2,1,0:T(8,128)S(1)}, f32[17,128,128]{2,1,0:T(8,128)S(1)}, u32[]{:S(2)}, u32[]{:S(2)}) collective-permute-start(f32[17,128,128]{2,1,0:T(8,128)S(1)} %get-tuple-element.372), channel_id=1, source_target_pairs={{0,64},{32,96},{64,0},{96,32},{128,192},{160,224},{192,128},{224,1... | collective-permute-start | bytes 3342344 | tf_op jit(solution)/shard_map/cond/branch_12_fun/ppermute | solution.py:29
  347.9 34.7 %all-to-all-start = ((f32[4,256,512]{2,1,0:T(8,128)}), f32[4,256,512]{2,1,0:T(8,128)S(1)}, u32[]{:S(2)}, u32[]{:S(2)}) async-start(f32[4,256,512]{2,1,0:T(8,128)} %bitcast.269), calls=%async_computation | async-start | bytes 4194304 | tf_op jit(solution)/shard_map/all_to_all | solution.py:246
Sparse Core Ops, SparseCore 0:
  18.9 223.9 all-reduce.2
